TPU v7x, 512 devices: a whole 4x8x8 slice. The times are simulated.
512 devices in a mesh: ctx: 128 (over x, z, y_hi), mp: 4 (over y_lo, core).
Axes of the slice: x: 4, y: 8 (y_hi: 4, y_lo: 2; y = y_hi * 2 + y_lo), z: 8, core: 2. Of those that a mesh axis runs over, the one named last changes fastest.
Arguments:
- q_in: bfloat16 [17408, 8192], P('ctx', 'mp'), may hold values from -6 to 6
- k_in: bfloat16 [17408, 8192], P('ctx', 'mp'), may hold values from -6 to 6
- value_projected: bfloat16 [17408, 8192], P('ctx', 'mp'), may hold values from -6 to 6
- grad_out: bfloat16 [17408, 8192], P('ctx', 'mp'), may hold values from -6 to 6
- filt_short: bfloat16 [7, 512], P(None, 'ctx'), may hold values from -2 to 2
- filt_medium: bfloat16 [128, 512], P(None, 'ctx'), may hold values from -0.5 to 0.5
Outputs:
- grad_q: bfloat16 [17408, 8192], P('ctx', 'mp')
- grad_k: bfloat16 [17408, 8192], P('ctx', 'mp')
- grad_v: bfloat16 [17408, 8192], P('ctx', 'mp')
- grad_filt_short: float32 [7, 512], P(None, 'ctx')
- grad_filt_medium: float32 [128, 512], P(None, 'ctx')
All inputs are finite; a program needn't handle non-finite values.
Results may differ from a plain program's by a relative error of at most 0.02.
Values may be sent and summed in bfloat16 or wider, within the bound.
No kernel may reach another device: no remote copies, remote signals or barrier semaphores. Data moves between devices by JAX's collectives and lax.ppermute only.
A program may use at most 128 MiB of HBM per device.

v0:
```python
import jax
import jax.numpy as jnp
from jax import lax
from jax.sharding import PartitionSpec as P

FEATURIZER_TAPS = 7
KB = 128
CPG = 16


def shifted_2(value, axis, steps):
    count = lax.axis_size(axis)
    leading, last = (max(0, -steps), min(count, count - steps))
    return lax.ppermute(value, axis, [(source, source + steps) for source in range(leading, last)])


def product_bf16(first, second):
    return (first.astype(jnp.float32) * second.astype(jnp.float32)).astype(jnp.bfloat16)


def filter_per_tap(padded, expanded, causal):
    count = expanded.shape[0]
    row_count = padded.shape[0] - count + 1
    running = jnp.zeros((row_count, padded.shape[1]), jnp.float32)
    for tap_index in range(count):
        start = count - 1 - tap_index if causal else tap_index
        running = running + expanded[tap_index][None, :] * padded[start : start + row_count].astype(
            jnp.float32
        )
    return running


def gradient_per_tap(grad, padded, count):
    row_count = grad.shape[0]
    grad_wide = grad.astype(jnp.float32)
    columns = []
    for tap_index in range(count):
        start = count - 1 - tap_index
        shifted = padded[start : start + row_count].astype(jnp.float32)
        columns.append(jnp.sum(grad_wide * shifted, 0).reshape(-1, CPG).sum(1))
    return jnp.stack(columns, 0)


def toeplitz(kernel_rows, row_count):
    groups, count = kernel_rows.shape
    padded_line = jnp.concatenate(
        [kernel_rows, jnp.zeros((groups, row_count), kernel_rows.dtype)], 1
    )
    repeated = jnp.tile(padded_line, (1, row_count))[:, : row_count * (row_count + count - 1)]
    return repeated.reshape(groups, row_count, row_count + count - 1)


def group_major(signal, groups):
    return signal.reshape(signal.shape[0], groups, CPG).transpose(1, 2, 0)


def matrix_filter(padded, kernel):
    count = kernel.shape[0]
    groups = kernel.shape[1]
    row_count = padded.shape[0] - count + 1
    matrix = toeplitz(kernel.T, row_count)
    blocks = group_major(padded, groups)
    result = jnp.einsum("gts,gcs->gct", matrix, blocks, preferred_element_type=jnp.float32)
    return result.transpose(2, 0, 1).reshape(row_count, -1)


def matrix_gradient(grad, padded, count):
    row_count = grad.shape[0]
    groups = grad.shape[1] // CPG
    group_block = min(16, groups)
    left = group_major(grad, groups)
    right = group_major(padded, groups)

    def one_block(number):
        left_block = lax.dynamic_slice_in_dim(left, number * group_block, group_block, 0)
        right_block = lax.dynamic_slice_in_dim(right, number * group_block, group_block, 0)
        products = jnp.einsum(
            "gct,gcs->gts", left_block, right_block, preferred_element_type=jnp.float32
        )
        flattened = products.reshape(group_block, -1)
        flattened = jnp.concatenate(
            [flattened, jnp.zeros((group_block, row_count), jnp.float32)], 1
        )
        diagonal = flattened.reshape(group_block, row_count, row_count + count)[:, :, :count]
        return diagonal.sum(1)

    pieces = lax.map(one_block, jnp.arange(groups // group_block))
    return pieces.reshape(groups, count)[:, ::-1].T


def shards(q_in, k_in, value_projected, grad_out, filt_short, filt_medium):
    row_count = q_in.shape[0]
    channels = q_in.shape[1]
    groups = channels // CPG
    brain_float_half = jnp.bfloat16
    f32 = jnp.float32
    mp_index = lax.axis_index("mp")
    every_short, every_medium = (
        lax.all_gather(filt_short, "ctx", axis=1, tiled=True),
        lax.all_gather(filt_medium, "ctx", axis=1, tiled=True),
    )
    short_filter_taps = lax.dynamic_slice_in_dim(every_short, mp_index * groups, groups, 1)
    taps_medium = lax.dynamic_slice_in_dim(every_medium, mp_index * groups, groups, 1)
    reversed_medium = taps_medium[::-1]
    short_expanded = jnp.repeat(short_filter_taps.astype(f32), CPG, axis=1)
    outgoing = jnp.stack(
        [
            q_in[row_count - (FEATURIZER_TAPS - 1) :],
            k_in[row_count - (FEATURIZER_TAPS - 1) :],
            value_projected[row_count - (FEATURIZER_TAPS - 1) :],
        ],
        0,
    )
    preceding_rows = shifted_2(outgoing, "ctx", 1)
    qpad = jnp.concatenate([preceding_rows[0], q_in], 0)
    kpad = jnp.concatenate([preceding_rows[1], k_in], 0)
    value_padded = jnp.concatenate([preceding_rows[2], value_projected], 0)
    q_feat = filter_per_tap(qpad, short_expanded, True).astype(brain_float_half)
    k_feat = filter_per_tap(kpad, short_expanded, True).astype(brain_float_half)
    value_featurized = filter_per_tap(value_padded, short_expanded, True).astype(brain_float_half)
    u_inner = product_bf16(k_feat, value_featurized)
    before_inner = shifted_2(u_inner[row_count - (KB - 1) :], "ctx", 1)
    upad_inner = jnp.concatenate([before_inner, u_inner], 0)
    z_inner = matrix_filter(upad_inner, reversed_medium)
    d_inner = product_bf16(grad_out, q_feat)
    after_inner = shifted_2(d_inner[: KB - 1], "ctx", -1)
    du_inner = matrix_filter(jnp.concatenate([d_inner, after_inner], 0), taps_medium)
    dq_feat = (grad_out.astype(f32) * z_inner).astype(brain_float_half)
    dk_feat = (du_inner * value_featurized.astype(f32)).astype(brain_float_half)
    value_featurized_gradient = (du_inner * k_feat.astype(f32)).astype(brain_float_half)
    upward = jnp.stack(
        [
            dq_feat[: FEATURIZER_TAPS - 1],
            dk_feat[: FEATURIZER_TAPS - 1],
            value_featurized_gradient[: FEATURIZER_TAPS - 1],
        ],
        0,
    )
    after = shifted_2(upward, "ctx", -1)
    dq_pad = jnp.concatenate([dq_feat, after[0]], 0)
    dk_pad = jnp.concatenate([dk_feat, after[1]], 0)
    dv_pad = jnp.concatenate([value_featurized_gradient, after[2]], 0)
    grad_q = filter_per_tap(dq_pad, short_expanded, False).astype(brain_float_half)
    grad_k = filter_per_tap(dk_pad, short_expanded, False).astype(brain_float_half)
    grad_v = filter_per_tap(dv_pad, short_expanded, False).astype(brain_float_half)
    part_medium = matrix_gradient(d_inner, upad_inner, KB)
    part_short = (
        gradient_per_tap(dq_feat, qpad, FEATURIZER_TAPS)
        + gradient_per_tap(dk_feat, kpad, FEATURIZER_TAPS)
        + gradient_per_tap(value_featurized_gradient, value_padded, FEATURIZER_TAPS)
    )
    summed_short, summed_medium = lax.psum((part_short, part_medium), "ctx")
    whole_short, whole_medium = (
        lax.all_gather(summed_short, "mp", axis=1, tiled=True),
        lax.all_gather(summed_medium, "mp", axis=1, tiled=True),
    )
    own_count = whole_short.shape[1] // lax.axis_size("ctx")
    ctx_index = lax.axis_index("ctx")
    grad_filt_short = lax.dynamic_slice_in_dim(whole_short, ctx_index * own_count, own_count, 1)
    grad_filt_medium = lax.dynamic_slice_in_dim(whole_medium, ctx_index * own_count, own_count, 1)
    return (grad_q, grad_k, grad_v, grad_filt_short, grad_filt_medium)


def solution(mesh):
    placed = (
        P("ctx", "mp"),
        P("ctx", "mp"),
        P("ctx", "mp"),
        P("ctx", "mp"),
        P(None, "ctx"),
        P(None, "ctx"),
    )
    return jax.shard_map(
        shards,
        mesh=mesh,
        in_specs=placed,
        out_specs=(P("ctx", "mp"), P("ctx", "mp"), P("ctx", "mp"), P(None, "ctx"), P(None, "ctx")),
        check_vma=False,
    )
```

profile of v0, /device:TPU:1, one launch (start us, length us, event | category | flops | bytes accessed | tf_op | source)
XLA Modules:
  0.0 2243.6 jit_solution(13380555999171827701)
XLA Ops:
  8.9 5.0 collective-permute-start
  14.0 323.4 %all-gather = bf16[128,4,7]{2,1,0:T(4,128)(2,1)S(1)} all-gather(bf16[1,4,7]{2,1,0:T(4,128)(2,1)} %bitcast.139), channel_id=1, replica_groups=mesh['ctx'=128,'mp'=4] {'ctx'}, dimensions={0}, use_global_device_ids=true | all-gather | bytes 7224 | tf_op jit(solution)/shard_map/all_gather | solution.py:99
  341.1 317.5 %all-gather.1 = bf16[128,4,128]{2,1,0:T(4,128)(2,1)S(1)} all-gather(bf16[1,4,128]{2,1,0:T(4,128)(2,1)S(1)} %bitcast.140), channel_id=1, replica_groups=mesh['ctx'=128,'mp'=4] {'ctx'}, dimensions={0}, use_global_device_ids=true | all-gather | bytes 132096 | tf_op jit(solution)/shard_map/all_gather | solution.py:100
  660.1 4.1 slice.365
  664.2 13.8 reshape.147
  678.0 17.0 copy.36
  696.2 4.2 slice.351
  700.4 13.8 reshape.144
  714.2 17.0 copy.33
  734.1 10.0 fusion.108
  744.9 6.1 fusion.71
  759.5 8.5 collective-permute-done.1
  769.7 94.2 %while.10 = (s32[]{:T(128)}, f32[8,16,128]{2,1,0:T(8,128)}, s32[8]{0:T(128)S(1)}, bf16[128,16,136]{2,1,0:T(8,128)(2,1)}, bf16[128,16,263]{2,1,0:T(8,128)(2,1)}, ...) while((s32[]{:T(128)}, f32[8,16,128]{2,1,0:T(8,128)}, s32[8]{0:T(128)S(1)}, ...), condition=%wide.region_45.46_spmd, body=%wide.region_43.45_spmd.sunk | while | flops 18589700 | bytes 17517744 | solution.py:87
  776.6 3.0 reshape.179
  788.3 3.0 reshape.179
  800.1 3.0 reshape.179
  811.9 3.0 reshape.179
  865.5 10.0 fusion.107
  876.2 4.2 fusion.43
  882.0 321.0 %psum.14 = f32[7,128]{1,0:T(8,128)S(1)} all-reduce(f32[7,128]{1,0:T(8,128)S(1)} %add_add_fusion), channel_id=1, replica_groups=mesh['ctx'=128,'mp'=4] {'ctx'}, use_global_device_ids=true, to_apply=%region_42.43 | all-reduce | flops 896 | bytes 7168 | tf_op jit(solution)/shard_map/psum | solution.py:152
  1203.0 171.5 %all_gather.14 = f32[7,512]{1,0:T(8,128)S(1)} all-gather(f32[7,128]{1,0:T(8,128)S(1)} %psum.14), channel_id=1, replica_groups=mesh['ctx'=128,'mp'=4] {'mp'}, dimensions={1}, use_global_device_ids=true | all-gather | bytes 17920 | tf_op jit(solution)/shard_map/all_gather | solution.py:154
  1376.6 821.1 %all-reduce.5.cloned.1.call-done = f32[128,128]{0,1:T(8,128)} async-done(((f32[128,128]{0,1:T(8,128)}), f32[128,128]{0,1:T(8,128)}) %all-reduce.5.cloned.1.call-update) | async-done | bytes 65552 | tf_op jit(solution)/shard_map/psum | solution.py:152
  2197.7 33.4 %all_gather.15 = f32[128,512]{0,1:T(8,128)S(1)} all-gather(f32[128,128]{0,1:T(8,128)} %all-reduce.5.cloned.1.call-done), channel_id=1, replica_groups=mesh['ctx'=128,'mp'=4] {'mp'}, dimensions={1}, use_global_device_ids=true | all-gather | bytes 327680 | tf_op jit(solution)/shard_map/all_gather | solution.py:155
  2233.5 3.2 fusion.64
  (177 shorter events, 106.5 us)
Async XLA Ops:
  7.2 331.5 %copy-start.6 = (bf16[136,2048]{1,0:T(8,128)(2,1)S(1)}, bf16[136,2048]{1,0:T(8,128)(2,1)}, u32[]{:S(2)}) copy-start(bf16[136,2048]{1,0:T(8,128)(2,1)} %param.8) | copy-start | bytes 1671172
  7.2 331.5 %copy-start.7 = (bf16[136,2048]{1,0:T(8,128)(2,1)S(1)}, bf16[136,2048]{1,0:T(8,128)(2,1)}, u32[]{:S(2)}) copy-start(bf16[136,2048]{1,0:T(8,128)(2,1)} %param.11) | copy-start | bytes 1671172
  7.2 2190.5 %all-reduce.5.cloned.1.call-start = ((), (), s32[]{:S(2)}) async-start(), calls=%async_computation | async-start | bytes 131072 | tf_op jit(solution)/shard_map/psum | solution.py:152
  8.9 329.7 %collective-permute-start = (bf16[3,6,2048]{2,1,0:T(8,128)(2,1)S(1)}, bf16[3,6,2048]{2,1,0:T(8,128)(2,1)S(1)}, u32[]{:S(2)}, u32[]{:S(2)}) collective-permute-start(bf16[3,6,2048]{2,1,0:T(8,128)(2,1)S(1)} %pad_maximum_fusion.8), channel_id=1, source_target_pairs={{0,4},{4,8},{8,12},{12,16},{16,20},{20,24},{24,28},{28,32},{32,36}... | collective-permute-start | bytes 221192 | tf_op jit(solution)/shard_map/ppermute | solution.py:14
  338.7 2.5 copy-start.8
  339.8 392.6 %collective-permute-start.2 = (bf16[127,2048]{1,0:T(8,128)(2,1)S(1)}, bf16[127,2048]{1,0:T(8,128)(2,1)S(1)}, u32[]{:S(2)}, u32[]{:S(2)}) collective-permute-start(bf16[127,2048]{1,0:T(8,128)(2,1)S(1)} %slice.364), channel_id=1, source_target_pairs={{4,0},{8,4},{12,8},{16,12},{20,16},{24,20},{28,24},{32,28},{36,32}... | collective-permute-start | bytes 1560584 | tf_op jit(solution)/shard_map/ppermute | solution.py:14
  744.9 6.1 copy-start
  744.9 6.1 copy-start.1
  751.0 5.5 copy-start.2
  753.4 6.1 copy-start.4
  753.7 14.3 collective-permute-start.1
  880.5 1351.3 %copy-start.5 = (bf16[136,2048]{1,0:T(8,128)(2,1)S(1)}, bf16[136,2048]{1,0:T(8,128)(2,1)}, u32[]{:S(2)}) copy-start(bf16[136,2048]{1,0:T(8,128)(2,1)} %copy-done.4) | copy-start | bytes 1671172
  881.6 1352.0 %copy-start.3 = (bf16[136,2048]{1,0:T(8,128)(2,1)S(1)}, bf16[136,2048]{1,0:T(8,128)(2,1)}, u32[]{:S(2)}) copy-start(bf16[136,2048]{1,0:T(8,128)(2,1)} %copy-done.2) | copy-start | bytes 1671172
  1375.3 856.4 %collective-permute-start.3 = (bf16[3,6,2048]{2,1,0:T(8,128)(2,1)S(1)}, bf16[3,6,2048]{2,1,0:T(8,128)(2,1)S(1)}, u32[]{:S(2)}, u32[]{:S(2)}) collective-permute-start(bf16[3,6,2048]{2,1,0:T(8,128)(2,1)S(1)} %pad_maximum_fusion.9), channel_id=1, source_target_pairs={{4,0},{8,4},{12,8},{16,12},{20,16},{24,20},{28,24},{32,28},{36,32}... | collective-permute-start | bytes 221192 | tf_op jit(solution)/shard_map/ppermute | solution.py:14
Sparse Core Ops, SparseCore 0:
  865.6 1332.0 all-reduce.4
where the time goes:
time: 2250 us; the launch traced here: 2240 us
  blocking collectives  1170 us (52%)
  waiting for transfers between devices  830 us (37%)
  local copies, waits for them, and re-layouts  150 us (7%)
  matrix products  34.2 us (2%)
  other arithmetic  31.9 us (1%)
    psum x1, waiting for transfers between devices, shards(): summed_short, summed_medium = lax.psum((part_short, part_medium), 'ctx')  821 us
    all_gather x1, blocking collectives, shards(): lax.all_gather(filt_short, 'ctx', axis=1, tiled=True)  323 us
    psum x1, blocking collectives, shards(): summed_short, summed_medium = lax.psum((part_short, part_medium), 'ctx')  321 us
    all_gather x1, blocking collectives, shards(): lax.all_gather(filt_medium, 'ctx', axis=1, tiled=True)  318 us
    all_gather x1, blocking collectives, shards(): lax.all_gather(summed_short, 'mp', axis=1, tiled=True)  172 us
    reshape x4, local copies, waits for them, and re-layouts, toeplitz(): return repeated.reshape(groups, row_count, row_count + count - 1)  61.6 us
  transfers between devices with their start and end apart: 5, of which 2 were waited for; matrix products, arithmetic and copies ran while one was open for 4% of the time, Pallas kernels for 0%

commit v1 on v0

v1 whole, which is shorter than its diff:
```python
import jax
import jax.numpy as jnp
from jax import lax
from jax.experimental import pallas as pl
from jax.experimental.pallas import tpu as pltpu
from jax.sharding import Mesh, PartitionSpec as P

F32 = jnp.float32
BF16 = jnp.bfloat16
CPG = 16
KS = 7
KB = 128
LANES = 128
GPB = LANES // CPG
HALO = 8
CTX = ("x", "z", "yh")
MP = ("yl", "core")
ALL = CTX + MP
SIZES = (4, 8, 4, 4)
VMEM = 56 * 1024 * 1024


def params(**more):
    return pltpu.CompilerParams(vmem_limit_bytes=VMEM, **more)


def lane_group(shape):
    return lax.broadcasted_iota(jnp.int32, shape, len(shape) - 1) // CPG


def short_taps(taps):
    row = lax.broadcasted_iota(jnp.int32, (16, LANES), 0)
    group = jnp.where(row % 8 >= 4, row // 8 * 4 + row % 4, -1)
    spread = (lane_group((16, LANES)) == group).astype(F32)
    return lax.dot_general(
        taps[:, :LANES].T, spread, (((1,), (0,)), ((), ())), precision=lax.Precision.HIGHEST,
        preferred_element_type=F32,
    )[:8]


def load_rows(scratch, first, second):
    cut = first.shape[0]
    scratch[0:cut] = first
    scratch[cut : cut + second.shape[0]] = second


def featurize_kernel(q, k, v, g, before, taps, u, d, kf, vf, u_send, d_send, hexp, pad):
    rows = q.shape[0]
    for b in range(q.shape[1] // LANES):
        lanes = slice(b * LANES, (b + 1) * LANES)
        both = taps[2 * b : 2 * b + 2].astype(F32).reshape(16, LANES)
        h = short_taps(both)
        hexp[:, lanes] = h
        early = before[:, lanes].astype(F32)
        feats = []
        for i, x in enumerate((q, k, v)):
            slot = pad.at[(3 * b + i) % 2]
            load_rows(slot, early[8 * i : 8 * i + 8], x[:, lanes].astype(F32))
            total = h[0:1] * slot[HALO : HALO + rows]
            for j in range(1, KS):
                total = total + h[j : j + 1] * slot[HALO - j : HALO - j + rows]
            feats.append(total.astype(BF16).astype(F32))
        qf, kfeat, vfeat = feats
        kf[:, lanes] = kfeat.astype(BF16)
        vf[:, lanes] = vfeat.astype(BF16)
        inner = kfeat * vfeat
        u[:, lanes] = inner.astype(BF16)
        u_send[:, lanes] = inner[rows - KB :].astype(BF16)
        gated = g[:, lanes].astype(F32) * qf
        d[:, lanes] = gated.astype(BF16)
        d_send[:, lanes] = gated[:KB].astype(BF16)


def featurize(q, k, v, g, before, taps, interpret=False):
    rows, channels = q.shape
    wide = 512
    block = lambda r: pl.BlockSpec((r, wide), lambda i: (0, i))
    shape = lambda r, t=BF16: jax.ShapeDtypeStruct((r, channels), t)
    return pl.pallas_call(
        featurize_kernel,
        grid=(channels // wide,),
        in_specs=[block(rows)] * 4
        + [block(24), pl.BlockSpec((2 * wide // LANES, 8, LANES), lambda i: (i, 0, 0))],
        out_specs=[block(rows)] * 4 + [block(KB), block(KB), block(8)],
        out_shape=[shape(rows)] * 4 + [shape(KB), shape(KB), shape(8, F32)],
        scratch_shapes=[pltpu.VMEM((2, HALO + rows, LANES), F32)],
        compiler_params=params(),
        cost_estimate=pl.CostEstimate(flops=50_000_000, bytes_accessed=6_000_000, transcendentals=0),
        interpret=interpret,
        name="featurize",
    )(q, k, v, g, before, taps)


def toeplitz_kernel(taps, after, tc, ta):
    del after
    both = taps[...].reshape(16, LANES)
    row = lax.broadcasted_iota(jnp.int32, (LANES, LANES), 0)
    col = lax.broadcasted_iota(jnp.int32, (LANES, LANES), 1)
    flip = (row + col == LANES - 1).astype(BF16)
    turned = jnp.dot(both, flip, preferred_element_type=F32)
    straight = both.astype(F32)
    nothing = jnp.zeros((8, LANES), F32)
    for g in range(GPB):
        at = g // 4 * 8 + g % 4
        for out, lines, first in ((tc, turned, 1), (ta, straight, 0)):
            line = jnp.concatenate([jnp.broadcast_to(lines[at : at + 1], (8, LANES)), nothing], 1)
            base = pltpu.roll(line, first, 1, stride=1, stride_axis=0)
            for a in range(KB // 16):
                low = pltpu.roll(base, 16 * a, 1) if a else base
                high = pltpu.roll(base, 16 * a + 8, 1)
                out[g * KB + 16 * a : g * KB + 16 * a + 16] = jnp.concatenate([low, high], 0).astype(BF16)


def toeplitz(taps, after, interpret=False):
    blocks = taps.shape[0] // 2
    out = jax.ShapeDtypeStruct((blocks * GPB * KB, 2 * KB), BF16)
    return pl.pallas_call(
        toeplitz_kernel,
        grid=(blocks,),
        in_specs=[
            pl.BlockSpec((2, 8, LANES), lambda i: (i, 0, 0)),
            pl.BlockSpec((8, LANES), lambda i: (0, 0)),
        ],
        out_specs=[pl.BlockSpec((GPB * KB, 2 * KB), lambda i: (i, 0))] * 2,
        out_shape=[out, out],
        compiler_params=params(),
        cost_estimate=pl.CostEstimate(flops=50_000_000, bytes_accessed=17_000_000, transcendentals=0),
        interpret=interpret,
        name="toeplitz",
    )(taps, after)


def pick_groups(stacked, rows, start, count):
    groups = lane_group((count, LANES))
    out = stacked[start : start + count]
    for g in range(1, GPB):
        out = jnp.where(groups == g, stacked[g * rows + start : g * rows + start + count], out)
    return out


def align_left(tile):
    width = tile.shape[1]
    row = lax.broadcasted_iota(jnp.int32, tile.shape, 0)
    for bit in (1, 2, 4):
        tile = jnp.where(row // bit % 2 == 1, pltpu.roll(tile, width - bit, 1), tile)
    return tile


def inner_kernel(
    u, u_halo, d, d_halo, kf, vf, g, q, k, v, before, hexp, tc, ta,
    dq, dk, dv, up, part, pad, medium, grid_prod, last_prod,
):
    rows = u.shape[0]
    body = rows - 8
    uw = jnp.concatenate([u_halo[...].astype(F32), u[...].astype(F32)], 0)
    dw = jnp.concatenate([d[...].astype(F32), d_halo[...].astype(F32)], 0)
    u_low, u_high = uw[: 2 * KB].astype(BF16), uw[8:].astype(BF16)
    d_low, d_high = dw[: 2 * KB].astype(BF16), dw[8:].astype(BF16)

    grid_prod[:, :LANES] = jnp.dot(tc[...], u_low, preferred_element_type=F32)
    z_low = pick_groups(grid_prod.at[:, :LANES], KB, 0, KB)
    tails = jnp.concatenate([tc[i * KB + KB - 16 : (i + 1) * KB] for i in range(GPB)], 0)
    z_high = pick_groups(jnp.dot(tails, u_high, preferred_element_type=F32), 16, 8, 8)
    z = jnp.concatenate([z_low, z_high], 0)
    dq_feat = (g[...].astype(F32) * z).astype(BF16)

    grid_prod[:, LANES:] = jnp.dot(ta[...], d_high, preferred_element_type=F32)
    du_high = pick_groups(grid_prod.at[:, LANES:], KB, 0, KB)
    heads = jnp.concatenate([ta[i * KB : i * KB + 16] for i in range(GPB)], 0)
    du_low = pick_groups(jnp.dot(heads, d_low, preferred_element_type=F32), 16, 0, 8)
    du = jnp.concatenate([du_low, du_high], 0)
    dk_feat = (du * vf[...].astype(F32)).astype(BF16)
    dv_feat = (du * kf[...].astype(F32)).astype(BF16)

    sums = [jnp.zeros((1, LANES), F32)] * 8
    early = before[...].astype(F32)
    first = []
    for i, (x, feat, out) in enumerate(((q, dq_feat, dq), (k, dk_feat, dk), (v, dv_feat, dv))):
        out[...] = feat
        wide = feat.astype(F32)
        first.append(wide[:8])
        load_rows(pad, early[8 * i : 8 * i + 8], x[...].astype(F32))
        for j in range(KS):
            sums[j] = sums[j] + jnp.sum(wide * pad[HALO - j : HALO - j + rows], 0, keepdims=True)
    up[...] = jnp.concatenate(first, 0).astype(BF16)
    short = jnp.concatenate(sums + [jnp.zeros((LANES - 8, LANES), F32)], 0)
    gather = (lane_group((8, LANES)) == lax.broadcasted_iota(jnp.int32, (8, LANES), 0)).astype(F32)
    short = lax.dot_general(
        gather, short, (((1,), (1,)), ((), ())), precision=lax.Precision.HIGHEST,
        preferred_element_type=F32,
    )

    dv32 = dw[:rows]
    groups = lane_group((rows, LANES))
    masked = [jnp.where(groups == i, dv32, 0.0) for i in range(GPB)]
    contract = (((1,), (1,)), ((), ()))
    grid_prod[...] = lax.dot_general(
        jnp.concatenate([m[:body] for m in masked], 0).astype(BF16), u_low, contract,
        preferred_element_type=F32,
    )
    last_prod[...] = lax.dot_general(
        jnp.concatenate([m[body:] for m in masked], 0).astype(BF16), u_high, contract,
        preferred_element_type=F32,
    )
    for i in range(GPB):
        total = grid_prod[i * KB : i * KB + 8]
        for a in range(1, KB // 8):
            tile = grid_prod[i * KB + 8 * a : i * KB + 8 * a + 8]
            if a == KB // 8 - 1:
                tile = tile + last_prod[8 * i : 8 * i + 8]
            total = total + pltpu.roll(tile, 2 * KB - 8 * a, 1)
        line = jnp.sum(align_left(total), 0, keepdims=True)
        medium[i : i + 1] = pltpu.roll(line, 2 * KB - 1, 1)[:, :LANES]
    for half in range(2):
        part[half, 0:4] = medium[4 * half : 4 * half + 4]
        part[half, 4:8] = short[4 * half : 4 * half + 4]


def inner(u, u_halo, d, d_halo, kf, vf, g, q, k, v, before, hexp, tc, ta, interpret=False):
    rows, channels = u.shape
    blocks = channels // LANES
    block = lambda r: pl.BlockSpec((r, LANES), lambda i: (0, i))
    square = pl.BlockSpec((GPB * KB, 2 * KB), lambda i: (i, 0))
    shape = lambda r: jax.ShapeDtypeStruct((r, channels), BF16)
    return pl.pallas_call(
        inner_kernel,
        grid=(blocks,),
        in_specs=[block(rows), block(KB), block(rows), block(KB)]
        + [block(rows)] * 6
        + [block(24), block(8), square, square],
        out_specs=[block(rows)] * 3 + [block(24), pl.BlockSpec((2, 8, LANES), lambda i: (i, 0, 0))],
        out_shape=[shape(rows)] * 3
        + [shape(24), jax.ShapeDtypeStruct((2 * blocks, 8, LANES), F32)],
        scratch_shapes=[
            pltpu.VMEM((HALO + rows, LANES), F32),
            pltpu.VMEM((GPB, LANES), F32),
            pltpu.VMEM((GPB * KB, 2 * KB), F32),
            pltpu.VMEM((GPB * 8, 2 * KB), F32),
        ],
        compiler_params=params(),
        cost_estimate=pl.CostEstimate(flops=3_000_000_000, bytes_accessed=25_000_000, transcendentals=0),
        interpret=interpret,
        name="inner",
    )(u, u_halo, d, d_halo, kf, vf, g, q, k, v, before, hexp, tc, ta)


def project_kernel(dq, dk, dv, after, hexp, gq, gk, gv, pad):
    rows = dq.shape[0]
    for b in range(dq.shape[1] // LANES):
        lanes = slice(b * LANES, (b + 1) * LANES)
        h = hexp[:, lanes]
        late = after[:, lanes].astype(F32)
        for i, (x, out) in enumerate(((dq, gq), (dk, gk), (dv, gv))):
            slot = pad.at[(3 * b + i) % 2]
            load_rows(slot, x[:, lanes].astype(F32), late[8 * i : 8 * i + 8])
            total = h[0:1] * slot[0:rows]
            for j in range(1, KS):
                total = total + h[j : j + 1] * slot[j : j + rows]
            out[:, lanes] = total.astype(BF16)


def project(dq, dk, dv, after, hexp, interpret=False):
    rows, channels = dq.shape
    wide = 512
    block = lambda r: pl.BlockSpec((r, wide), lambda i: (0, i))
    return pl.pallas_call(
        project_kernel,
        grid=(channels // wide,),
        in_specs=[block(rows)] * 3 + [block(24), block(8)],
        out_specs=[block(rows)] * 3,
        out_shape=[jax.ShapeDtypeStruct((rows, channels), BF16)] * 3,
        scratch_shapes=[pltpu.VMEM((2, rows + HALO, LANES), F32)],
        compiler_params=params(),
        cost_estimate=pl.CostEstimate(flops=30_000_000, bytes_accessed=4_000_000, transcendentals=0),
        interpret=interpret,
        name="project",
    )(dq, dk, dv, after, hexp)


def step_ctx(value, step):
    count = lax.axis_size(CTX)
    return lax.ppermute(value, CTX, [(i, i + step) for i in range(count) if 0 <= i + step < count])


def swap_x_mp(value):
    nx, nz, ny, nm = SIZES
    at = lambda x, z, y, m: ((x * nz + z) * ny + y) * nm + m
    pairs = [
        (at(x, z, y, m), at(m, z, y, x))
        for x in range(nx) for z in range(nz) for y in range(ny) for m in range(nm)
    ]
    return lax.ppermute(value, ALL, pairs)


def pack_taps(filt_short, filt_medium):
    short = jnp.pad(filt_short.T, ((0, 0), (0, LANES - KS)))
    return jnp.concatenate([filt_medium.T, short], 0)


def shards(q, k, v, g, filt_short, filt_medium):
    rows = q.shape[0]
    tails = jnp.concatenate([x[rows - HALO :] for x in (q, k, v)], 0)
    before = step_ctx(tails, 1)
    own = swap_x_mp(pack_taps(filt_short, filt_medium))
    taps = lax.all_to_all(
        jnp.broadcast_to(own[None], (32, 8, LANES)), ("z", "yh"), 0, 0, tiled=True
    )
    u, d, kf, vf, u_send, d_send, hexp = featurize(q, k, v, g, before, taps)
    u_halo = step_ctx(u_send, 1)
    d_halo = step_ctx(d_send, -1)
    tc, ta = toeplitz(taps, hexp)
    dq, dk, dv, up, part = inner(u, u_halo, d, d_halo, kf, vf, g, q, k, v, before, hexp, tc, ta)
    after = step_ctx(up, -1)
    pieces = lax.all_to_all(part, ("z", "yh"), 0, 0, tiled=True)
    total = lax.psum(swap_x_mp(jnp.sum(pieces, 0)), MP)
    grad_q, grad_k, grad_v = project(dq, dk, dv, after, hexp)
    return grad_q, grad_k, grad_v, total[4:8, :KS].T, total[0:4, ::-1].T


def solution(mesh):
    fine = Mesh(mesh.devices.reshape(4, 8, 4, 2, 2), ALL)
    signal = P(CTX, MP)
    taps = P(None, CTX)
    return jax.shard_map(
        shards,
        mesh=fine,
        in_specs=(signal,) * 4 + (taps,) * 2,
        out_specs=(signal,) * 3 + (taps,) * 2,
        check_vma=False,
    )
```

time: 2250 us -> 141 us (0.06)
  blocking collectives: 1170 us -> 7.09 us
  waiting for transfers between devices: 830 us -> 29.2 us
  local copies, waits for them, and re-layouts: 150 us -> 6.19 us
  Pallas kernels: 0 us -> 48.5 us
  starting transfers between devices: 10.5 us -> 46.9 us
  matrix products: 34.2 us -> 0 us
  other arithmetic: 31.9 us -> 0.75 us
    all_gather x4 -> x0, blocking collectives: 846 us -> none  [the longest x1 323 us: shards(): lax.all_gather(filt_short, 'ctx', axis=1, tiled=True)]
    psum x1 -> x0, waiting for transfers between devices: 821 us -> none  [shards(): summed_short, summed_medium = lax.psum((part_short, part_medium), 'ctx')]
    psum x1, blocking collectives: 321 us -> 7.09 us  [shards(): total = lax.psum(swap_x_mp(jnp.sum(pieces, 0)), MP)]
    reshape x43 -> x0, local copies, waits for them, and re-layouts: 105 us -> none  [the longest x4 61.6 us: toeplitz(): return repeated.reshape(groups, row_count, row_count + count - 1)]
    pallas_call x0 -> x4, Pallas kernels: none -> 48.5 us  [the longest x1 23.5 us: inner(): pl.pallas_call(inner_kernel, grid=(blocks,), in_specs=[block(rows), block...]
    dot_general x10 -> x0, matrix products: 34.2 us -> none  [the longest x2 20 us: matrix_filter(): jnp.einsum('gts,gcs->gct', matrix, blocks, preferred_element_type=jnp.flo...]
    all_to_all x0 -> x2, starting transfers between devices: none -> 28.7 us  [the longest x1 15.7 us: shards(): lax.all_to_all(jnp.broadcast_to(own[None], (32, 8, LANES)), ('z', 'yh'),...]
    reduce_sum x32 -> x1, other arithmetic: 25.4 us -> 0.04 us  [shards(): total = lax.psum(swap_x_mp(jnp.sum(pieces, 0)), MP)]
  transfers between devices with their start and end apart: 5 -> 8, of which waited for: 2 -> 4; matrix products, arithmetic and copies ran while one was open for 4% -> 2% of each run, Pallas kernels for 0% -> 13%
where the time goes in v1:
time: 141 us; the launch traced here: 139 us
  Pallas kernels  48.5 us (34%)
  starting transfers between devices  46.9 us (33%)
  waiting for transfers between devices  29.2 us (21%)
  blocking collectives  7.09 us (5%)
  local copies, waits for them, and re-layouts  6.19 us (4%)
    pallas_call x1, Pallas kernels, inner(): pl.pallas_call(inner_kernel, grid=(blocks,), in_specs=[block(rows), block...  23.5 us
    all_to_all x1, starting transfers between devices, shards(): lax.all_to_all(jnp.broadcast_to(own[None], (32, 8, LANES)), ('z', 'yh'),...  15.7 us
    ppermute x4, waiting for transfers between devices, step_ctx(): lax.ppermute(value, CTX, [(i, i + step) for i in range(count) if 0 <= i +...  13.9 us
    pallas_call x1, Pallas kernels, toeplitz(): pl.pallas_call(toeplitz_kernel, grid=(blocks,), in_specs=[pl.BlockSpec((2...  13.8 us
    all_to_all x1, starting transfers between devices, shards(): pieces = lax.all_to_all(part, ('z', 'yh'), 0, 0, tiled=True)  13 us
    all_to_all x1, waiting for transfers between devices, shards(): pieces = lax.all_to_all(part, ('z', 'yh'), 0, 0, tiled=True)  9.94 us
    ppermute x2, starting transfers between devices, swap_x_mp(): return lax.ppermute(value, ALL, pairs)  9.24 us
    ppermute x4, starting transfers between devices, step_ctx(): lax.ppermute(value, CTX, [(i, i + step) for i in range(count) if 0 <= i +...  9.02 us
  transfers between devices with their start and end apart: 8, of which 4 were waited for; matrix products, arithmetic and copies ran while one was open for 2% of the time, Pallas kernels for 13%

profile of v1, /device:TPU:1, one launch (start us, length us, event | category | flops | bytes accessed | tf_op | source)
XLA Modules:
  0.0 139.4 jit_solution(16371298840227238720)
XLA Ops:
  0.6 0.7 fusion.1
  1.3 4.5 %collective-permute-start.1 = (bf16[8,128]{1,0:T(8,128)(2,1)S(1)}, bf16[8,128]{1,0:T(8,128)(2,1)S(1)}, u32[]{:S(2)}, u32[]{:S(2)}) collective-permute-start(bf16[8,128]{1,0:T(8,128)(2,1)S(1)} %fusion.1), channel_id=1, source_target_pairs={{0,0},{1,128},{2,256},{3,384},{4,4},{5,132},{6,260},{7,388},{8,8},... | collective-permute-start | bytes 6152 | tf_op jit(solution)/shard_map/ppermute | solution.py:292
  5.8 0.8 slice.15
  6.6 0.8 slice.16
  7.4 0.8 slice.17
  8.1 0.6 broadcast_in_dim.2
  8.8 15.7 %all-to-all-start = ((bf16[32,8,128]{2,1,0:T(8,128)(2,1)}), bf16[32,8,128]{2,1,0:T(8,128)(2,1)S(1)}, u32[]{:S(2)}, u32[]{:S(2)}) async-start(bf16[32,8,128]{2,1,0:T(8,128)(2,1)} %broadcast_in_dim.2), calls=%async_computation | async-start | bytes 131072 | tf_op jit(solution)/shard_map/all_to_all | solution.py:305
  24.5 4.0 %collective-permute-start = (bf16[24,2048]{1,0:T(8,128)(2,1)S(1)}, bf16[24,2048]{1,0:T(8,128)(2,1)S(1)}, u32[]{:S(2)}, u32[]{:S(2)}) collective-permute-start(bf16[24,2048]{1,0:T(8,128)(2,1)S(1)} %pad_maximum_fusion), channel_id=1, source_target_pairs={{0,4},{4,8},{8,12},{12,16},{16,20},{20,24},{24,28},{28,32},{32,36}... | collective-permute-start | bytes 294920 | tf_op jit(solution)/shard_map/ppermute | solution.py:282
  28.5 1.7 %collective-permute-done.before = bf16[24,2048]{1,0:T(8,128)(2,1)S(1)} collective-permute-done((bf16[24,2048]{1,0:T(8,128)(2,1)S(1)}, bf16[24,2048]{1,0:T(8,128)(2,1)S(1)}, u32[]{:S(2)}, u32[]{:S(2)}) %collective-permute-start) | collective-permute-done | bytes 98336 | tf_op jit(solution)/shard_map/ppermute | solution.py:282
  30.2 5.4 %all-to-all-done.taps = bf16[32,8,128]{2,1,0:T(8,128)(2,1)S(1)} async-done(((bf16[32,8,128]{2,1,0:T(8,128)(2,1)}), bf16[32,8,128]{2,1,0:T(8,128)(2,1)S(1)}, u32[]{:S(2)}, u32[]{:S(2)}) %all-to-all-start) | async-done | bytes 65568 | tf_op jit(solution)/shard_map/all_to_all | solution.py:305
  36.3 6.3 %featurize.1 = (bf16[136,2048]{1,0:T(8,128)(2,1)}, bf16[136,2048]{1,0:T(8,128)(2,1)}, bf16[136,2048]{1,0:T(8,128)(2,1)}, bf16[136,2048]{1,0:T(8,128)(2,1)}, bf16...) custom-call(bf16[136,2048]{1,0:T(8,128)(2,1)} %q.3, bf16[136,2048]{1,0:T(8,128)(2,1)} %k.3, ...), custom_call_target="tpu_custom_call" | custom-call | flops 50000000 | bytes 6000000 | tf_op jit(solution)/shard_map/featurize/pallas_call | solution.py:79
  42.5 2.4 %collective-permute-start.2 = (bf16[128,2048]{1,0:T(8,128)(2,1)}, bf16[128,2048]{1,0:T(8,128)(2,1)S(1)}, u32[]{:S(2)}, u32[]{:S(2)}) collective-permute-start(bf16[128,2048]{1,0:T(8,128)(2,1)} %get-tuple-element.23), channel_id=1, source_target_pairs={{0,4},{4,8},{8,12},{12,16},{16,20},{20,24},{24,28},{28,32},{32,36}... | collective-permute-start | bytes 1572872 | tf_op jit(solution)/shard_map/ppermute | solution.py:282
  44.9 1.3 collective-permute-start.3
  46.2 13.8 %toeplitz.1 = (bf16[16384,256]{1,0:T(8,128)(2,1)}, bf16[16384,256]{1,0:T(8,128)(2,1)}) custom-call(bf16[32,8,128]{2,1,0:T(8,128)(2,1)} %copy-done.3, f32[8,2048]{1,0:T(8,128)} %get-tuple-element.28.after.hexp), custom_call_target="tpu_custom_call" | custom-call | flops 50000000 | bytes 17000000 | tf_op jit(solution)/shard_map/toeplitz/pallas_call | solution.py:117
  60.1 12.1 %collective-permute-done.3.d_halo = bf16[128,2048]{1,0:T(8,128)(2,1)S(1)} collective-permute-done((bf16[128,2048]{1,0:T(8,128)(2,1)}, bf16[128,2048]{1,0:T(8,128)(2,1)S(1)}, u32[]{:S(2)}, u32[]{:S(2)}) %collective-permute-start.3) | collective-permute-done | bytes 524320 | tf_op jit(solution)/shard_map/ppermute | solution.py:282
  72.2 0.8 copy-done.1
  73.0 23.5 %inner.1 = (bf16[136,2048]{1,0:T(8,128)(2,1)}, bf16[136,2048]{1,0:T(8,128)(2,1)}, bf16[136,2048]{1,0:T(8,128)(2,1)}, bf16[24,2048]{1,0:T(8,128)(2,1)}, f32[32,8,128]{2,1,0:T(8,128)}) custom-call(bf16[136,2048]{1,0:T(8,128)(2,1)} %get-tuple-element.22.u, bf16[128,2048]{1,0:T(8,128)(2,1)} %copy-done, bf16[136,2048]{1,0:T(8,128)(2,1)} %get-tuple-element.24.d, ...), custom_call_target="tpu_custom_call" | custom-call | flops 3000000000 | bytes 25000000 | tf_op jit(solution)/shard_map/inner/pallas_call | solution.py:225
  96.5 13.0 %all-to-all-start.1 = ((f32[32,8,128]{2,1,0:T(8,128)}), f32[32,8,128]{2,1,0:T(8,128)S(1)}, u32[]{:S(2)}, u32[]{:S(2)}) async-start(f32[32,8,128]{2,1,0:T(8,128)} %get-tuple-element.38), calls=%async_computation.1 | async-start | bytes 262144 | tf_op jit(solution)/shard_map/all_to_all | solution.py:314
  109.5 1.3 collective-permute-start.4
  110.8 9.9 %all-to-all-done.1 = f32[32,8,128]{2,1,0:T(8,128)S(1)} async-done(((f32[32,8,128]{2,1,0:T(8,128)}), f32[32,8,128]{2,1,0:T(8,128)S(1)}, u32[]{:S(2)}, u32[]{:S(2)}) %all-to-all-start.1) | async-done | bytes 131104 | tf_op jit(solution)/shard_map/all_to_all | solution.py:314
  120.8 4.7 %collective-permute-start.5 = (f32[8,128]{1,0:T(8,128)S(1)}, f32[8,128]{1,0:T(8,128)S(1)}, u32[]{:S(2)}, u32[]{:S(2)}) collective-permute-start(f32[8,128]{1,0:T(8,128)S(1)} %reduce_sum.9), channel_id=1, source_target_pairs={{0,0},{1,128},{2,256},{3,384},{4,4},{5,132},{6,260},{7,388},{8,8},... | collective-permute-start | bytes 12296 | tf_op jit(solution)/shard_map/ppermute | solution.py:292
  126.2 4.9 %project.1 = (bf16[136,2048]{1,0:T(8,128)(2,1)}, bf16[136,2048]{1,0:T(8,128)(2,1)}, bf16[136,2048]{1,0:T(8,128)(2,1)}) custom-call(bf16[136,2048]{1,0:T(8,128)(2,1)} %get-tuple-element.31.dq, bf16[136,2048]{1,0:T(8,128)(2,1)} %get-tuple-element.32.dk, bf16[136,2048]{1,0:T(8,128)(2,1)} %get-tuple-element.33.dv, bf16[24,2048]{1,0:T(8,128)(2,1)} %copy-done.4, ...), custom_call_target="tpu_custom_call" | custom-call | flops 30000000 | bytes 4000000 | tf_op jit(solution)/shard_map/project/pallas_call | solution.py:266
  131.0 7.1 %psum.7 = f32[8,128]{1,0:T(8,128)S(1)} all-reduce(f32[8,128]{1,0:T(8,128)S(1)} %collective-permute-done.5), channel_id=1, replica_groups=mesh['x'=4,'z'=8,'yh'=4,'yl'=2,'core'=2] {'yl','core'}, use_global_device_ids=true, to_apply=%region_1.2 | all-reduce | flops 1024 | bytes 8192 | tf_op jit(solution)/shard_map/psum | solution.py:315
  138.7 0.7 rev.3
  (17 shorter events, 1.9 us)
Async XLA Ops:
  1.3 6.8 %collective-permute-start.1 = (bf16[8,128]{1,0:T(8,128)(2,1)S(1)}, bf16[8,128]{1,0:T(8,128)(2,1)S(1)}, u32[]{:S(2)}, u32[]{:S(2)}) collective-permute-start(bf16[8,128]{1,0:T(8,128)(2,1)S(1)} %fusion.1), channel_id=1, source_target_pairs={{0,0},{1,128},{2,256},{3,384},{4,4},{5,132},{6,260},{7,388},{8,8},... | collective-permute-start | bytes 6152 | tf_op jit(solution)/shard_map/ppermute | solution.py:292
  8.8 26.9 %all-to-all-start = ((bf16[32,8,128]{2,1,0:T(8,128)(2,1)}), bf16[32,8,128]{2,1,0:T(8,128)(2,1)S(1)}, u32[]{:S(2)}, u32[]{:S(2)}) async-start(bf16[32,8,128]{2,1,0:T(8,128)(2,1)} %broadcast_in_dim.2), calls=%async_computation | async-start | bytes 131072 | tf_op jit(solution)/shard_map/all_to_all | solution.py:305
  24.5 5.8 %collective-permute-start = (bf16[24,2048]{1,0:T(8,128)(2,1)S(1)}, bf16[24,2048]{1,0:T(8,128)(2,1)S(1)}, u32[]{:S(2)}, u32[]{:S(2)}) collective-permute-start(bf16[24,2048]{1,0:T(8,128)(2,1)S(1)} %pad_maximum_fusion), channel_id=1, source_target_pairs={{0,4},{4,8},{8,12},{12,16},{16,20},{20,24},{24,28},{28,32},{32,36}... | collective-permute-start | bytes 294920 | tf_op jit(solution)/shard_map/ppermute | solution.py:282
  30.2 5.4 %copy-start.2 = (bf16[24,2048]{1,0:T(8,128)(2,1)}, bf16[24,2048]{1,0:T(8,128)(2,1)S(1)}, u32[]{:S(2)}) copy-start(bf16[24,2048]{1,0:T(8,128)(2,1)S(1)} %collective-permute-done.before) | copy-start | bytes 294916
  35.7 0.6 copy-start.3
  42.5 17.5 %collective-permute-start.2 = (bf16[128,2048]{1,0:T(8,128)(2,1)}, bf16[128,2048]{1,0:T(8,128)(2,1)S(1)}, u32[]{:S(2)}, u32[]{:S(2)}) collective-permute-start(bf16[128,2048]{1,0:T(8,128)(2,1)} %get-tuple-element.23), channel_id=1, source_target_pairs={{0,4},{4,8},{8,12},{12,16},{16,20},{20,24},{24,28},{28,32},{32,36}... | collective-permute-start | bytes 1572872 | tf_op jit(solution)/shard_map/ppermute | solution.py:282
  44.9 27.3 %collective-permute-start.3 = (bf16[128,2048]{1,0:T(8,128)(2,1)}, bf16[128,2048]{1,0:T(8,128)(2,1)S(1)}, u32[]{:S(2)}, u32[]{:S(2)}) collective-permute-start(bf16[128,2048]{1,0:T(8,128)(2,1)} %get-tuple-element.25), channel_id=1, source_target_pairs={{4,0},{8,4},{12,8},{16,12},{20,16},{24,20},{28,24},{32,28},{36,32}... | collective-permute-start | bytes 1572872 | tf_op jit(solution)/shard_map/ppermute | solution.py:282
  60.1 12.2 %copy-start = (bf16[128,2048]{1,0:T(8,128)(2,1)}, bf16[128,2048]{1,0:T(8,128)(2,1)S(1)}, u32[]{:S(2)}) copy-start(bf16[128,2048]{1,0:T(8,128)(2,1)S(1)} %collective-permute-done.2.u_halo) | copy-start | bytes 1572868
  72.2 0.8 copy-start.1
  96.5 24.2 %all-to-all-start.1 = ((f32[32,8,128]{2,1,0:T(8,128)}), f32[32,8,128]{2,1,0:T(8,128)S(1)}, u32[]{:S(2)}, u32[]{:S(2)}) async-start(f32[32,8,128]{2,1,0:T(8,128)} %get-tuple-element.38), calls=%async_computation.1 | async-start | bytes 262144 | tf_op jit(solution)/shard_map/all_to_all | solution.py:314
  109.5 16.0 %collective-permute-start.4 = (bf16[24,2048]{1,0:T(8,128)(2,1)}, bf16[24,2048]{1,0:T(8,128)(2,1)S(1)}, u32[]{:S(2)}, u32[]{:S(2)}) collective-permute-start(bf16[24,2048]{1,0:T(8,128)(2,1)} %get-tuple-element.34), channel_id=1, source_target_pairs={{4,0},{8,4},{12,8},{16,12},{20,16},{24,20},{28,24},{32,28},{36,32}... | collective-permute-start | bytes 294920 | tf_op jit(solution)/shard_map/ppermute | solution.py:282
  120.8 10.2 %collective-permute-start.5 = (f32[8,128]{1,0:T(8,128)S(1)}, f32[8,128]{1,0:T(8,128)S(1)}, u32[]{:S(2)}, u32[]{:S(2)}) collective-permute-start(f32[8,128]{1,0:T(8,128)S(1)} %reduce_sum.9), channel_id=1, source_target_pairs={{0,0},{1,128},{2,256},{3,384},{4,4},{5,132},{6,260},{7,388},{8,8},... | collective-permute-start | bytes 12296 | tf_op jit(solution)/shard_map/ppermute | solution.py:292
  125.6 0.6 copy-start.4

commit v2 on v1

v2 whole, which is shorter than its diff:
```python
import jax
import jax.numpy as jnp
from jax import lax
from jax.experimental import pallas as pl
from jax.experimental.pallas import tpu as pltpu
from jax.sharding import Mesh, PartitionSpec as P

F32 = jnp.float32
BF16 = jnp.bfloat16
CPG = 16
KS = 7
KB = 128
LANES = 128
GPB = LANES // CPG
HALO = 8
CTX = ("x", "z", "yh")
MP = ("yl", "core")
ALL = CTX + MP
SIZES = (4, 8, 4, 4)
VMEM = 56 * 1024 * 1024


def params(**more):
    return pltpu.CompilerParams(vmem_limit_bytes=VMEM, **more)


def lane_group(shape):
    return lax.broadcasted_iota(jnp.int32, shape, len(shape) - 1) // CPG


def short_taps(taps):
    row = lax.broadcasted_iota(jnp.int32, (16, LANES), 0)
    group = jnp.where(row % 8 >= 4, row // 8 * 4 + row % 4, -1)
    spread = (lane_group((16, LANES)) == group).astype(F32)
    return lax.dot_general(
        taps[:, :LANES].T, spread, (((1,), (0,)), ((), ())), precision=lax.Precision.HIGHEST,
        preferred_element_type=F32,
    )[:8]


def fused_kernel(
    q, k, v, g, below, above, taps, gq, gk, gv, part,
    qs, ks, vs, feats, tc, ta, prod, last, medium,
):
    rows = q.shape[0]
    near = rows + 8
    lane = lax.broadcasted_iota(jnp.int32, (16, LANES), 1)
    row = lax.broadcasted_iota(jnp.int32, (16, LANES), 0)
    both = taps[...].reshape(16, LANES)
    straight = both.astype(F32)
    h = short_taps(straight)

    at = lax.broadcasted_iota(jnp.int32, (LANES, LANES), 0)
    to = lax.broadcasted_iota(jnp.int32, (LANES, LANES), 1)
    flip = (at + to == LANES - 1).astype(BF16)
    turned = jnp.dot(both, flip, preferred_element_type=F32)
    for i in range(GPB):
        line = i // 4 * 8 + i % 4
        for out, lines, first in ((tc, turned, 1), (ta, straight, 0)):
            base = pltpu.roll(
                jnp.broadcast_to(lines[line : line + 1], (16, LANES)), first, 1, stride=1, stride_axis=0
            )
            for a in range(KB // 16):
                tile = pltpu.roll(base, 16 * a, 1) if a else base
                if first:
                    upper = lane > row + 16 * a
                else:
                    upper = lane >= row + 16 * a
                place = slice(i * KB + 16 * a, i * KB + 16 * a + 16)
                out[place, :KB] = jnp.where(upper, tile, 0.0).astype(BF16)
                out[place, KB:] = jnp.where(upper, 0.0, tile).astype(BF16)

    early, late = below[...].astype(F32), above[...].astype(F32)
    ks[0:rows] = early[:rows]
    ks[rows : 2 * rows] = k[...].astype(F32)
    ks[2 * rows : 2 * rows + 8] = late[2 * rows : 2 * rows + 8]
    vs[0:rows] = early[rows : 2 * rows]
    vs[rows : 2 * rows] = v[...].astype(F32)
    vs[2 * rows : 2 * rows + 8] = late[2 * rows + 8 :]
    qs[0:8] = early[2 * rows + 8 :]
    qs[8 : rows + 8] = q[...].astype(F32)
    qs[rows + 8 : 2 * rows + 8] = late[:rows]

    def causal(slot):
        count = 2 * rows
        total = h[0:1] * slot[8 : 8 + count]
        for j in range(1, KS):
            total = total + h[j : j + 1] * slot[8 - j : 8 - j + count]
        return total.astype(BF16)

    kf, vf, qf = causal(ks), causal(vs), causal(qs)
    gate = jnp.concatenate([g[...].astype(F32), late[rows : 2 * rows]], 0)
    uw = kf.astype(F32) * vf.astype(F32)
    dw = gate * qf.astype(F32)
    u_low, u_high = uw[: 2 * KB].astype(BF16), uw[16:].astype(BF16)
    d_low, d_high = dw[: 2 * KB].astype(BF16), dw[16:].astype(BF16)

    prod[:, :LANES] = jnp.dot(tc[...], u_low, preferred_element_type=F32)
    z_low = pick_groups(prod.at[:, :LANES], KB, 0, KB)
    tails = jnp.concatenate([tc[(i + 1) * KB - 16 : (i + 1) * KB] for i in range(GPB)], 0)
    z_high = pick_groups(jnp.dot(tails, u_high, preferred_element_type=F32), 16, 0, 16)
    z = jnp.concatenate([z_low, z_high], 0)
    feats[0] = (gate[:near] * z).astype(BF16).astype(F32)

    prod[:, LANES:] = jnp.dot(ta[...], d_high, preferred_element_type=F32)
    du_high = pick_groups(prod.at[:, LANES:], KB, 0, KB)
    heads = jnp.concatenate([ta[i * KB : i * KB + 16] for i in range(GPB)], 0)
    du_low = pick_groups(jnp.dot(heads, d_low, preferred_element_type=F32), 16, 0, 16)
    du = jnp.concatenate([du_low, du_high], 0)
    feats[1] = (du * vf[KB:].astype(F32)).astype(BF16).astype(F32)
    feats[2] = (du * kf[KB:].astype(F32)).astype(BF16).astype(F32)

    sums = [jnp.zeros((1, LANES), F32)] * 8
    for i, (slot, base, out) in enumerate(((qs, 8, gq), (ks, rows, gk), (vs, rows, gv))):
        wide = feats[i, 0:rows]
        for j in range(KS):
            sums[j] = sums[j] + jnp.sum(wide * slot[base - j : base - j + rows], 0, keepdims=True)
        total = h[0:1] * wide
        for j in range(1, KS):
            total = total + h[j : j + 1] * feats[i, j : j + rows]
        out[...] = total.astype(BF16)
    short = jnp.concatenate(sums + [jnp.zeros((LANES - 8, LANES), F32)], 0)
    gather = (lane_group((8, LANES)) == lax.broadcasted_iota(jnp.int32, (8, LANES), 0)).astype(F32)
    short = lax.dot_general(
        gather, short, (((1,), (1,)), ((), ())), precision=lax.Precision.HIGHEST,
        preferred_element_type=F32,
    )

    own = jnp.concatenate([dw[:rows], jnp.zeros((8, LANES), F32)], 0)
    groups = lane_group((near, LANES))
    masked = [jnp.where(groups == i, own, 0.0) for i in range(GPB)]
    contract = (((1,), (1,)), ((), ()))
    prod[...] = lax.dot_general(
        jnp.concatenate([m[:KB] for m in masked], 0).astype(BF16), u_low, contract,
        preferred_element_type=F32,
    )
    last[...] = lax.dot_general(
        jnp.concatenate([m[KB:] for m in masked], 0).astype(BF16), u_high, contract,
        preferred_element_type=F32,
    )
    lane8, row8 = lane[:8], row[:8]
    for i in range(GPB):
        total = None
        for a in range(KB // 8):
            tile = prod[i * KB + 8 * a : i * KB + 8 * a + 8]
            if a == KB // 8 - 2:
                tile = tile + last[16 * i : 16 * i + 8]
            tile = jnp.where(lane8 > row8 + 8 * a, tile[:, :KB], tile[:, KB:])
            total = tile if a == 0 else total + pltpu.roll(tile, KB - 8 * a, 1)
        line = jnp.sum(align_left(total), 0, keepdims=True)
        medium[i : i + 1] = pltpu.roll(line, KB - 1, 1)
    ahead = jnp.dot(
        medium[...], flip.astype(F32), precision=lax.Precision.HIGHEST, preferred_element_type=F32
    )
    for half in range(2):
        part[half, 0:4] = ahead[4 * half : 4 * half + 4]
        part[half, 4:8] = short[4 * half : 4 * half + 4]


def fused(q, k, v, g, below, above, taps, interpret=False):
    rows, channels = q.shape
    blocks = channels // LANES
    block = lambda r: pl.BlockSpec((r, LANES), lambda i: (0, i))
    chunk = pl.BlockSpec((2, 8, LANES), lambda i: (i, 0, 0))
    return pl.pallas_call(
        fused_kernel,
        grid=(blocks,),
        in_specs=[block(rows)] * 4 + [block(2 * rows + 16)] * 2 + [chunk],
        out_specs=[block(rows)] * 3 + [chunk],
        out_shape=[jax.ShapeDtypeStruct((rows, channels), BF16)] * 3
        + [jax.ShapeDtypeStruct((2 * blocks, 8, LANES), F32)],
        scratch_shapes=[pltpu.VMEM((2 * rows + 8, LANES), F32)] * 3
        + [
            pltpu.VMEM((3, rows + 8, LANES), F32),
            pltpu.VMEM((GPB * KB, 2 * KB), BF16),
            pltpu.VMEM((GPB * KB, 2 * KB), BF16),
            pltpu.VMEM((GPB * KB, 2 * KB), F32),
            pltpu.VMEM((GPB * 16, 2 * KB), F32),
            pltpu.VMEM((GPB, LANES), F32),
        ],
        compiler_params=params(),
        cost_estimate=pl.CostEstimate(flops=4_000_000_000, bytes_accessed=10_000_000, transcendentals=0),
        interpret=interpret,
        name="fused",
    )(q, k, v, g, below, above, taps)


def pick_groups(stacked, rows, start, count):
    groups = lane_group((count, LANES))
    out = stacked[start : start + count]
    for g in range(1, GPB):
        out = jnp.where(groups == g, stacked[g * rows + start : g * rows + start + count], out)
    return out


def align_left(tile):
    width = tile.shape[1]
    row = lax.broadcasted_iota(jnp.int32, tile.shape, 0)
    for bit in (1, 2, 4):
        tile = jnp.where(row // bit % 2 == 1, pltpu.roll(tile, width - bit, 1), tile)
    return tile


def step_ctx(value, step):
    count = lax.axis_size(CTX)
    return lax.ppermute(value, CTX, [(i, i + step) for i in range(count) if 0 <= i + step < count])


def swap_x_mp(value):
    nx, nz, ny, nm = SIZES
    at = lambda x, z, y, m: ((x * nz + z) * ny + y) * nm + m
    pairs = [
        (at(x, z, y, m), at(m, z, y, x))
        for x in range(nx) for z in range(nz) for y in range(ny) for m in range(nm)
    ]
    return lax.ppermute(value, ALL, pairs)


def pack_taps(filt_short, filt_medium):
    short = jnp.pad(filt_short.T, ((0, 0), (0, LANES - KS)))
    return jnp.concatenate([filt_medium.T, short], 0)


def shards(q, k, v, g, filt_short, filt_medium):
    rows = q.shape[0]
    own, lower, upper = lax.optimization_barrier((
        swap_x_mp(pack_taps(filt_short, filt_medium)),
        jnp.concatenate([k, v, q[rows - 16 :]], 0),
        jnp.concatenate([q, g, k[:8], v[:8]], 0),
    ))
    below, above = step_ctx(lower, 1), step_ctx(upper, -1)
    taps = lax.all_to_all(
        jnp.broadcast_to(own[None], (32, 8, LANES)), ("z", "yh"), 0, 0, tiled=True
    )
    grad_q, grad_k, grad_v, part = fused(q, k, v, g, below, above, taps)
    pieces = lax.all_to_all(part, ("z", "yh"), 0, 0, tiled=True)
    total = lax.psum(swap_x_mp(jnp.sum(pieces, 0)), MP)
    return grad_q, grad_k, grad_v, total[4:8, :KS].T, total[0:4].T


def solution(mesh):
    fine = Mesh(mesh.devices.reshape(4, 8, 4, 2, 2), ALL)
    signal = P(CTX, MP)
    taps = P(None, CTX)
    return jax.shard_map(
        shards,
        mesh=fine,
        in_specs=(signal,) * 4 + (taps,) * 2,
        out_specs=(signal,) * 3 + (taps,) * 2,
        check_vma=False,
    )
```

time: 141 us -> 157 us (1.11)
  blocking collectives: 7.09 us -> 94.9 us
  starting transfers between devices: 46.9 us -> 13.8 us
  waiting for transfers between devices: 29.2 us -> 1.28 us
  Pallas kernels: 48.5 us -> 38 us
  other arithmetic: 0.75 us -> 2.46 us
    all_to_all x0 -> x2, blocking collectives: none -> 83 us  [the longest x1 59.4 us: shards(): lax.all_to_all(jnp.broadcast_to(own[None], (32, 8, LANES)), ('z', 'yh'),...]
    all_to_all x2 -> x0, starting transfers between devices: 28.7 us -> none  [the longest x1 15.7 us: shards(): lax.all_to_all(jnp.broadcast_to(own[None], (32, 8, LANES)), ('z', 'yh'),...]
    all_to_all x2 -> x0, waiting for transfers between devices: 15.3 us -> none  [the longest x1 9.94 us: shards(): pieces = lax.all_to_all(part, ('z', 'yh'), 0, 0, tiled=True)]
    ppermute x4 -> x2, waiting for transfers between devices: 13.9 us -> 0.01 us  [step_ctx(): lax.ppermute(value, CTX, [(i, i + step) for i in range(count) if 0 <= i +...]
    pallas_call x4 -> x1, Pallas kernels: 48.5 us -> 38 us  [fused(): pl.pallas_call(fused_kernel, grid=(blocks,), in_specs=[block(rows)] * 4 +...]
    psum x1, blocking collectives: 7.09 us -> 11.9 us  [shards(): total = lax.psum(swap_x_mp(jnp.sum(pieces, 0)), MP)]
    ppermute x4 -> x2, starting transfers between devices: 9.02 us -> 5.58 us  [step_ctx(): lax.ppermute(value, CTX, [(i, i + step) for i in range(count) if 0 <= i +...]
    concatenate x1, other arithmetic: 0.01 us -> 1.71 us  [shards(): jnp.concatenate([k, v, q[rows - 16:]], 0)]
  transfers between devices with their start and end apart: 8 -> 4, of which waited for: 4 -> 1; matrix products, arithmetic and copies ran while one was open for 2% -> 3% of each run, Pallas kernels for 13% -> 0%
where the time goes in v2:
time: 157 us
  blocking collectives  94.9 us (60%)
  Pallas kernels  38 us (24%)
  starting transfers between devices  13.8 us (9%)
  local copies, waits for them, and re-layouts  5.61 us (4%)
  other arithmetic  2.46 us (2%)
    all_to_all x1, blocking collectives, shards(): lax.all_to_all(jnp.broadcast_to(own[None], (32, 8, LANES)), ('z', 'yh'),...  59.4 us
    pallas_call x1, Pallas kernels, fused(): pl.pallas_call(fused_kernel, grid=(blocks,), in_specs=[block(rows)] * 4 +...  38 us
    all_to_all x1, blocking collectives, shards(): pieces = lax.all_to_all(part, ('z', 'yh'), 0, 0, tiled=True)  23.7 us
    psum x1, blocking collectives, shards(): total = lax.psum(swap_x_mp(jnp.sum(pieces, 0)), MP)  11.9 us
    ppermute x2, starting transfers between devices, swap_x_mp(): return lax.ppermute(value, ALL, pairs)  8.18 us
    ppermute x2, starting transfers between devices, step_ctx(): lax.ppermute(value, CTX, [(i, i + step) for i in range(count) if 0 <= i +...  5.58 us
  transfers between devices with their start and end apart: 4, of which 1 were waited for; matrix products, arithmetic and copies ran while one was open for 3% of the time, Pallas kernels for 0%

profile of v2, /device:TPU:1, one launch (start us, length us, event | category | flops | bytes accessed | tf_op | source)
XLA Modules:
  0.0 156.7 jit_solution(4989871738462885908)
XLA Ops:
  0.6 0.7 fusion.1
  1.3 4.5 %collective-permute-start = (bf16[8,128]{1,0:T(8,128)(2,1)S(1)}, bf16[8,128]{1,0:T(8,128)(2,1)S(1)}, u32[]{:S(2)}, u32[]{:S(2)}) collective-permute-start(bf16[8,128]{1,0:T(8,128)(2,1)S(1)} %fusion.1), channel_id=1, source_target_pairs={{0,0},{1,128},{2,256},{3,384},{4,4},{5,132},{6,260},{7,388},{8,8},... | collective-permute-start | bytes 6152 | tf_op jit(solution)/shard_map/ppermute | solution.py:216
  5.8 0.8 slice.16
  6.6 0.8 slice.17
  7.4 0.8 slice.15
  8.2 1.7 %pad_maximum_fusion = (bf16[288,2048]{1,0:T(8,128)(2,1)S(1)}, bf16[288,2048]{1,0:T(8,128)(2,1)S(1)}) fusion(bf16[16,2048]{1,0:T(8,128)(2,1)S(1)} %slice.15, bf16[136,2048]{1,0:T(8,128)(2,1)} %v.1, bf16[136,2048]{1,0:T(8,128)(2,1)} %k.1, bf16[8,2048]{1,0:T(8,128)(2,1)S(1)} %slice.17, bf16[8,2048]{1,0:T(8,128)(2,1)S(1)} %slice.16, bf16[136,2048]{1,0:T(8,128)(2,1)} %g.1, ...), kind=kLoop, calls=%fused_computation | loop fusion | flops 8257536 | bytes 4718592 | tf_op jit(solution)/shard_map/concatenate | solution.py:228
  9.9 0.0 collective-permute-done
  9.9 4.3 %collective-permute-start.1 = (bf16[288,2048]{1,0:T(8,128)(2,1)S(1)}, bf16[288,2048]{1,0:T(8,128)(2,1)S(1)}, u32[]{:S(2)}, u32[]{:S(2)}) collective-permute-start(bf16[288,2048]{1,0:T(8,128)(2,1)S(1)} %get-tuple-element.12), channel_id=1, source_target_pairs={{0,4},{4,8},{8,12},{12,16},{16,20},{20,24},{24,28},{28,32},{32,36}... | collective-permute-start | bytes 3538952 | tf_op jit(solution)/shard_map/ppermute | solution.py:206
  14.2 1.3 collective-permute-start.2
  15.6 59.4 %all_to_all.10.taps = bf16[32,8,128]{2,1,0:T(8,128)(2,1)} all-to-all(bf16[32,8,128]{2,1,0:T(8,128)(2,1)S(1)} %broadcast_in_dim.2), channel_id=1, replica_groups=mesh['x'=4,'z'=8,'yh'=4,'yl'=2,'core'=2] {'z','yh'}, dimensions={0} | all-to-all | bytes 131072 | tf_op jit(solution)/shard_map/all_to_all | solution.py:232
  74.9 0.0 collective-permute-done.1.below
  74.9 0.0 copy-start
  74.9 0.0 collective-permute-done.2.above
  74.9 1.0 copy-done
  75.9 0.0 copy-start.1
  75.9 1.1 copy-done.1
  77.0 38.0 %fused.1 = (bf16[136,2048]{1,0:T(8,128)(2,1)}, bf16[136,2048]{1,0:T(8,128)(2,1)}, bf16[136,2048]{1,0:T(8,128)(2,1)}, f32[32,8,128]{2,1,0:T(8,128)}) custom-call(bf16[136,2048]{1,0:T(8,128)(2,1)} %q.1, bf16[136,2048]{1,0:T(8,128)(2,1)} %k.1, bf16[136,2048]{1,0:T(8,128)(2,1)} %v.1, bf16[136,2048]{1,0:T(8,128)(2,1)} %g.1, bf16[288,2048]{1,0:T(8,128)(2,1)} %copy-done, ...), custom_call_target="tpu_custom_call" | custom-call | flops 4000000000 | bytes 10000000 | tf_op jit(solution)/shard_map/fused/pallas_call | solution.py:165
  115.0 23.7 %all_to_all.11 = f32[32,8,128]{2,1,0:T(8,128)S(1)} all-to-all(f32[32,8,128]{2,1,0:T(8,128)} %get-tuple-element.18), channel_id=1, replica_groups=mesh['x'=4,'z'=8,'yh'=4,'yl'=2,'core'=2] {'z','yh'}, dimensions={0} | all-to-all | bytes 262144 | tf_op jit(solution)/shard_map/all_to_all | solution.py:236
  138.7 3.7 %collective-permute-start.3 = (f32[8,128]{1,0:T(8,128)S(1)}, f32[8,128]{1,0:T(8,128)S(1)}, u32[]{:S(2)}, u32[]{:S(2)}) collective-permute-start(f32[8,128]{1,0:T(8,128)S(1)} %reduce_sum.9), channel_id=1, source_target_pairs={{0,0},{1,128},{2,256},{3,384},{4,4},{5,132},{6,260},{7,388},{8,8},... | collective-permute-start | bytes 12296 | tf_op jit(solution)/shard_map/ppermute | solution.py:216
  142.4 1.3 collective-permute-done.3
  143.6 11.9 %psum.7 = f32[8,128]{1,0:T(8,128)S(1)} all-reduce(f32[8,128]{1,0:T(8,128)S(1)} %collective-permute-done.3), channel_id=1, replica_groups=mesh['x'=4,'z'=8,'yh'=4,'yl'=2,'core'=2] {'yl','core'}, use_global_device_ids=true, to_apply=%region_1.2 | all-reduce | flops 1024 | bytes 8192 | tf_op jit(solution)/shard_map/psum | solution.py:237
  155.5 0.6 slice_bitcast_fusion
  156.1 0.6 slice_bitcast_fusion.1
  (2 shorter events, 0.0 us)
Async XLA Ops:
  1.3 8.6 %collective-permute-start = (bf16[8,128]{1,0:T(8,128)(2,1)S(1)}, bf16[8,128]{1,0:T(8,128)(2,1)S(1)}, u32[]{:S(2)}, u32[]{:S(2)}) collective-permute-start(bf16[8,128]{1,0:T(8,128)(2,1)S(1)} %fusion.1), channel_id=1, source_target_pairs={{0,0},{1,128},{2,256},{3,384},{4,4},{5,132},{6,260},{7,388},{8,8},... | collective-permute-start | bytes 6152 | tf_op jit(solution)/shard_map/ppermute | solution.py:216
  9.9 65.0 %collective-permute-start.1 = (bf16[288,2048]{1,0:T(8,128)(2,1)S(1)}, bf16[288,2048]{1,0:T(8,128)(2,1)S(1)}, u32[]{:S(2)}, u32[]{:S(2)}) collective-permute-start(bf16[288,2048]{1,0:T(8,128)(2,1)S(1)} %get-tuple-element.12), channel_id=1, source_target_pairs={{0,4},{4,8},{8,12},{12,16},{16,20},{20,24},{24,28},{28,32},{32,36}... | collective-permute-start | bytes 3538952 | tf_op jit(solution)/shard_map/ppermute | solution.py:206
  14.2 60.7 %collective-permute-start.2 = (bf16[288,2048]{1,0:T(8,128)(2,1)S(1)}, bf16[288,2048]{1,0:T(8,128)(2,1)S(1)}, u32[]{:S(2)}, u32[]{:S(2)}) collective-permute-start(bf16[288,2048]{1,0:T(8,128)(2,1)S(1)} %get-tuple-element.13), channel_id=1, source_target_pairs={{4,0},{8,4},{12,8},{16,12},{20,16},{24,20},{28,24},{32,28},{36,32}... | collective-permute-start | bytes 3538952 | tf_op jit(solution)/shard_map/ppermute | solution.py:206
  74.9 1.0 copy-start
  75.9 1.1 copy-start.1
  138.7 5.0 %collective-permute-start.3 = (f32[8,128]{1,0:T(8,128)S(1)}, f32[8,128]{1,0:T(8,128)S(1)}, u32[]{:S(2)}, u32[]{:S(2)}) collective-permute-start(f32[8,128]{1,0:T(8,128)S(1)} %reduce_sum.9), channel_id=1, source_target_pairs={{0,0},{1,128},{2,256},{3,384},{4,4},{5,132},{6,260},{7,388},{8,8},... | collective-permute-start | bytes 12296 | tf_op jit(solution)/shard_map/ppermute | solution.py:216

commit v3 on v2

v3 whole, which is shorter than its diff:
```python
import functools

import jax
import jax.numpy as jnp
from jax import lax
from jax.experimental import pallas as pl
from jax.experimental.pallas import tpu as pltpu
from jax.sharding import Mesh, PartitionSpec as P

F32 = jnp.float32
BF16 = jnp.bfloat16
CPG = 16
KS = 7
KB = 128
LANES = 128
GPB = LANES // CPG
HALO = 8
CTX = ("x", "z", "yh")
MP = ("yl", "core")
ALL = CTX + MP
SIZES = (4, 8, 4, 4)
VMEM = 12 * 1024 * 1024


def params(**more):
    return pltpu.CompilerParams(vmem_limit_bytes=VMEM, **more)


def lane_group(shape):
    return lax.broadcasted_iota(jnp.int32, shape, len(shape) - 1) // CPG


def short_taps(taps):
    row = lax.broadcasted_iota(jnp.int32, (16, LANES), 0)
    group = jnp.where(row % 8 >= 4, row // 8 * 4 + row % 4, -1)
    spread = (lane_group((16, LANES)) == group).astype(BF16)
    return lax.dot_general(taps, spread, (((0,), (0,)), ((), ())), preferred_element_type=F32)[:8]


def fused_kernel(raw, q, k, v, g, below, above, extra, taps, *rest_refs):
    gq, gk, gv, part, qs, ks, vs, feats = rest_refs[-8:]
    rows = q.shape[0]
    near = rows + 8
    both = taps[...].reshape(16, LANES)
    h = short_taps(both)

    def causal(slot, count):
        total = h[0:1] * slot[8 : 8 + count]
        for j in range(1, KS):
            total = total + h[j : j + 1] * slot[8 - j : 8 - j + count]
        return total.astype(BF16).astype(F32)

    early, late = below[...].astype(F32), above[...].astype(F32)
    if raw:
        ks[0:rows] = early[:rows]
        ks[rows : 2 * rows] = k[...].astype(F32)
        ks[2 * rows : 2 * rows + 8] = late[2 * rows : 2 * rows + 8]
        vs[0:rows] = early[rows : 2 * rows]
        vs[rows : 2 * rows] = v[...].astype(F32)
        vs[2 * rows : 2 * rows + 8] = late[2 * rows + 8 :]
        qs[0:8] = early[2 * rows + 8 :]
        qs[8 : rows + 8] = q[...].astype(F32)
        qs[rows + 8 : 2 * rows + 8] = late[:rows]
        kf, vf, qf = (causal(x, 2 * rows) for x in (ks, vs, qs))
        gate = jnp.concatenate([g[...].astype(F32), late[rows : 2 * rows]], 0)
        uw = kf * vf
        dw = gate * qf
        kf, vf = kf[KB:], vf[KB:]
        own_at = rows
    else:
        tails = extra[...].astype(F32)
        for i, (slot, x) in enumerate(((ks, k), (vs, v), (qs, q))):
            slot[0:8] = tails[16 * i + 8 : 16 * i + 16]
            slot[8 : rows + 8] = x[...].astype(F32)
        kf, vf, qf = (causal(x, rows) for x in (ks, vs, qs))
        gate = jnp.concatenate([g[...].astype(F32), late[rows : rows + 8]], 0)
        kf = jnp.concatenate([kf, late[rows + 8 : rows + 16]], 0)
        vf = jnp.concatenate([vf, late[rows + 16 :]], 0)
        uw = jnp.concatenate([early, kf * vf], 0)
        dw = jnp.concatenate([gate[:rows] * qf, late[:rows]], 0)
        own_at = 8
    u_low, u_high = uw[: 2 * KB].astype(BF16), uw[16:].astype(BF16)
    d_low, d_high = dw[: 2 * KB].astype(BF16), dw[16:].astype(BF16)
    own = jnp.concatenate([dw[:rows], jnp.zeros((8, LANES), F32)], 0).astype(BF16)

    at = lax.broadcasted_iota(jnp.int32, (LANES, LANES), 0)
    to = lax.broadcasted_iota(jnp.int32, (LANES, LANES), 1)
    flip = (at + to == LANES - 1).astype(BF16)
    straight = both.astype(F32)
    turned = jnp.dot(both, flip, preferred_element_type=F32)
    lane = lax.broadcasted_iota(jnp.int32, (16, LANES), 1)
    row = lax.broadcasted_iota(jnp.int32, (16, LANES), 0)
    lane8, row8 = lane[:8], row[:8]
    contract = (((1,), (1,)), ((), ()))
    wide = lane_group((2 * KB, LANES))

    def square(line, first):
        base = pltpu.roll(jnp.broadcast_to(line, (16, LANES)), first, 1, stride=1, stride_axis=0)
        tiles = []
        for a in range(KB // 16):
            tile = pltpu.roll(base, 16 * a, 1) if a else base
            upper = lane > row + 16 * a if first else lane >= row + 16 * a
            parts = [jnp.where(upper, tile, 0.0), jnp.where(upper, 0.0, tile)]
            tiles.append(jnp.concatenate(parts, 1).astype(BF16))
        return tiles

    z_low = du_high = jnp.zeros((KB, LANES), F32)
    tails, heads, medium = [], [], []
    rest = jnp.concatenate([jnp.where(wide[:16] == i, own[KB:], 0) for i in range(GPB)], 0)
    last = lax.dot_general(rest, u_high, contract, preferred_element_type=F32)
    for i in range(GPB):
        line = i // 4 * 8 + i % 4
        tc = square(turned[line : line + 1], 1)
        ta = square(straight[line : line + 1], 0)
        tails.append(tc[-1])
        heads.append(ta[0])
        z_low = z_low + jnp.dot(
            jnp.concatenate(tc, 0), jnp.where(wide == i, u_low, 0), preferred_element_type=F32
        )
        du_high = du_high + jnp.dot(
            jnp.concatenate(ta, 0), jnp.where(wide == i, d_high, 0), preferred_element_type=F32
        )
        mine = jnp.where(wide[:KB] == i, own[:KB], 0)
        prod = lax.dot_general(mine, u_low, contract, preferred_element_type=F32)
        total = None
        for a in range(KB // 8):
            tile = prod[8 * a : 8 * a + 8]
            if a == KB // 8 - 2:
                tile = tile + last[16 * i : 16 * i + 8]
            tile = jnp.where(lane8 > row8 + 8 * a, tile[:, :KB], tile[:, KB:])
            total = tile if a == 0 else total + pltpu.roll(tile, KB - 8 * a, 1)
        medium.append(jnp.sum(align_left(total), 0, keepdims=True))
    for half in range(2):
        part[half, 0, 0:4] = jnp.concatenate(medium[4 * half : 4 * half + 4], 0)

    z_high = pick_groups(
        jnp.dot(jnp.concatenate(tails, 0), u_high, preferred_element_type=F32), 16, 0, 16
    )
    du_low = pick_groups(
        jnp.dot(jnp.concatenate(heads, 0), d_low, preferred_element_type=F32), 16, 0, 16
    )
    z = jnp.concatenate([z_low, z_high], 0)
    du = jnp.concatenate([du_low, du_high], 0)
    feats[0] = (gate[:near] * z).astype(BF16).astype(F32)
    feats[1] = (du * vf).astype(BF16).astype(F32)
    feats[2] = (du * kf).astype(BF16).astype(F32)

    sums = [jnp.zeros((8, LANES), F32)] * 8
    for i, (slot, base, out) in enumerate(((qs, 8, gq), (ks, own_at, gk), (vs, own_at, gv))):
        wide_feat = feats[i, 0:rows]
        for j in range(KS):
            both_rows = wide_feat * slot[base - j : base - j + rows]
            sums[j] = sums[j] + jnp.sum(both_rows.reshape(rows // 8, 8, LANES), 0)
        total = h[0:1] * wide_feat
        for j in range(1, KS):
            total = total + h[j : j + 1] * feats[i, j : j + rows]
        out[...] = total.astype(BF16)
    short = jnp.concatenate([jnp.sum(x, 0, keepdims=True) for x in sums], 0)
    swapped = pltpu.roll(short, LANES // 2, 1)
    left = lane[:4] < LANES // 2
    part[0, 0, 4:8] = jnp.where(left, short[:4], swapped[4:])
    part[1, 0, 4:8] = jnp.where(left, swapped[:4], short[4:])


def fused(raw, q, k, v, g, below, above, extra, taps, first, count, written=None, interpret=False):
    rows, channels = q.shape
    every = channels // LANES
    block = lambda r: pl.BlockSpec((r, LANES), lambda i: (0, first + i))
    chunk = pl.BlockSpec((2, 1, 8, LANES), lambda i: ((first + i) % 2, (first + i) // 2, 0, 0))
    written = () if written is None else tuple(written)
    depth = 2 * rows + 8 if raw else rows + 8
    return pl.pallas_call(
        functools.partial(fused_kernel, raw),
        grid=(count,),
        in_specs=[block(rows)] * 4
        + [
            pl.BlockSpec((2 * rows + 16 if raw else KB, LANES), lambda i: (0, i)),
            pl.BlockSpec((2 * rows + 16 if raw else rows + 24, LANES), lambda i: (0, i)),
            pl.BlockSpec((48, LANES), lambda i: (0, i)),
            chunk,
        ]
        + [pl.BlockSpec(memory_space=pl.ANY)] * len(written),
        out_specs=[block(rows)] * 3 + [chunk],
        out_shape=[jax.ShapeDtypeStruct((rows, channels), BF16)] * 3
        + [jax.ShapeDtypeStruct((4, every // 2, 8, LANES), F32)],
        scratch_shapes=[pltpu.VMEM((depth, LANES), F32)] * 3
        + [pltpu.VMEM((3, rows + 8, LANES), F32)],
        input_output_aliases={8 + n: n for n in range(len(written))},
        compiler_params=params(),
        cost_estimate=pl.CostEstimate(
            flops=250_000_000 * count, bytes_accessed=500_000 * count, transcendentals=0
        ),
        interpret=interpret,
        name="fused_raw" if raw else "fused_sent",
    )(q, k, v, g, below, above, extra, taps, *written)


def pack_kernel(q, k, v, g, qb, kb, vb, lower, upper, tails):
    rows = q.shape[0]
    tail = lambda x: x[...].astype(F32)[rows - 16 :]
    lower[...] = jnp.concatenate(
        [k[...].astype(F32), v[...].astype(F32), tail(q)], 0
    ).astype(BF16)
    tails[...] = jnp.concatenate([tail(kb), tail(vb), tail(qb)], 0).astype(BF16)
    upper[...] = jnp.concatenate(
        [q[...].astype(F32), g[...].astype(F32), k[...].astype(F32)[:8], v[...].astype(F32)[:8]], 0
    ).astype(BF16)


def pack(q, k, v, g, split, interpret=False):
    rows, channels = q.shape
    wide = 256
    assert channels == 2 * split
    low = lambda r: pl.BlockSpec((r, wide), lambda i: (0, i))
    high = pl.BlockSpec((rows, wide), lambda i: (0, split // wide + i))
    return pl.pallas_call(
        pack_kernel,
        grid=(split // wide,),
        in_specs=[low(rows)] * 4 + [high] * 3,
        out_specs=[low(2 * rows + 16), low(2 * rows + 16), low(48)],
        out_shape=[
            jax.ShapeDtypeStruct((2 * rows + 16, split), BF16),
            jax.ShapeDtypeStruct((2 * rows + 16, split), BF16),
            jax.ShapeDtypeStruct((48, split), BF16),
        ],
        compiler_params=params(),
        interpret=interpret,
        name="pack",
    )(q, k, v, g, q, k, v)


def products_kernel(q, k, v, g, extra, taps, lower, upper, qs, ks, vs):
    rows = q.shape[0]
    h = short_taps(taps[...].reshape(16, LANES))
    tails = extra[...].astype(F32)
    made = []
    for i, (slot, x) in enumerate(((ks, k), (vs, v), (qs, q))):
        slot[0:8] = tails[16 * i + 8 : 16 * i + 16]
        slot[8 : rows + 8] = x[...].astype(F32)
        total = h[0:1] * slot[8 : 8 + rows]
        for j in range(1, KS):
            total = total + h[j : j + 1] * slot[8 - j : 8 - j + rows]
        made.append(total.astype(BF16).astype(F32))
    kf, vf, qf = made
    lower[...] = (kf * vf)[rows - KB :].astype(BF16)
    gate = g[...].astype(F32)
    upper[...] = jnp.concatenate([gate * qf, gate[:8], kf[:8], vf[:8]], 0).astype(BF16)


def products(q, k, v, g, extra, taps, split, interpret=False):
    rows, channels = q.shape
    first = split // LANES
    block = pl.BlockSpec((rows, LANES), lambda i: (0, first + i))
    out = lambda r: pl.BlockSpec((r, LANES), lambda i: (0, i))
    chunk = pl.BlockSpec((2, 1, 8, LANES), lambda i: ((first + i) % 2, (first + i) // 2, 0, 0))
    return pl.pallas_call(
        products_kernel,
        grid=((channels - split) // LANES,),
        in_specs=[block] * 4 + [pl.BlockSpec((48, LANES), lambda i: (0, i)), chunk],
        out_specs=[out(KB), out(rows + 24)],
        out_shape=[
            jax.ShapeDtypeStruct((KB, channels - split), BF16),
            jax.ShapeDtypeStruct((rows + 24, channels - split), BF16),
        ],
        scratch_shapes=[pltpu.VMEM((rows + 8, LANES), F32)] * 3,
        compiler_params=params(),
        cost_estimate=pl.CostEstimate(flops=20_000_000, bytes_accessed=3_000_000, transcendentals=0),
        interpret=interpret,
        name="products",
    )(q, k, v, g, extra, taps)


def pick_groups(stacked, rows, start, count):
    groups = lane_group((count, LANES))
    out = stacked[start : start + count]
    for g in range(1, GPB):
        out = jnp.where(groups == g, stacked[g * rows + start : g * rows + start + count], out)
    return out


def align_left(tile):
    width = tile.shape[1]
    row = lax.broadcasted_iota(jnp.int32, tile.shape, 0)
    for bit in (1, 2, 4):
        tile = jnp.where(row // bit % 2 == 1, pltpu.roll(tile, width - bit, 1), tile)
    return tile


def step_ctx(value, step):
    count = lax.axis_size(CTX)
    return lax.ppermute(value, CTX, [(i, i + step) for i in range(count) if 0 <= i + step < count])


def turn(value, back=False):
    nx, nz, ny, nm = SIZES
    at = lambda x, z, y, m: ((x * nz + z) * ny + y) * nm + m
    pairs = [
        (at(x, z, y, m), at(y, z, m, x))
        for x in range(nx) for z in range(nz) for y in range(ny) for m in range(nm)
    ]
    if back:
        pairs = [(b, a) for a, b in pairs]
    return lax.ppermute(value, ALL, pairs)


def pack_taps(filt_short, filt_medium):
    short = jnp.pad(filt_short.T, ((0, 0), (0, LANES - KS)))
    return jnp.concatenate([filt_medium.T, short], 0)


def shards(q, k, v, g, filt_short, filt_medium):
    rows, channels = q.shape
    split = channels // 2
    lower, upper, tails = pack(q, k, v, g, split)
    own, tails, lower, upper = lax.optimization_barrier(
        (turn(pack_taps(filt_short, filt_medium)), step_ctx(tails, 1), lower, upper)
    )
    below, above = step_ctx(lower, 1), step_ctx(upper, -1)
    taps = lax.all_to_all(
        jnp.broadcast_to(own[None], (32, 8, LANES)), ("x", "z"), 0, 0, tiled=True
    ).reshape(4, 8, 8, LANES)
    u_send, d_send = products(q, k, v, g, tails, taps, split)
    u_halo, d_halo = step_ctx(u_send, 1), step_ctx(d_send, -1)
    blocks = split // LANES
    made = fused(True, q, k, v, g, below, above, tails, taps, 0, blocks)
    made = fused(False, q, k, v, g, u_halo, d_halo, tails, taps, blocks, blocks, made)
    grad_q, grad_k, grad_v, part = made
    pieces = lax.all_to_all(part.reshape(32, 8, LANES), ("x", "z"), 0, 0, tiled=True)
    total = lax.psum(turn(jnp.sum(pieces, 0), back=True), MP)
    grad_short, grad_medium = finish(total)
    return grad_q, grad_k, grad_v, grad_short[:, :KS].T, grad_medium.T


def finish_kernel(total, short, medium):
    at = lax.broadcasted_iota(jnp.int32, (LANES, LANES), 0)
    to = lax.broadcasted_iota(jnp.int32, (LANES, LANES), 1)
    medium[...] = jnp.dot(
        total[0:4], ((at + to) % LANES == 0).astype(F32), precision=lax.Precision.HIGHEST,
        preferred_element_type=F32,
    )
    group = lax.broadcasted_iota(jnp.int32, (4, LANES), 0)
    for half in range(2):
        spread = (lane_group((4, LANES)) == group + 4 * half).astype(F32)
        short[:, 4 * half : 4 * half + 4] = lax.dot_general(
            spread, total[4:8], (((1,), (1,)), ((), ())), precision=lax.Precision.HIGHEST,
            preferred_element_type=F32,
        )


def finish(total, interpret=False):
    return pl.pallas_call(
        finish_kernel,
        out_shape=[jax.ShapeDtypeStruct((4, 8), F32), jax.ShapeDtypeStruct((4, LANES), F32)],
        interpret=interpret,
        name="finish",
    )(total)


def solution(mesh):
    fine = Mesh(mesh.devices.reshape(4, 8, 4, 2, 2), ALL)
    signal = P(CTX, MP)
    taps = P(None, CTX)
    return jax.shard_map(
        shards,
        mesh=fine,
        in_specs=(signal,) * 4 + (taps,) * 2,
        out_specs=(signal,) * 3 + (taps,) * 2,
        check_vma=False,
    )
```

time: 157 us -> 133 us (0.85); the launches traced: 157 us -> 131 us
  blocking collectives: 94.9 us -> 62.5 us
  starting transfers between devices: 13.8 us -> 29.7 us
  Pallas kernels: 38 us -> 30.2 us
  other arithmetic: 2.46 us -> 0.05 us
    all_to_all x2, blocking collectives: 83 us -> 50.7 us  [the longest x1 36.7 us: shards(): lax.all_to_all(jnp.broadcast_to(own[None], (32, 8, LANES)), ('x', 'z'), 0...]
    ppermute x2 -> x5, starting transfers between devices: 5.58 us -> 17.3 us  [step_ctx(): lax.ppermute(value, CTX, [(i, i + step) for i in range(count) if 0 <= i +...]
    pallas_call x1 -> x5, Pallas kernels: 38 us -> 30.2 us  [the longest x2 25 us: fused(): pl.pallas_call(functools.partial(fused_kernel, raw), grid=(count,), in_sp...]
    ppermute x2, starting transfers between devices: 8.18 us -> 12.4 us  [turn(): return lax.ppermute(value, ALL, pairs)]
    unnamed x4 -> x12, local copies, waits for them, and re-layouts: 2.07 us -> 4.87 us
    slice x3 -> x0, local copies, waits for them, and re-layouts: 2.37 us -> none  [the longest x1 0.84 us: shards(): q[rows - 16:]]
    concatenate x1 -> x0, other arithmetic: 1.71 us -> none  [shards(): jnp.concatenate([k, v, q[rows - 16:]], 0)]
  transfers between devices with their start and end apart: 4 -> 7, of which waited for: 1 -> 2; matrix products, arithmetic and copies ran while one was open for 3% -> 0% of each run, Pallas kernels for 0% -> 12%
where the time goes in v3:
time: 133 us; the launch traced here: 131 us
  blocking collectives  62.5 us (47%)
  Pallas kernels  30.2 us (23%)
  starting transfers between devices  29.7 us (22%)
  local copies, waits for them, and re-layouts  6.11 us (5%)
  waiting for transfers between devices  1.46 us (1%)
    all_to_all x1, blocking collectives, shards(): lax.all_to_all(jnp.broadcast_to(own[None], (32, 8, LANES)), ('x', 'z'), 0...  36.7 us
    pallas_call x2, Pallas kernels, fused(): pl.pallas_call(functools.partial(fused_kernel, raw), grid=(count,), in_sp...  25 us
    ppermute x5, starting transfers between devices, step_ctx(): lax.ppermute(value, CTX, [(i, i + step) for i in range(count) if 0 <= i +...  17.3 us
    all_to_all x1, blocking collectives, shards(): lax.all_to_all(part.reshape(32, 8, LANES), ('x', 'z'), 0, 0, tiled=True)  14.1 us
    ppermute x2, starting transfers between devices, turn(): return lax.ppermute(value, ALL, pairs)  12.4 us
    psum x1, blocking collectives, shards(): total = lax.psum(turn(jnp.sum(pieces, 0), back=True), MP)  11.7 us
    unnamed x12, local copies, waits for them, and re-layouts  4.87 us
    pallas_call x1, Pallas kernels, products(): pl.pallas_call(products_kernel, grid=((channels - split) // LANES,), in_s...  3.08 us
  transfers between devices with their start and end apart: 7, of which 2 were waited for; matrix products, arithmetic and copies ran while one was open for 0% of the time, Pallas kernels for 12%

profile of v3, /device:TPU:1, one launch (start us, length us, event | category | flops | bytes accessed | tf_op | source)
XLA Modules:
  0.0 130.7 jit_solution(16710988588241395281)
XLA Ops:
  0.6 1.0 copy-done
  1.7 1.1 copy-done.1
  2.7 1.1 copy-done.2
  3.8 1.1 copy-done.3
  4.8 0.6 pack.1
  5.5 5.0 %collective-permute-start.1 = (bf16[48,1024]{1,0:T(8,128)(2,1)S(1)}, bf16[48,1024]{1,0:T(8,128)(2,1)S(1)}, u32[]{:S(2)}, u32[]{:S(2)}) collective-permute-start(bf16[48,1024]{1,0:T(8,128)(2,1)S(1)} %get-tuple-element.24), channel_id=1, source_target_pairs={{0,4},{4,8},{8,12},{12,16},{16,20},{20,24},{24,28},{28,32},{32,36}... | collective-permute-start | bytes 294920 | tf_op jit(solution)/shard_map/ppermute | solution.py:291
  10.5 0.0 copy-start.4
  10.6 0.7 copy-done.4
  11.2 6.3 %collective-permute-start = (bf16[8,128]{1,0:T(8,128)(2,1)S(1)}, bf16[8,128]{1,0:T(8,128)(2,1)S(1)}, u32[]{:S(2)}, u32[]{:S(2)}) collective-permute-start(bf16[8,128]{1,0:T(8,128)(2,1)S(1)} %fusion.1), channel_id=1, source_target_pairs={{0,0},{1,4},{2,8},{3,12},{4,128},{5,132},{6,136},{7,140},{8,256},{... | collective-permute-start | bytes 6152 | tf_op jit(solution)/shard_map/ppermute | solution.py:303
  17.5 0.7 collective-permute-done
  18.2 4.8 %collective-permute-start.4 = (bf16[288,1024]{1,0:T(8,128)(2,1)S(1)}, bf16[288,1024]{1,0:T(8,128)(2,1)S(1)}, u32[]{:S(2)}, u32[]{:S(2)}) collective-permute-start(bf16[288,1024]{1,0:T(8,128)(2,1)S(1)} %get-tuple-element.31), channel_id=1, source_target_pairs={{0,4},{4,8},{8,12},{12,16},{16,20},{20,24},{24,28},{28,32},{32,36}... | collective-permute-start | bytes 1769480 | tf_op jit(solution)/shard_map/ppermute | solution.py:291
  23.0 1.3 collective-permute-start.5
  24.3 36.7 %all_to_all.10 = bf16[32,8,128]{2,1,0:T(8,128)(2,1)S(1)} all-to-all(bf16[32,8,128]{2,1,0:T(8,128)(2,1)S(1)} %broadcast_in_dim.2), channel_id=1, replica_groups=mesh['x'=4,'z'=8,'yh'=4,'yl'=2,'core'=2] {'x','z'}, dimensions={0} | all-to-all | bytes 131072 | tf_op jit(solution)/shard_map/all_to_all | solution.py:319
  61.0 3.1 %products.1 = (bf16[128,1024]{1,0:T(8,128)(2,1)S(1)}, bf16[160,1024]{1,0:T(8,128)(2,1)S(1)}) custom-call(bf16[136,2048]{1,0:T(8,128)(2,1)S(1)} %copy-done, bf16[136,2048]{1,0:T(8,128)(2,1)S(1)} %copy-done.1, bf16[136,2048]{1,0:T(8,128)(2,1)S(1)} %copy-done.2, bf16[136,2048]{1,0:T(8,128)(2,1)S(1)} %copy-done.3, ...), custom_call_target="tpu_custom_call" | custom-call | flops 20000000 | bytes 3000000 | tf_op jit(solution)/shard_map/products/pallas_call | solution.py:256
  64.1 1.3 collective-permute-start.3
  65.4 4.9 %collective-permute-start.2 = (bf16[128,1024]{1,0:T(8,128)(2,1)S(1)}, bf16[128,1024]{1,0:T(8,128)(2,1)S(1)}, u32[]{:S(2)}, u32[]{:S(2)}) collective-permute-start(bf16[128,1024]{1,0:T(8,128)(2,1)S(1)} %get-tuple-element.29), channel_id=1, source_target_pairs={{0,4},{4,8},{8,12},{12,16},{16,20},{20,24},{24,28},{28,32},{32,36}... | collective-permute-start | bytes 786440 | tf_op jit(solution)/shard_map/ppermute | solution.py:291
  70.3 12.9 %fused_raw.1 = (bf16[136,2048]{1,0:T(8,128)(2,1)}, bf16[136,2048]{1,0:T(8,128)(2,1)}, bf16[136,2048]{1,0:T(8,128)(2,1)}, f32[4,8,8,128]{3,2,1,0:T(8,128)S(1)}) custom-call(bf16[136,2048]{1,0:T(8,128)(2,1)S(1)} %copy-done, bf16[136,2048]{1,0:T(8,128)(2,1)S(1)} %copy-done.1, bf16[136,2048]{1,0:T(8,128)(2,1)S(1)} %copy-done.2, bf16[136,2048]{1,0:T(8,128)(2,1)S(1)} %copy-done.3, ...), custom_call_target="tpu_custom_call" | custom-call | flops 2000000000 | bytes 4000000 | tf_op jit(solution)/shard_map/fused_raw/pallas_call | solution.py:172
  83.3 12.1 %fused_sent.1 = (bf16[136,2048]{1,0:T(8,128)(2,1)}, bf16[136,2048]{1,0:T(8,128)(2,1)}, bf16[136,2048]{1,0:T(8,128)(2,1)}, f32[4,8,8,128]{3,2,1,0:T(8,128)S(1)}) custom-call(bf16[136,2048]{1,0:T(8,128)(2,1)S(1)} %copy-done, bf16[136,2048]{1,0:T(8,128)(2,1)S(1)} %copy-done.1, ...), custom_call_target="tpu_custom_call", output_to_operand_aliasing={{0}: (8, {}), {1}: (9, {}), {2}: (10, {}), {3}: (11, {})} | custom-call | flops 2000000000 | bytes 4000000 | tf_op jit(solution)/shard_map/fused_sent/pallas_call | solution.py:172
  95.3 14.1 %all_to_all.11 = f32[32,8,128]{2,1,0:T(8,128)S(1)} all-to-all(f32[32,8,128]{2,1,0:T(8,128)S(1)} %bitcast.10), channel_id=1, replica_groups=mesh['x'=4,'z'=8,'yh'=4,'yl'=2,'core'=2] {'x','z'}, dimensions={0} | all-to-all | bytes 262144 | tf_op jit(solution)/shard_map/all_to_all | solution.py:328
  109.4 6.1 %collective-permute-start.6 = (f32[8,128]{1,0:T(8,128)S(1)}, f32[8,128]{1,0:T(8,128)S(1)}, u32[]{:S(2)}, u32[]{:S(2)}) collective-permute-start(f32[8,128]{1,0:T(8,128)S(1)} %reduce_sum.9), channel_id=1, source_target_pairs={{0,0},{4,1},{8,2},{12,3},{128,4},{132,5},{136,6},{140,7},{256,8},{... | collective-permute-start | bytes 12296 | tf_op jit(solution)/shard_map/ppermute | solution.py:303
  115.5 0.7 collective-permute-done.6
  116.3 11.7 %psum.7.total = f32[8,128]{1,0:T(8,128)} all-reduce(f32[8,128]{1,0:T(8,128)S(1)} %collective-permute-done.6), channel_id=1, replica_groups=mesh['x'=4,'z'=8,'yh'=4,'yl'=2,'core'=2] {'yl','core'}, use_global_device_ids=true, to_apply=%region_1.2 | all-reduce | flops 1024 | bytes 8192 | tf_op jit(solution)/shard_map/psum | solution.py:329
  128.0 1.5 %finish.1 = (f32[4,8]{1,0:T(4,128)}, f32[4,128]{1,0:T(4,128)}) custom-call(f32[8,128]{1,0:T(8,128)} %psum.7.total), custom_call_target="tpu_custom_call" | custom-call | tf_op jit(solution)/shard_map/finish/pallas_call | solution.py:351
  129.5 1.2 slice_bitcast_fusion
  (14 shorter events, 0.1 us)
Async XLA Ops:
  0.6 1.1 copy-start
  1.7 1.1 copy-start.1
  2.7 1.1 copy-start.2
  3.8 1.1 copy-start.3
  4.8 5.7 %copy-start.5 = (bf16[128,4]{0,1:T(4,128)(2,1)S(1)}, bf16[128,4]{0,1:T(4,128)(2,1)}, u32[]{:S(2)}) copy-start(bf16[128,4]{0,1:T(4,128)(2,1)} %param.11) | copy-start | bytes 3076
  5.5 12.7 %collective-permute-start.1 = (bf16[48,1024]{1,0:T(8,128)(2,1)S(1)}, bf16[48,1024]{1,0:T(8,128)(2,1)S(1)}, u32[]{:S(2)}, u32[]{:S(2)}) collective-permute-start(bf16[48,1024]{1,0:T(8,128)(2,1)S(1)} %get-tuple-element.24), channel_id=1, source_target_pairs={{0,4},{4,8},{8,12},{12,16},{16,20},{20,24},{24,28},{28,32},{32,36}... | collective-permute-start | bytes 294920 | tf_op jit(solution)/shard_map/ppermute | solution.py:291
  10.5 0.7 copy-start.4
  11.2 7.0 %collective-permute-start = (bf16[8,128]{1,0:T(8,128)(2,1)S(1)}, bf16[8,128]{1,0:T(8,128)(2,1)S(1)}, u32[]{:S(2)}, u32[]{:S(2)}) collective-permute-start(bf16[8,128]{1,0:T(8,128)(2,1)S(1)} %fusion.1), channel_id=1, source_target_pairs={{0,0},{1,4},{2,8},{3,12},{4,128},{5,132},{6,136},{7,140},{8,256},{... | collective-permute-start | bytes 6152 | tf_op jit(solution)/shard_map/ppermute | solution.py:303
  18.2 52.1 %collective-permute-start.4 = (bf16[288,1024]{1,0:T(8,128)(2,1)S(1)}, bf16[288,1024]{1,0:T(8,128)(2,1)S(1)}, u32[]{:S(2)}, u32[]{:S(2)}) collective-permute-start(bf16[288,1024]{1,0:T(8,128)(2,1)S(1)} %get-tuple-element.31), channel_id=1, source_target_pairs={{0,4},{4,8},{8,12},{12,16},{16,20},{20,24},{24,28},{28,32},{32,36}... | collective-permute-start | bytes 1769480 | tf_op jit(solution)/shard_map/ppermute | solution.py:291
  23.0 47.3 %collective-permute-start.5 = (bf16[288,1024]{1,0:T(8,128)(2,1)S(1)}, bf16[288,1024]{1,0:T(8,128)(2,1)S(1)}, u32[]{:S(2)}, u32[]{:S(2)}) collective-permute-start(bf16[288,1024]{1,0:T(8,128)(2,1)S(1)} %get-tuple-element.32), channel_id=1, source_target_pairs={{4,0},{8,4},{12,8},{16,12},{20,16},{24,20},{28,24},{32,28},{36,32}... | collective-permute-start | bytes 1769480 | tf_op jit(solution)/shard_map/ppermute | solution.py:291
  64.1 19.1 %collective-permute-start.3 = (bf16[160,1024]{1,0:T(8,128)(2,1)S(1)}, bf16[160,1024]{1,0:T(8,128)(2,1)S(1)}, u32[]{:S(2)}, u32[]{:S(2)}) collective-permute-start(bf16[160,1024]{1,0:T(8,128)(2,1)S(1)} %get-tuple-element.30), channel_id=1, source_target_pairs={{4,0},{8,4},{12,8},{16,12},{20,16},{24,20},{28,24},{32,28},{36,32}... | collective-permute-start | bytes 983048 | tf_op jit(solution)/shard_map/ppermute | solution.py:291
  65.4 17.8 %collective-permute-start.2 = (bf16[128,1024]{1,0:T(8,128)(2,1)S(1)}, bf16[128,1024]{1,0:T(8,128)(2,1)S(1)}, u32[]{:S(2)}, u32[]{:S(2)}) collective-permute-start(bf16[128,1024]{1,0:T(8,128)(2,1)S(1)} %get-tuple-element.29), channel_id=1, source_target_pairs={{0,4},{4,8},{8,12},{12,16},{16,20},{20,24},{24,28},{28,32},{32,36}... | collective-permute-start | bytes 786440 | tf_op jit(solution)/shard_map/ppermute | solution.py:291
  109.4 6.9 %collective-permute-start.6 = (f32[8,128]{1,0:T(8,128)S(1)}, f32[8,128]{1,0:T(8,128)S(1)}, u32[]{:S(2)}, u32[]{:S(2)}) collective-permute-start(f32[8,128]{1,0:T(8,128)S(1)} %reduce_sum.9), channel_id=1, source_target_pairs={{0,0},{4,1},{8,2},{12,3},{128,4},{132,5},{136,6},{140,7},{256,8},{... | collective-permute-start | bytes 12296 | tf_op jit(solution)/shard_map/ppermute | solution.py:303

commit v4 on v3

v4 whole, which is shorter than its diff:
```python
import functools

import jax
import jax.numpy as jnp
from jax import lax
from jax.experimental import pallas as pl
from jax.experimental.pallas import tpu as pltpu
from jax.sharding import Mesh, PartitionSpec as P

F32 = jnp.float32
BF16 = jnp.bfloat16
CPG = 16
KS = 7
KB = 128
LANES = 128
GPB = LANES // CPG
HALO = 8
CTX = ("x", "z", "yh")
MP = ("yl", "core")
ALL = CTX + MP
SIZES = (4, 8, 4, 4)
VMEM = 12 * 1024 * 1024


def params(**more):
    return pltpu.CompilerParams(vmem_limit_bytes=VMEM, **more)


def lane_group(shape):
    return lax.broadcasted_iota(jnp.int32, shape, len(shape) - 1) // CPG


def short_taps(taps):
    row = lax.broadcasted_iota(jnp.int32, (16, LANES), 0)
    group = jnp.where(row % 8 >= 4, row // 8 * 4 + row % 4, -1)
    spread = (lane_group((16, LANES)) == group).astype(BF16)
    return lax.dot_general(taps, spread, (((0,), (0,)), ((), ())), preferred_element_type=F32)[:8]


def fused_kernel(q, k, v, g, u_before, d_after, tails, heads, taps, *refs):
    gq, gk, gv, part, qs, ks, vs, feats = refs[-8:]
    rows = q.shape[0]
    near = rows + 8
    both = taps[...].reshape(16, LANES)
    h = short_taps(both)
    early, late = tails[...].astype(F32), heads[...].astype(F32)
    made = []
    for i, (slot, x) in enumerate(((ks, k), (vs, v), (qs, q))):
        slot[0:8] = early[16 * i : 16 * i + 8]
        slot[8 : near] = x[...].astype(F32)
        count = rows
        if i < 2:
            slot[near : near + 8] = late[16 * i : 16 * i + 8]
            count = near
        made.append(causal(h, slot, count))
    kf, vf, qf = made
    gate = jnp.concatenate([g[...].astype(F32), late[32:40]], 0)
    uw = jnp.concatenate([u_before[...].astype(F32), kf * vf], 0)
    dw = jnp.concatenate([gate[:rows] * qf, d_after[...].astype(F32)], 0)
    u_low, u_high = uw[: 2 * KB].astype(BF16), uw[16:].astype(BF16)
    d_low, d_high = dw[: 2 * KB].astype(BF16), dw[16:].astype(BF16)
    own = jnp.concatenate([dw[:rows], jnp.zeros((8, LANES), F32)], 0).astype(BF16)

    at = lax.broadcasted_iota(jnp.int32, (LANES, LANES), 0)
    to = lax.broadcasted_iota(jnp.int32, (LANES, LANES), 1)
    flip = (at + to == LANES - 1).astype(BF16)
    straight = both.astype(F32)
    turned = jnp.dot(both, flip, preferred_element_type=F32)
    lane = lax.broadcasted_iota(jnp.int32, (16, LANES), 1)
    row = lax.broadcasted_iota(jnp.int32, (16, LANES), 0)
    lane8, row8 = lane[:8], row[:8]
    contract = (((1,), (1,)), ((), ()))
    wide = lane_group((2 * KB, LANES))

    def square(line, first):
        base = pltpu.roll(jnp.broadcast_to(line, (16, LANES)), first, 1, stride=1, stride_axis=0)
        tiles = []
        for a in range(KB // 16):
            tile = pltpu.roll(base, 16 * a, 1) if a else base
            upper = lane > row + 16 * a if first else lane >= row + 16 * a
            parts = [jnp.where(upper, tile, 0.0), jnp.where(upper, 0.0, tile)]
            tiles.append(jnp.concatenate(parts, 1).astype(BF16))
        return tiles

    z_low = du_high = jnp.zeros((KB, LANES), F32)
    tails, heads, medium = [], [], []
    rest = jnp.concatenate([jnp.where(wide[:16] == i, own[KB:], 0) for i in range(GPB)], 0)
    last = lax.dot_general(rest, u_high, contract, preferred_element_type=F32)
    for i in range(GPB):
        line = i // 4 * 8 + i % 4
        tc = square(turned[line : line + 1], 1)
        ta = square(straight[line : line + 1], 0)
        tails.append(tc[-1])
        heads.append(ta[0])
        z_low = z_low + jnp.dot(
            jnp.concatenate(tc, 0), jnp.where(wide == i, u_low, 0), preferred_element_type=F32
        )
        du_high = du_high + jnp.dot(
            jnp.concatenate(ta, 0), jnp.where(wide == i, d_high, 0), preferred_element_type=F32
        )
        mine = jnp.where(wide[:KB] == i, own[:KB], 0)
        prod = lax.dot_general(mine, u_low, contract, preferred_element_type=F32)
        total = None
        for a in range(KB // 8):
            tile = prod[8 * a : 8 * a + 8]
            if a == KB // 8 - 2:
                tile = tile + last[16 * i : 16 * i + 8]
            tile = jnp.where(lane8 > row8 + 8 * a, tile[:, :KB], tile[:, KB:])
            total = tile if a == 0 else total + pltpu.roll(tile, KB - 8 * a, 1)
        medium.append(jnp.sum(align_left(total), 0, keepdims=True))
    for half in range(2):
        part[half, 0, 0:4] = jnp.concatenate(medium[4 * half : 4 * half + 4], 0)

    z_high = pick_groups(
        jnp.dot(jnp.concatenate(tails, 0), u_high, preferred_element_type=F32), 16, 0, 16
    )
    du_low = pick_groups(
        jnp.dot(jnp.concatenate(heads, 0), d_low, preferred_element_type=F32), 16, 0, 16
    )
    z = jnp.concatenate([z_low, z_high], 0)
    du = jnp.concatenate([du_low, du_high], 0)
    feats[0] = (gate[:near] * z).astype(BF16).astype(F32)
    feats[1] = (du * vf).astype(BF16).astype(F32)
    feats[2] = (du * kf).astype(BF16).astype(F32)

    sums = [jnp.zeros((8, LANES), F32)] * 8
    for i, (slot, base, out) in enumerate(((qs, 8, gq), (ks, 8, gk), (vs, 8, gv))):
        wide_feat = feats[i, 0:rows]
        for j in range(KS):
            both_rows = wide_feat * slot[base - j : base - j + rows]
            sums[j] = sums[j] + jnp.sum(both_rows.reshape(rows // 8, 8, LANES), 0)
        total = h[0:1] * wide_feat
        for j in range(1, KS):
            total = total + h[j : j + 1] * feats[i, j : j + rows]
        out[...] = total.astype(BF16)
    short = jnp.concatenate([jnp.sum(x, 0, keepdims=True) for x in sums], 0)
    swapped = pltpu.roll(short, LANES // 2, 1)
    left = lane[:4] < LANES // 2
    part[0, 0, 4:8] = jnp.where(left, short[:4], swapped[4:])
    part[1, 0, 4:8] = jnp.where(left, swapped[:4], short[4:])


def fused(q, k, v, g, u_before, d_after, tails, heads, taps, first, count, written=(), interpret=False):
    rows, channels = q.shape
    block = lambda r: pl.BlockSpec((r, LANES), lambda i: (0, first + i))
    sent = lambda r: pl.BlockSpec((r, LANES), lambda i: (0, i))
    chunk = pl.BlockSpec((2, 1, 8, LANES), lambda i: ((first + i) % 2, (first + i) // 2, 0, 0))
    return pl.pallas_call(
        fused_kernel,
        grid=(count,),
        in_specs=[block(rows)] * 4 + [sent(KB), sent(rows), block(48), block(48), chunk]
        + [pl.BlockSpec(memory_space=pl.ANY)] * len(written),
        out_specs=[block(rows)] * 3 + [chunk],
        out_shape=[jax.ShapeDtypeStruct((rows, channels), BF16)] * 3
        + [jax.ShapeDtypeStruct((4, channels // LANES // 2, 8, LANES), F32)],
        scratch_shapes=[pltpu.VMEM((rows + 16, LANES), F32)] * 3
        + [pltpu.VMEM((3, rows + 8, LANES), F32)],
        input_output_aliases={9 + n: n for n in range(len(written))},
        compiler_params=params(),
        cost_estimate=pl.CostEstimate(
            flops=250_000_000 * count, bytes_accessed=500_000 * count, transcendentals=0
        ),
        interpret=interpret,
        name="fused",
    )(q, k, v, g, u_before, d_after, tails, heads, taps, *written)


def causal(h, slot, count):
    total = h[0:1] * slot[8 : 8 + count]
    for j in range(1, KS):
        total = total + h[j : j + 1] * slot[8 - j : 8 - j + count]
    return total.astype(BF16).astype(F32)


def ends_kernel(qt, kt, vt, kh, vh, gh, tails, heads):
    for out, parts in ((tails, (kt, vt, qt)), (heads, (kh, vh, gh))):
        for i, x in enumerate(parts):
            out[16 * i : 16 * i + 16] = x[...]


def ends(q, k, v, g, interpret=False):
    rows, channels = q.shape
    wide = channels // 2
    tail = pl.BlockSpec((16, wide), lambda i: (rows // 16, i))
    head = pl.BlockSpec((16, wide), lambda i: (0, i))
    whole = pl.BlockSpec((48, wide), lambda i: (0, i))
    return pl.pallas_call(
        ends_kernel,
        grid=(2,),
        in_specs=[tail] * 3 + [head] * 3,
        out_specs=[whole] * 2,
        out_shape=[jax.ShapeDtypeStruct((48, channels), BF16)] * 2,
        compiler_params=pltpu.CompilerParams(vmem_limit_bytes=56 * 1024 * 1024),
        interpret=interpret,
        name="ends",
    )(q, k, v, k, v, g)


def products_kernel(q, k, v, g, tails, taps, lower, upper, qs, ks, vs):
    rows = q.shape[0]
    h = short_taps(taps[...].reshape(16, LANES))
    early = tails[...].astype(F32)
    made = []
    for i, (slot, x) in enumerate(((ks, k), (vs, v), (qs, q))):
        slot[0:8] = early[16 * i : 16 * i + 8]
        slot[8 : rows + 8] = x[...].astype(F32)
        made.append(causal(h, slot, rows))
    kf, vf, qf = made
    lower[...] = (kf * vf)[rows - KB :].astype(BF16)
    upper[...] = (g[...].astype(F32) * qf).astype(BF16)


def products(q, k, v, g, tails, taps, first, count, interpret=False):
    rows = q.shape[0]
    block = lambda r: pl.BlockSpec((r, LANES), lambda i: (0, first + i))
    chunk = pl.BlockSpec((2, 1, 8, LANES), lambda i: ((first + i) % 2, (first + i) // 2, 0, 0))
    out = lambda r: pl.BlockSpec((r, LANES), lambda i: (0, i))
    return pl.pallas_call(
        products_kernel,
        grid=(count,),
        in_specs=[block(rows)] * 4 + [block(48), chunk],
        out_specs=[out(KB), out(rows)],
        out_shape=[jax.ShapeDtypeStruct((r, count * LANES), BF16) for r in (KB, rows)],
        scratch_shapes=[pltpu.VMEM((rows + 8, LANES), F32)] * 3,
        compiler_params=params(),
        cost_estimate=pl.CostEstimate(flops=20_000_000, bytes_accessed=3_000_000, transcendentals=0),
        interpret=interpret,
        name="products",
    )(q, k, v, g, tails, taps)


def pick_groups(stacked, rows, start, count):
    groups = lane_group((count, LANES))
    out = stacked[start : start + count]
    for g in range(1, GPB):
        out = jnp.where(groups == g, stacked[g * rows + start : g * rows + start + count], out)
    return out


def align_left(tile):
    width = tile.shape[1]
    row = lax.broadcasted_iota(jnp.int32, tile.shape, 0)
    for bit in (1, 2, 4):
        tile = jnp.where(row // bit % 2 == 1, pltpu.roll(tile, width - bit, 1), tile)
    return tile


def step_ctx(value, step):
    count = lax.axis_size(CTX)
    return lax.ppermute(value, CTX, [(i, i + step) for i in range(count) if 0 <= i + step < count])


def turn(value, back=False):
    nx, nz, ny, nm = SIZES
    at = lambda x, z, y, m: ((x * nz + z) * ny + y) * nm + m
    pairs = [
        (at(x, z, y, m), at(y, z, m, x))
        for x in range(nx) for z in range(nz) for y in range(ny) for m in range(nm)
    ]
    if back:
        pairs = [(b, a) for a, b in pairs]
    return lax.ppermute(value, ALL, pairs)


def pack_taps(filt_short, filt_medium):
    short = jnp.pad(filt_short.T, ((0, 0), (0, LANES - KS)))
    return jnp.concatenate([filt_medium.T, short], 0)


def shards(q, k, v, g, filt_short, filt_medium):
    blocks = q.shape[1] // LANES
    packed, *signals = lax.optimization_barrier((pack_taps(filt_short, filt_medium), q, k, v, g))
    own = turn(packed)
    tails, heads = ends(*signals)
    own, tails, heads = lax.optimization_barrier((own, step_ctx(tails, 1), step_ctx(heads, -1)))
    taps = lax.all_to_all(
        jnp.broadcast_to(own[None], (32, 8, LANES)), ("x", "z"), 0, 0, tiled=True
    ).reshape(4, 8, 8, LANES)
    half = blocks // 2
    pieces = [(0, half), (half, blocks - half)]
    sent = []
    for first, count in pieces:
        lower, upper = products(q, k, v, g, tails, taps, first, count)
        sent.append((step_ctx(lower, 1), step_ctx(upper, -1)))
    made = ()
    for (first, count), (u_before, d_after) in zip(pieces, sent):
        made = fused(q, k, v, g, u_before, d_after, tails, heads, taps, first, count, made)
    grad_q, grad_k, grad_v, part = made
    parts = lax.all_to_all(part.reshape(32, 8, LANES), ("x", "z"), 0, 0, tiled=True)
    total = lax.psum(turn(jnp.sum(parts, 0), back=True), MP)
    grad_short, grad_medium = finish(total)
    return grad_q, grad_k, grad_v, grad_short.T, grad_medium.T


def finish_kernel(total, short, medium):
    at = lax.broadcasted_iota(jnp.int32, (LANES, LANES), 0)
    to = lax.broadcasted_iota(jnp.int32, (LANES, LANES), 1)
    medium[...] = jnp.dot(
        total[0:4], ((at + to) % LANES == 0).astype(F32), precision=lax.Precision.HIGHEST,
        preferred_element_type=F32,
    )
    group = lax.broadcasted_iota(jnp.int32, (4, LANES), 0)
    halves = []
    for half in range(2):
        spread = (lane_group((4, LANES)) == group + 4 * half).astype(F32)
        halves.append(
            lax.dot_general(
                spread, total[4:8], (((1,), (1,)), ((), ())), precision=lax.Precision.HIGHEST,
                preferred_element_type=F32,
            )
        )
    short[...] = jnp.concatenate(halves, 1)[:, :KS]


def finish(total, interpret=False):
    return pl.pallas_call(
        finish_kernel,
        out_shape=[jax.ShapeDtypeStruct((4, KS), F32), jax.ShapeDtypeStruct((4, LANES), F32)],
        interpret=interpret,
        name="finish",
    )(total)


def solution(mesh):
    fine = Mesh(mesh.devices.reshape(4, 8, 4, 2, 2), ALL)
    signal = P(CTX, MP)
    taps = P(None, CTX)
    return jax.shard_map(
        shards,
        mesh=fine,
        in_specs=(signal,) * 4 + (taps,) * 2,
        out_specs=(signal,) * 3 + (taps,) * 2,
        check_vma=False,
    )
```

time: 133 us -> 133 us (level)
  blocking collectives: 62.5 us -> 48.9 us
  starting transfers between devices: 29.7 us -> 38.3 us
  waiting for transfers between devices: 1.46 us -> 8.86 us
  local copies, waits for them, and re-layouts: 6.11 us -> 0.71 us
  Pallas kernels: 30.2 us -> 33.6 us
    all_to_all x1, blocking collectives: 36.7 us -> 19.4 us  [shards(): lax.all_to_all(jnp.broadcast_to(own[None], (32, 8, LANES)), ('x', 'z'), 0...]
    all_to_all x1, blocking collectives: 14.1 us -> 22.3 us  [shards(): lax.all_to_all(part.reshape(32, 8, LANES), ('x', 'z'), 0, 0, tiled=True)]
    ppermute x2, waiting for transfers between devices: 1.45 us -> 8.5 us  [turn(): return lax.ppermute(value, ALL, pairs)]
    ppermute x2, starting transfers between devices: 12.4 us -> 18.1 us  [turn(): return lax.ppermute(value, ALL, pairs)]
    psum x1, blocking collectives: 11.7 us -> 7.18 us  [shards(): total = lax.psum(turn(jnp.sum(parts, 0), back=True), MP)]
    unnamed x12, local copies, waits for them, and re-layouts: 4.87 us -> 0.7 us
    pallas_call x5 -> x6, Pallas kernels: 30.2 us -> 33.6 us  [the longest x2 24.1 us: fused(): pl.pallas_call(fused_kernel, grid=(count,), in_specs=[block(rows)] * 4 +...]
    ppermute x5 -> x6, starting transfers between devices: 17.3 us -> 20.2 us  [step_ctx(): lax.ppermute(value, CTX, [(i, i + step) for i in range(count) if 0 <= i +...]
  transfers between devices with their start and end apart: 7 -> 8, of which waited for: 2 -> 3; matrix products, arithmetic and copies ran while one was open for 0% -> 0% of each run, Pallas kernels for 12% -> 12%
where the time goes in v4:
time: 133 us; the launch traced here: 131 us
  blocking collectives  48.9 us (37%)
  starting transfers between devices  38.3 us (29%)
  Pallas kernels  33.6 us (25%)
  waiting for transfers between devices  8.86 us (7%)
    pallas_call x2, Pallas kernels, fused(): pl.pallas_call(fused_kernel, grid=(count,), in_specs=[block(rows)] * 4 +...  24.1 us
    all_to_all x1, blocking collectives, shards(): lax.all_to_all(part.reshape(32, 8, LANES), ('x', 'z'), 0, 0, tiled=True)  22.3 us
    ppermute x6, starting transfers between devices, step_ctx(): lax.ppermute(value, CTX, [(i, i + step) for i in range(count) if 0 <= i +...  20.2 us
    all_to_all x1, blocking collectives, shards(): lax.all_to_all(jnp.broadcast_to(own[None], (32, 8, LANES)), ('x', 'z'), 0...  19.4 us
    ppermute x2, starting transfers between devices, turn(): return lax.ppermute(value, ALL, pairs)  18.1 us
    ppermute x2, waiting for transfers between devices, turn(): return lax.ppermute(value, ALL, pairs)  8.5 us
    psum x1, blocking collectives, shards(): total = lax.psum(turn(jnp.sum(parts, 0), back=True), MP)  7.18 us
    pallas_call x2, Pallas kernels, products(): pl.pallas_call(products_kernel, grid=(count,), in_specs=[block(rows)] * 4...  6.17 us
  transfers between devices with their start and end apart: 8, of which 3 were waited for; matrix products, arithmetic and copies ran while one was open for 0% of the time, Pallas kernels for 12%

profile of v4, /device:TPU:1, one launch (start us, length us, event | category | flops | bytes accessed | tf_op | source)
XLA Modules:
  0.0 131.2 jit_solution(9408430932719128536)
XLA Ops:
  0.7 0.7 copy-done.5
  1.3 0.0 copy-done.4
  1.4 0.0 copy-start.2
  1.4 0.0 copy-start.3
  1.4 1.8 %ends.1 = (bf16[48,2048]{1,0:T(8,128)(2,1)}, bf16[48,2048]{1,0:T(8,128)(2,1)}) custom-call(bf16[136,2048]{1,0:T(8,128)(2,1)} %q.7, bf16[136,2048]{1,0:T(8,128)(2,1)} %k.7, bf16[136,2048]{1,0:T(8,128)(2,1)} %v.7, bf16[136,2048]{1,0:T(8,128)(2,1)} %k.7, bf16[136,2048]{1,0:T(8,128)(2,1)} %v.7, bf16[136,2048]{1,0:T(8,128)(2,1)} %g.7), custom_call_target="tpu_custom_call" | custom-call | tf_op jit(solution)/shard_map/ends/pallas_call | solution.py:187
  3.1 5.0 %collective-permute-start.1 = (bf16[48,2048]{1,0:T(8,128)(2,1)}, bf16[48,2048]{1,0:T(8,128)(2,1)S(1)}, u32[]{:S(2)}, u32[]{:S(2)}) collective-permute-start(bf16[48,2048]{1,0:T(8,128)(2,1)} %get-tuple-element.34), channel_id=1, source_target_pairs={{0,4},{4,8},{8,12},{12,16},{16,20},{20,24},{24,28},{28,32},{32,36}... | collective-permute-start | bytes 589832 | tf_op jit(solution)/shard_map/ppermute | solution.py:250
  8.2 1.3 collective-permute-start.2
  9.5 8.2 %collective-permute-start = (bf16[8,128]{1,0:T(8,128)(2,1)S(1)}, bf16[8,128]{1,0:T(8,128)(2,1)S(1)}, u32[]{:S(2)}, u32[]{:S(2)}) collective-permute-start(bf16[8,128]{1,0:T(8,128)(2,1)S(1)} %fusion.1), channel_id=1, source_target_pairs={{0,0},{1,4},{2,8},{3,12},{4,128},{5,132},{6,136},{7,140},{8,256},{... | collective-permute-start | bytes 6152 | tf_op jit(solution)/shard_map/ppermute | solution.py:262
  17.7 7.8 %collective-permute-done = bf16[8,128]{1,0:T(8,128)(2,1)S(1)} collective-permute-done((bf16[8,128]{1,0:T(8,128)(2,1)S(1)}, bf16[8,128]{1,0:T(8,128)(2,1)S(1)}, u32[]{:S(2)}, u32[]{:S(2)}) %collective-permute-start) | collective-permute-done | bytes 2080 | tf_op jit(solution)/shard_map/ppermute | solution.py:262
  25.5 19.4 %all_to_all.10 = bf16[32,8,128]{2,1,0:T(8,128)(2,1)S(1)} all-to-all(bf16[32,8,128]{2,1,0:T(8,128)(2,1)S(1)} %broadcast_in_dim.2), channel_id=1, replica_groups=mesh['x'=4,'z'=8,'yh'=4,'yl'=2,'core'=2] {'x','z'}, dimensions={0} | all-to-all | bytes 131072 | tf_op jit(solution)/shard_map/all_to_all | solution.py:276
  44.9 3.1 %products.3 = (bf16[128,1024]{1,0:T(8,128)(2,1)S(1)}, bf16[136,1024]{1,0:T(8,128)(2,1)S(1)}) custom-call(bf16[136,2048]{1,0:T(8,128)(2,1)S(1)} %copy-done.2, bf16[136,2048]{1,0:T(8,128)(2,1)S(1)} %copy-done, bf16[136,2048]{1,0:T(8,128)(2,1)S(1)} %copy-done.1, bf16[136,2048]{1,0:T(8,128)(2,1)S(1)} %copy-done.3, ...), custom_call_target="tpu_custom_call" | custom-call | flops 20000000 | bytes 3000000 | tf_op jit(solution)/shard_map/products/pallas_call | solution.py:218
  48.0 1.3 collective-permute-start.6
  49.3 5.2 %collective-permute-start.5 = (bf16[128,1024]{1,0:T(8,128)(2,1)S(1)}, bf16[128,1024]{1,0:T(8,128)(2,1)S(1)}, u32[]{:S(2)}, u32[]{:S(2)}) collective-permute-start(bf16[128,1024]{1,0:T(8,128)(2,1)S(1)} %get-tuple-element.41), channel_id=1, source_target_pairs={{0,4},{4,8},{8,12},{12,16},{16,20},{20,24},{24,28},{28,32},{32,36}... | collective-permute-start | bytes 786440 | tf_op jit(solution)/shard_map/ppermute | solution.py:250
  54.5 3.1 %products.2 = (bf16[128,1024]{1,0:T(8,128)(2,1)S(1)}, bf16[136,1024]{1,0:T(8,128)(2,1)S(1)}) custom-call(bf16[136,2048]{1,0:T(8,128)(2,1)S(1)} %copy-done.2, bf16[136,2048]{1,0:T(8,128)(2,1)S(1)} %copy-done, bf16[136,2048]{1,0:T(8,128)(2,1)S(1)} %copy-done.1, bf16[136,2048]{1,0:T(8,128)(2,1)S(1)} %copy-done.3, ...), custom_call_target="tpu_custom_call" | custom-call | flops 20000000 | bytes 3000000 | tf_op jit(solution)/shard_map/products/pallas_call | solution.py:218
  57.6 1.3 collective-permute-start.4
  58.9 6.1 %collective-permute-start.3 = (bf16[128,1024]{1,0:T(8,128)(2,1)S(1)}, bf16[128,1024]{1,0:T(8,128)(2,1)S(1)}, u32[]{:S(2)}, u32[]{:S(2)}) collective-permute-start(bf16[128,1024]{1,0:T(8,128)(2,1)S(1)} %get-tuple-element.38), channel_id=1, source_target_pairs={{0,4},{4,8},{8,12},{12,16},{16,20},{20,24},{24,28},{28,32},{32,36}... | collective-permute-start | bytes 786440 | tf_op jit(solution)/shard_map/ppermute | solution.py:250
  65.0 12.0 %fused.2 = (bf16[136,2048]{1,0:T(8,128)(2,1)}, bf16[136,2048]{1,0:T(8,128)(2,1)}, bf16[136,2048]{1,0:T(8,128)(2,1)}, f32[4,8,8,128]{3,2,1,0:T(8,128)S(1)}) custom-call(bf16[136,2048]{1,0:T(8,128)(2,1)S(1)} %copy-done.2, bf16[136,2048]{1,0:T(8,128)(2,1)S(1)} %copy-done, bf16[136,2048]{1,0:T(8,128)(2,1)S(1)} %copy-done.1, bf16[136,2048]{1,0:T(8,128)(2,1)S(1)} %copy-done.3, ...), custom_call_target="tpu_custom_call" | custom-call | flops 2000000000 | bytes 4000000 | tf_op jit(solution)/shard_map/fused/pallas_call | solution.py:148
  77.0 0.3 collective-permute-done.4.d_after
  77.4 12.1 %fused.3 = (bf16[136,2048]{1,0:T(8,128)(2,1)}, bf16[136,2048]{1,0:T(8,128)(2,1)}, bf16[136,2048]{1,0:T(8,128)(2,1)}, f32[4,8,8,128]{3,2,1,0:T(8,128)S(1)}) custom-call(bf16[136,2048]{1,0:T(8,128)(2,1)S(1)} %copy-done.2, bf16[136,2048]{1,0:T(8,128)(2,1)S(1)} %copy-done, ...), custom_call_target="tpu_custom_call", output_to_operand_aliasing={{0}: (9, {}), {1}: (10, {}), {2}: (11, {}), {3}: (12, {})} | custom-call | flops 2000000000 | bytes 4000000 | tf_op jit(solution)/shard_map/fused/pallas_call | solution.py:148
  89.5 22.3 %all_to_all.11 = f32[32,8,128]{2,1,0:T(8,128)S(1)} all-to-all(f32[32,8,128]{2,1,0:T(8,128)S(1)} %bitcast.10), channel_id=1, replica_groups=mesh['x'=4,'z'=8,'yh'=4,'yl'=2,'core'=2] {'x','z'}, dimensions={0} | all-to-all | bytes 262144 | tf_op jit(solution)/shard_map/all_to_all | solution.py:289
  111.9 9.9 %collective-permute-start.7 = (f32[8,128]{1,0:T(8,128)S(1)}, f32[8,128]{1,0:T(8,128)S(1)}, u32[]{:S(2)}, u32[]{:S(2)}) collective-permute-start(f32[8,128]{1,0:T(8,128)S(1)} %reduce_sum.9), channel_id=1, source_target_pairs={{0,0},{4,1},{8,2},{12,3},{128,4},{132,5},{136,6},{140,7},{256,8},{... | collective-permute-start | bytes 12296 | tf_op jit(solution)/shard_map/ppermute | solution.py:262
  121.8 0.7 collective-permute-done.7
  122.5 7.2 %psum.7.total = f32[8,128]{1,0:T(8,128)} all-reduce(f32[8,128]{1,0:T(8,128)S(1)} %collective-permute-done.7), channel_id=1, replica_groups=mesh['x'=4,'z'=8,'yh'=4,'yl'=2,'core'=2] {'yl','core'}, use_global_device_ids=true, to_apply=%region_1.2 | all-reduce | flops 1024 | bytes 8192 | tf_op jit(solution)/shard_map/psum | solution.py:290
  129.7 1.5 %finish.1 = (f32[4,7]{1,0:T(4,128)}, f32[4,128]{1,0:T(4,128)}) custom-call(f32[8,128]{1,0:T(8,128)} %psum.7.total), custom_call_target="tpu_custom_call" | custom-call | tf_op jit(solution)/shard_map/finish/pallas_call | solution.py:316
  (16 shorter events, 0.1 us)
Async XLA Ops:
  0.6 0.7 copy-start.5
  0.6 0.7 copy-start.4
  1.3 43.5 %copy-start = (bf16[136,2048]{1,0:T(8,128)(2,1)S(1)}, bf16[136,2048]{1,0:T(8,128)(2,1)}, u32[]{:S(2)}) copy-start(bf16[136,2048]{1,0:T(8,128)(2,1)} %k.7) | copy-start | bytes 1671172
  1.4 43.5 %copy-start.1 = (bf16[136,2048]{1,0:T(8,128)(2,1)S(1)}, bf16[136,2048]{1,0:T(8,128)(2,1)}, u32[]{:S(2)}) copy-start(bf16[136,2048]{1,0:T(8,128)(2,1)} %v.7) | copy-start | bytes 1671172
  1.4 43.5 %copy-start.2 = (bf16[136,2048]{1,0:T(8,128)(2,1)S(1)}, bf16[136,2048]{1,0:T(8,128)(2,1)}, u32[]{:S(2)}) copy-start(bf16[136,2048]{1,0:T(8,128)(2,1)} %q.7) | copy-start | bytes 1671172
  1.4 43.5 %copy-start.3 = (bf16[136,2048]{1,0:T(8,128)(2,1)S(1)}, bf16[136,2048]{1,0:T(8,128)(2,1)}, u32[]{:S(2)}) copy-start(bf16[136,2048]{1,0:T(8,128)(2,1)} %g.7) | copy-start | bytes 1671172
  3.1 22.3 %collective-permute-start.1 = (bf16[48,2048]{1,0:T(8,128)(2,1)}, bf16[48,2048]{1,0:T(8,128)(2,1)S(1)}, u32[]{:S(2)}, u32[]{:S(2)}) collective-permute-start(bf16[48,2048]{1,0:T(8,128)(2,1)} %get-tuple-element.34), channel_id=1, source_target_pairs={{0,4},{4,8},{8,12},{12,16},{16,20},{20,24},{24,28},{28,32},{32,36}... | collective-permute-start | bytes 589832 | tf_op jit(solution)/shard_map/ppermute | solution.py:250
  8.2 17.3 %collective-permute-start.2 = (bf16[48,2048]{1,0:T(8,128)(2,1)}, bf16[48,2048]{1,0:T(8,128)(2,1)S(1)}, u32[]{:S(2)}, u32[]{:S(2)}) collective-permute-start(bf16[48,2048]{1,0:T(8,128)(2,1)} %get-tuple-element.35), channel_id=1, source_target_pairs={{4,0},{8,4},{12,8},{16,12},{20,16},{24,20},{28,24},{32,28},{36,32}... | collective-permute-start | bytes 589832 | tf_op jit(solution)/shard_map/ppermute | solution.py:250
  9.5 16.0 %collective-permute-start = (bf16[8,128]{1,0:T(8,128)(2,1)S(1)}, bf16[8,128]{1,0:T(8,128)(2,1)S(1)}, u32[]{:S(2)}, u32[]{:S(2)}) collective-permute-start(bf16[8,128]{1,0:T(8,128)(2,1)S(1)} %fusion.1), channel_id=1, source_target_pairs={{0,0},{1,4},{2,8},{3,12},{4,128},{5,132},{6,136},{7,140},{8,256},{... | collective-permute-start | bytes 6152 | tf_op jit(solution)/shard_map/ppermute | solution.py:262
  48.0 17.1 %collective-permute-start.6 = (bf16[136,1024]{1,0:T(8,128)(2,1)S(1)}, bf16[136,1024]{1,0:T(8,128)(2,1)S(1)}, u32[]{:S(2)}, u32[]{:S(2)}) collective-permute-start(bf16[136,1024]{1,0:T(8,128)(2,1)S(1)} %get-tuple-element.42), channel_id=1, source_target_pairs={{4,0},{8,4},{12,8},{16,12},{20,16},{24,20},{28,24},{32,28},{36,32}... | collective-permute-start | bytes 835592 | tf_op jit(solution)/shard_map/ppermute | solution.py:250
  49.3 15.8 %collective-permute-start.5 = (bf16[128,1024]{1,0:T(8,128)(2,1)S(1)}, bf16[128,1024]{1,0:T(8,128)(2,1)S(1)}, u32[]{:S(2)}, u32[]{:S(2)}) collective-permute-start(bf16[128,1024]{1,0:T(8,128)(2,1)S(1)} %get-tuple-element.41), channel_id=1, source_target_pairs={{0,4},{4,8},{8,12},{12,16},{16,20},{20,24},{24,28},{28,32},{32,36}... | collective-permute-start | bytes 786440 | tf_op jit(solution)/shard_map/ppermute | solution.py:250
  57.6 19.8 %collective-permute-start.4 = (bf16[136,1024]{1,0:T(8,128)(2,1)S(1)}, bf16[136,1024]{1,0:T(8,128)(2,1)S(1)}, u32[]{:S(2)}, u32[]{:S(2)}) collective-permute-start(bf16[136,1024]{1,0:T(8,128)(2,1)S(1)} %get-tuple-element.39), channel_id=1, source_target_pairs={{4,0},{8,4},{12,8},{16,12},{20,16},{24,20},{28,24},{32,28},{36,32}... | collective-permute-start | bytes 835592 | tf_op jit(solution)/shard_map/ppermute | solution.py:250
  58.9 18.1 %collective-permute-start.3 = (bf16[128,1024]{1,0:T(8,128)(2,1)S(1)}, bf16[128,1024]{1,0:T(8,128)(2,1)S(1)}, u32[]{:S(2)}, u32[]{:S(2)}) collective-permute-start(bf16[128,1024]{1,0:T(8,128)(2,1)S(1)} %get-tuple-element.38), channel_id=1, source_target_pairs={{0,4},{4,8},{8,12},{12,16},{16,20},{20,24},{24,28},{28,32},{32,36}... | collective-permute-start | bytes 786440 | tf_op jit(solution)/shard_map/ppermute | solution.py:250
  111.9 10.6 %collective-permute-start.7 = (f32[8,128]{1,0:T(8,128)S(1)}, f32[8,128]{1,0:T(8,128)S(1)}, u32[]{:S(2)}, u32[]{:S(2)}) collective-permute-start(f32[8,128]{1,0:T(8,128)S(1)} %reduce_sum.9), channel_id=1, source_target_pairs={{0,0},{4,1},{8,2},{12,3},{128,4},{132,5},{136,6},{140,7},{256,8},{... | collective-permute-start | bytes 12296 | tf_op jit(solution)/shard_map/ppermute | solution.py:262

commit v5 on v4

--- a/solution.py
+++ b/solution.py
@@ -37,26 +37,23 @@
     return lax.dot_general(taps, spread, (((0,), (0,)), ((), ())), preferred_element_type=F32)[:8]
 
 
-def fused_kernel(q, k, v, g, u_before, d_after, tails, heads, taps, *refs):
+def fused_kernel(q, k, v, g, below, above, taps, *refs):
     gq, gk, gv, part, qs, ks, vs, feats = refs[-8:]
-    rows = q.shape[0]
+    rows = gq.shape[0]
     near = rows + 8
     both = taps[...].reshape(16, LANES)
     h = short_taps(both)
-    early, late = tails[...].astype(F32), heads[...].astype(F32)
+    early, late = below[...].astype(F32), above[...].astype(F32)
     made = []
     for i, (slot, x) in enumerate(((ks, k), (vs, v), (qs, q))):
-        slot[0:8] = early[16 * i : 16 * i + 8]
-        slot[8 : near] = x[...].astype(F32)
-        count = rows
-        if i < 2:
-            slot[near : near + 8] = late[16 * i : 16 * i + 8]
-            count = near
-        made.append(causal(h, slot, count))
+        slot[0:8] = early[KB + 8 * i : KB + 8 * i + 8]
+        slot[8:near] = x[...].astype(F32)[:rows]
+        slot[near : near + 8] = late[KB + 8 * i : KB + 8 * i + 8]
+        made.append(causal(h, slot, near))
     kf, vf, qf = made
-    gate = jnp.concatenate([g[...].astype(F32), late[32:40]], 0)
-    uw = jnp.concatenate([u_before[...].astype(F32), kf * vf], 0)
-    dw = jnp.concatenate([gate[:rows] * qf, d_after[...].astype(F32)], 0)
+    gate = jnp.concatenate([g[...].astype(F32)[:rows], late[KB + 24 :]], 0)
+    uw = jnp.concatenate([early[:KB], kf * vf], 0)
+    dw = jnp.concatenate([gate * qf, late[:KB]], 0)
     u_low, u_high = uw[: 2 * KB].astype(BF16), uw[16:].astype(BF16)
     d_low, d_high = dw[: 2 * KB].astype(BF16), dw[16:].astype(BF16)
     own = jnp.concatenate([dw[:rows], jnp.zeros((8, LANES), F32)], 0).astype(BF16)
@@ -109,7 +106,7 @@
             total = tile if a == 0 else total + pltpu.roll(tile, KB - 8 * a, 1)
         medium.append(jnp.sum(align_left(total), 0, keepdims=True))
     for half in range(2):
-        part[half, 0, 0:4] = jnp.concatenate(medium[4 * half : 4 * half + 4], 0)
+        part[half, 0:4] = jnp.concatenate(medium[4 * half : 4 * half + 4], 0)
 
     z_high = pick_groups(
         jnp.dot(jnp.concatenate(tails, 0), u_high, preferred_element_type=F32), 16, 0, 16
@@ -136,33 +133,33 @@
     short = jnp.concatenate([jnp.sum(x, 0, keepdims=True) for x in sums], 0)
     swapped = pltpu.roll(short, LANES // 2, 1)
     left = lane[:4] < LANES // 2
-    part[0, 0, 4:8] = jnp.where(left, short[:4], swapped[4:])
-    part[1, 0, 4:8] = jnp.where(left, swapped[:4], short[4:])
-
-
-def fused(q, k, v, g, u_before, d_after, tails, heads, taps, first, count, written=(), interpret=False):
-    rows, channels = q.shape
-    block = lambda r: pl.BlockSpec((r, LANES), lambda i: (0, first + i))
+    part[0, 4:8] = jnp.where(left, short[:4], swapped[4:])
+    part[1, 4:8] = jnp.where(left, swapped[:4], short[4:])
+
+
+def fused(signals, rows, below, above, taps, first, count, written=(), interpret=False):
+    channels = signals.shape[1]
+    block = lambda r, n=0: pl.BlockSpec((r, LANES), lambda i: (n, first + i))
     sent = lambda r: pl.BlockSpec((r, LANES), lambda i: (0, i))
     chunk = pl.BlockSpec((2, 1, 8, LANES), lambda i: ((first + i) % 2, (first + i) // 2, 0, 0))
     return pl.pallas_call(
         fused_kernel,
         grid=(count,),
-        in_specs=[block(rows)] * 4 + [sent(KB), sent(rows), block(48), block(48), chunk]
+        in_specs=[block(signals.shape[0] // 4, n) for n in range(4)] + [sent(KB + 24), sent(KB + 32), chunk]
         + [pl.BlockSpec(memory_space=pl.ANY)] * len(written),
-        out_specs=[block(rows)] * 3 + [chunk],
+        out_specs=[block(rows)] * 3 + [pl.BlockSpec((2, 8, LANES), lambda i: (first + i, 0, 0))],
         out_shape=[jax.ShapeDtypeStruct((rows, channels), BF16)] * 3
-        + [jax.ShapeDtypeStruct((4, channels // LANES // 2, 8, LANES), F32)],
+        + [jax.ShapeDtypeStruct((channels // LANES * 2, 8, LANES), F32)],
         scratch_shapes=[pltpu.VMEM((rows + 16, LANES), F32)] * 3
         + [pltpu.VMEM((3, rows + 8, LANES), F32)],
-        input_output_aliases={9 + n: n for n in range(len(written))},
+        input_output_aliases={7 + n: n for n in range(len(written))},
         compiler_params=params(),
         cost_estimate=pl.CostEstimate(
             flops=250_000_000 * count, bytes_accessed=500_000 * count, transcendentals=0
         ),
         interpret=interpret,
         name="fused",
-    )(q, k, v, g, u_before, d_after, tails, heads, taps, *written)
+    )(*[signals] * 4, below, above, taps, *written)
 
 
 def causal(h, slot, count):
@@ -172,61 +169,35 @@
     return total.astype(BF16).astype(F32)
 
 
-def ends_kernel(qt, kt, vt, kh, vh, gh, tails, heads):
-    for out, parts in ((tails, (kt, vt, qt)), (heads, (kh, vh, gh))):
-        for i, x in enumerate(parts):
-            out[16 * i : 16 * i + 16] = x[...]
-
-
-def ends(q, k, v, g, interpret=False):
-    rows, channels = q.shape
-    wide = channels // 2
-    tail = pl.BlockSpec((16, wide), lambda i: (rows // 16, i))
-    head = pl.BlockSpec((16, wide), lambda i: (0, i))
-    whole = pl.BlockSpec((48, wide), lambda i: (0, i))
-    return pl.pallas_call(
-        ends_kernel,
-        grid=(2,),
-        in_specs=[tail] * 3 + [head] * 3,
-        out_specs=[whole] * 2,
-        out_shape=[jax.ShapeDtypeStruct((48, channels), BF16)] * 2,
-        compiler_params=pltpu.CompilerParams(vmem_limit_bytes=56 * 1024 * 1024),
-        interpret=interpret,
-        name="ends",
-    )(q, k, v, k, v, g)
-
-
-def products_kernel(q, k, v, g, tails, taps, lower, upper, qs, ks, vs):
-    rows = q.shape[0]
+def products_kernel(q, k, v, g, taps, lower, upper, qs, ks, vs):
+    rows = ks.shape[0]
     h = short_taps(taps[...].reshape(16, LANES))
-    early = tails[...].astype(F32)
-    made = []
-    for i, (slot, x) in enumerate(((ks, k), (vs, v), (qs, q))):
-        slot[0:8] = early[16 * i : 16 * i + 8]
-        slot[8 : rows + 8] = x[...].astype(F32)
-        made.append(causal(h, slot, rows))
-    kf, vf, qf = made
-    lower[...] = (kf * vf)[rows - KB :].astype(BF16)
-    upper[...] = (g[...].astype(F32) * qf).astype(BF16)
-
-
-def products(q, k, v, g, tails, taps, first, count, interpret=False):
-    rows = q.shape[0]
-    block = lambda r: pl.BlockSpec((r, LANES), lambda i: (0, first + i))
+    for slot, x in ((ks, k), (vs, v), (qs, q)):
+        slot[...] = x[...].astype(F32)[:rows]
+    kf, vf, qf = (causal(h, slot, KB) for slot in (ks, vs, qs))
+    gate = g[...].astype(F32)[:rows]
+    end = slice(rows - 8, rows)
+    lower[...] = jnp.concatenate([kf * vf, ks[end], vs[end], qs[end]], 0).astype(BF16)
+    upper[...] = jnp.concatenate([gate[8:] * qf, ks[0:8], vs[0:8], qs[0:8], gate[:8]], 0).astype(BF16)
+
+
+def products(signals, rows, taps, first, count, interpret=False):
+    assert rows == KB + 8
+    block = lambda n: pl.BlockSpec((signals.shape[0] // 4, LANES), lambda i: (n, first + i))
     chunk = pl.BlockSpec((2, 1, 8, LANES), lambda i: ((first + i) % 2, (first + i) // 2, 0, 0))
     out = lambda r: pl.BlockSpec((r, LANES), lambda i: (0, i))
     return pl.pallas_call(
         products_kernel,
         grid=(count,),
-        in_specs=[block(rows)] * 4 + [block(48), chunk],
-        out_specs=[out(KB), out(rows)],
-        out_shape=[jax.ShapeDtypeStruct((r, count * LANES), BF16) for r in (KB, rows)],
-        scratch_shapes=[pltpu.VMEM((rows + 8, LANES), F32)] * 3,
+        in_specs=[block(n) for n in range(4)] + [chunk],
+        out_specs=[out(KB + 24), out(KB + 32)],
+        out_shape=[jax.ShapeDtypeStruct((KB + r, count * LANES), BF16) for r in (24, 32)],
+        scratch_shapes=[pltpu.VMEM((rows, LANES), F32)] * 3,
         compiler_params=params(),
         cost_estimate=pl.CostEstimate(flops=20_000_000, bytes_accessed=3_000_000, transcendentals=0),
         interpret=interpret,
         name="products",
-    )(q, k, v, g, tails, taps)
+    )(*[signals] * 4, taps)
 
 
 def pick_groups(stacked, rows, start, count):
@@ -269,10 +240,12 @@
 
 def shards(q, k, v, g, filt_short, filt_medium):
     blocks = q.shape[1] // LANES
-    packed, *signals = lax.optimization_barrier((pack_taps(filt_short, filt_medium), q, k, v, g))
-    own = turn(packed)
-    tails, heads = ends(*signals)
-    own, tails, heads = lax.optimization_barrier((own, step_ctx(tails, 1), step_ctx(heads, -1)))
+    rows = q.shape[0]
+    pad = jnp.zeros((8, q.shape[1]), BF16)
+    own, signals = lax.optimization_barrier((
+        turn(pack_taps(filt_short, filt_medium)),
+        jnp.concatenate([q, pad, k, pad, v, pad, g, pad], 0),
+    ))
     taps = lax.all_to_all(
         jnp.broadcast_to(own[None], (32, 8, LANES)), ("x", "z"), 0, 0, tiled=True
     ).reshape(4, 8, 8, LANES)
@@ -280,19 +253,22 @@
     pieces = [(0, half), (half, blocks - half)]
     sent = []
     for first, count in pieces:
-        lower, upper = products(q, k, v, g, tails, taps, first, count)
+        lower, upper = products(signals, rows, taps, first, count)
         sent.append((step_ctx(lower, 1), step_ctx(upper, -1)))
     made = ()
-    for (first, count), (u_before, d_after) in zip(pieces, sent):
-        made = fused(q, k, v, g, u_before, d_after, tails, heads, taps, first, count, made)
+    for (first, count), (below, above) in zip(pieces, sent):
+        made = fused(signals, rows, below, above, taps, first, count, made)
     grad_q, grad_k, grad_v, part = made
-    parts = lax.all_to_all(part.reshape(32, 8, LANES), ("x", "z"), 0, 0, tiled=True)
-    total = lax.psum(turn(jnp.sum(parts, 0), back=True), MP)
-    grad_short, grad_medium = finish(total)
+    parts = lax.all_to_all(part, ("z", "yh"), 0, 0, tiled=True)
+    goes = (jnp.arange(16) // 4 == lax.axis_index(MP)).astype(F32)
+    spread = goes[:, None, None] * jnp.sum(parts, 0)
+    arrived = lax.all_to_all(spread, ("x",) + MP, 0, 0, tiled=True)
+    grad_short, grad_medium = finish(arrived)
     return grad_q, grad_k, grad_v, grad_short.T, grad_medium.T
 
 
-def finish_kernel(total, short, medium):
+def finish_kernel(arrived, short, medium):
+    total = jnp.sum(arrived[...], 0)
     at = lax.broadcasted_iota(jnp.int32, (LANES, LANES), 0)
     to = lax.broadcasted_iota(jnp.int32, (LANES, LANES), 1)
     medium[...] = jnp.dot(

time: 133 us -> 122 us (0.917)
  blocking collectives: 48.9 us -> 38.2 us
  starting transfers between devices: 38.3 us -> 31.1 us
  waiting for transfers between devices: 8.86 us -> 15.3 us
  local copies, waits for them, and re-layouts: 0.71 us -> 2.3 us
    ppermute x2 -> x1, starting transfers between devices: 18.1 us -> 5.6 us  [turn(): return lax.ppermute(value, ALL, pairs)]
    all_to_all x0 -> x1, waiting for transfers between devices: none -> 11.3 us  [shards(): parts = lax.all_to_all(part, ('z', 'yh'), 0, 0, tiled=True)]
    all_to_all x0 -> x1, starting transfers between devices: none -> 11.2 us  [shards(): parts = lax.all_to_all(part, ('z', 'yh'), 0, 0, tiled=True)]
    ppermute x2 -> x1, waiting for transfers between devices: 8.5 us -> 0.01 us  [turn(): return lax.ppermute(value, ALL, pairs)]
    all_to_all x1, blocking collectives: 22.3 us -> 14.1 us  [shards(): arrived = lax.all_to_all(spread, ('x',) + MP, 0, 0, tiled=True)]
    psum x1 -> x0, blocking collectives: 7.18 us -> none  [shards(): total = lax.psum(turn(jnp.sum(parts, 0), back=True), MP)]
    ppermute x6 -> x4, starting transfers between devices: 20.2 us -> 14.2 us  [step_ctx(): lax.ppermute(value, CTX, [(i, i + step) for i in range(count) if 0 <= i +...]
    all_to_all x1, blocking collectives: 19.4 us -> 24.1 us  [shards(): lax.all_to_all(jnp.broadcast_to(own[None], (32, 8, LANES)), ('x', 'z'), 0...]
  transfers between devices with their start and end apart: 8 -> 6, of which waited for: 3 -> 3; matrix products, arithmetic and copies ran while one was open for 0% -> 2% of each run, Pallas kernels for 12% -> 13%
where the time goes in v5:
time: 122 us; the launch traced here: 121 us
  blocking collectives  38.2 us (31%)
  Pallas kernels  32.4 us (27%)
  starting transfers between devices  31.1 us (25%)
  waiting for transfers between devices  15.3 us (13%)
  local copies, waits for them, and re-layouts  2.3 us (2%)
    pallas_call x2, Pallas kernels, fused(): pl.pallas_call(fused_kernel, grid=(count,), in_specs=[block(signals.shape...  24.7 us
    all_to_all x1, blocking collectives, shards(): lax.all_to_all(jnp.broadcast_to(own[None], (32, 8, LANES)), ('x', 'z'), 0...  24.1 us
    ppermute x4, starting transfers between devices, step_ctx(): lax.ppermute(value, CTX, [(i, i + step) for i in range(count) if 0 <= i +...  14.2 us
    all_to_all x1, blocking collectives, shards(): arrived = lax.all_to_all(spread, ('x',) + MP, 0, 0, tiled=True)  14.1 us
    all_to_all x1, waiting for transfers between devices, shards(): parts = lax.all_to_all(part, ('z', 'yh'), 0, 0, tiled=True)  11.3 us
    all_to_all x1, starting transfers between devices, shards(): parts = lax.all_to_all(part, ('z', 'yh'), 0, 0, tiled=True)  11.2 us
    pallas_call x2, Pallas kernels, products(): pl.pallas_call(products_kernel, grid=(count,), in_specs=[block(n) for n i...  6.01 us
    ppermute x1, starting transfers between devices, turn(): return lax.ppermute(value, ALL, pairs)  5.6 us
  transfers between devices with their start and end apart: 6, of which 3 were waited for; matrix products, arithmetic and copies ran while one was open for 2% of the time, Pallas kernels for 13%

profile of v5, /device:TPU:1, one launch (start us, length us, event | category | flops | bytes accessed | tf_op | source)
XLA Modules:
  0.0 121.1 jit_solution(17240673559257144955)
XLA Ops:
  0.6 0.0 copy-start
  0.7 0.8 fusion.1
  1.4 5.6 %collective-permute-start = (bf16[8,128]{1,0:T(8,128)(2,1)S(1)}, bf16[8,128]{1,0:T(8,128)(2,1)S(1)}, u32[]{:S(2)}, u32[]{:S(2)}) collective-permute-start(bf16[8,128]{1,0:T(8,128)(2,1)S(1)} %fusion.1), channel_id=1, source_target_pairs={{0,0},{1,4},{2,8},{3,12},{4,128},{5,132},{6,136},{7,140},{8,256},{... | collective-permute-start | bytes 6152 | tf_op jit(solution)/shard_map/ppermute | solution.py:233
  7.1 1.1 constant_dynamic-update-slice_fusion.7
  8.2 1.1 constant_dynamic-update-slice_fusion.5
  9.4 0.0 collective-permute-done
  9.4 24.1 %all_to_all.15 = bf16[32,8,128]{2,1,0:T(8,128)(2,1)S(1)} all-to-all(bf16[32,8,128]{2,1,0:T(8,128)(2,1)S(1)} %broadcast_in_dim.5), channel_id=1, replica_groups=mesh['x'=4,'z'=8,'yh'=4,'yl'=2,'core'=2] {'x','z'}, dimensions={0} | all-to-all | bytes 131072 | tf_op jit(solution)/shard_map/all_to_all | solution.py:249
  33.5 3.0 %products.3 = (bf16[152,1024]{1,0:T(8,128)(2,1)S(1)}, bf16[160,1024]{1,0:T(8,128)(2,1)S(1)}) custom-call(bf16[576,2048]{1,0:T(8,128)(2,1)S(1)} %constant_dynamic-update-slice_fusion.q.k.v.g, bf16[576,2048]{1,0:T(8,128)(2,1)S(1)} %constant_dynamic-update-slice_fusion.q.k.v.g, bf16[576,2048]{1,0:T(8,128)(2,1)S(1)} %constant_dynamic-update-slice_fusion.q.k.v.g, ...), custom_call_target="tpu_custom_call" | custom-call | flops 20000000 | bytes 3000000 | tf_op jit(solution)/shard_map/products/pallas_call | solution.py:189
  36.5 1.3 %collective-permute-start.4 = (bf16[160,1024]{1,0:T(8,128)(2,1)S(1)}, bf16[160,1024]{1,0:T(8,128)(2,1)S(1)}, u32[]{:S(2)}, u32[]{:S(2)}) collective-permute-start(bf16[160,1024]{1,0:T(8,128)(2,1)S(1)} %get-tuple-element.26), channel_id=1, source_target_pairs={{4,0},{8,4},{12,8},{16,12},{20,16},{24,20},{28,24},{32,28},{36,32}... | collective-permute-start | bytes 983048 | tf_op jit(solution)/shard_map/ppermute | solution.py:221
  37.8 5.5 %collective-permute-start.3 = (bf16[152,1024]{1,0:T(8,128)(2,1)S(1)}, bf16[152,1024]{1,0:T(8,128)(2,1)S(1)}, u32[]{:S(2)}, u32[]{:S(2)}) collective-permute-start(bf16[152,1024]{1,0:T(8,128)(2,1)S(1)} %get-tuple-element.25), channel_id=1, source_target_pairs={{0,4},{4,8},{8,12},{12,16},{16,20},{20,24},{24,28},{28,32},{32,36}... | collective-permute-start | bytes 933896 | tf_op jit(solution)/shard_map/ppermute | solution.py:221
  43.3 3.0 %products.2 = (bf16[152,1024]{1,0:T(8,128)(2,1)S(1)}, bf16[160,1024]{1,0:T(8,128)(2,1)S(1)}) custom-call(bf16[576,2048]{1,0:T(8,128)(2,1)S(1)} %constant_dynamic-update-slice_fusion.q.k.v.g, bf16[576,2048]{1,0:T(8,128)(2,1)S(1)} %constant_dynamic-update-slice_fusion.q.k.v.g, bf16[576,2048]{1,0:T(8,128)(2,1)S(1)} %constant_dynamic-update-slice_fusion.q.k.v.g, ...), custom_call_target="tpu_custom_call" | custom-call | flops 20000000 | bytes 3000000 | tf_op jit(solution)/shard_map/products/pallas_call | solution.py:189
  46.4 1.3 %collective-permute-start.2 = (bf16[160,1024]{1,0:T(8,128)(2,1)S(1)}, bf16[160,1024]{1,0:T(8,128)(2,1)S(1)}, u32[]{:S(2)}, u32[]{:S(2)}) collective-permute-start(bf16[160,1024]{1,0:T(8,128)(2,1)S(1)} %get-tuple-element.24), channel_id=1, source_target_pairs={{4,0},{8,4},{12,8},{16,12},{20,16},{24,20},{28,24},{32,28},{36,32}... | collective-permute-start | bytes 983048 | tf_op jit(solution)/shard_map/ppermute | solution.py:221
  47.7 6.1 %collective-permute-start.1 = (bf16[152,1024]{1,0:T(8,128)(2,1)S(1)}, bf16[152,1024]{1,0:T(8,128)(2,1)S(1)}, u32[]{:S(2)}, u32[]{:S(2)}) collective-permute-start(bf16[152,1024]{1,0:T(8,128)(2,1)S(1)} %get-tuple-element.23), channel_id=1, source_target_pairs={{0,4},{4,8},{8,12},{12,16},{16,20},{20,24},{24,28},{28,32},{32,36}... | collective-permute-start | bytes 933896 | tf_op jit(solution)/shard_map/ppermute | solution.py:221
  53.8 0.0 collective-permute-done.3.below
  53.8 2.5 %collective-permute-done.4.above = bf16[160,1024]{1,0:T(8,128)(2,1)S(1)} collective-permute-done((bf16[160,1024]{1,0:T(8,128)(2,1)S(1)}, bf16[160,1024]{1,0:T(8,128)(2,1)S(1)}, u32[]{:S(2)}, u32[]{:S(2)}) %collective-permute-start.4) | collective-permute-done | bytes 327712 | tf_op jit(solution)/shard_map/ppermute | solution.py:221
  56.3 12.3 %fused.2 = (bf16[136,2048]{1,0:T(8,128)(2,1)}, bf16[136,2048]{1,0:T(8,128)(2,1)}, bf16[136,2048]{1,0:T(8,128)(2,1)}, f32[32,8,128]{2,1,0:T(8,128)}) custom-call(bf16[576,2048]{1,0:T(8,128)(2,1)S(1)} %constant_dynamic-update-slice_fusion.q.k.v.g, bf16[576,2048]{1,0:T(8,128)(2,1)S(1)} %constant_dynamic-update-slice_fusion.q.k.v.g, ...), custom_call_target="tpu_custom_call" | custom-call | flops 2000000000 | bytes 4000000 | tf_op jit(solution)/shard_map/fused/pallas_call | solution.py:145
  68.6 0.0 collective-permute-done.1.below
  68.6 1.6 %collective-permute-done.2.above = bf16[160,1024]{1,0:T(8,128)(2,1)S(1)} collective-permute-done((bf16[160,1024]{1,0:T(8,128)(2,1)S(1)}, bf16[160,1024]{1,0:T(8,128)(2,1)S(1)}, u32[]{:S(2)}, u32[]{:S(2)}) %collective-permute-start.2) | collective-permute-done | bytes 327712 | tf_op jit(solution)/shard_map/ppermute | solution.py:221
  70.2 12.4 %fused.3 = (bf16[136,2048]{1,0:T(8,128)(2,1)}, bf16[136,2048]{1,0:T(8,128)(2,1)}, bf16[136,2048]{1,0:T(8,128)(2,1)}, f32[32,8,128]{2,1,0:T(8,128)}) custom-call(bf16[576,2048]{1,0:T(8,128)(2,1)S(1)} %constant_dynamic-update-slice_fusion.q.k.v.g, ...), custom_call_target="tpu_custom_call", output_to_operand_aliasing={{0}: (7, {}), {1}: (8, {}), {2}: (9, {}), {3}: (10, {})} | custom-call | flops 2000000000 | bytes 4000000 | tf_op jit(solution)/shard_map/fused/pallas_call | solution.py:145
  82.6 11.2 %all-to-all-start.1 = ((f32[32,8,128]{2,1,0:T(8,128)}), f32[32,8,128]{2,1,0:T(8,128)S(1)}, u32[]{:S(2)}, u32[]{:S(2)}) async-start(f32[32,8,128]{2,1,0:T(8,128)} %get-tuple-element.34), calls=%async_computation.1 | async-start | bytes 262144 | tf_op jit(solution)/shard_map/all_to_all | solution.py:262
  93.8 11.3 %all-to-all-done.1 = f32[32,8,128]{2,1,0:T(8,128)S(1)} async-done(((f32[32,8,128]{2,1,0:T(8,128)}), f32[32,8,128]{2,1,0:T(8,128)S(1)}, u32[]{:S(2)}, u32[]{:S(2)}) %all-to-all-start.1) | async-done | bytes 131104 | tf_op jit(solution)/shard_map/all_to_all | solution.py:262
  105.2 0.1 broadcast_multiply_fusion
  105.2 14.1 %all_to_all.16.arrived = f32[16,8,128]{2,1,0:T(8,128)} all-to-all(f32[16,8,128]{2,1,0:T(8,128)S(1)} %broadcast_multiply_fusion), channel_id=1, replica_groups=mesh['x'=4,'z'=8,'yh'=4,'yl'=2,'core'=2] {'x','yl','core'}, dimensions={0} | all-to-all | bytes 131072 | tf_op jit(solution)/shard_map/all_to_all | solution.py:265
  119.4 1.7 %finish.1 = (f32[4,7]{1,0:T(4,128)}, f32[4,128]{1,0:T(4,128)}) custom-call(f32[16,8,128]{2,1,0:T(8,128)} %all_to_all.16.arrived), custom_call_target="tpu_custom_call" | custom-call | tf_op jit(solution)/shard_map/finish/pallas_call | solution.py:292
  (12 shorter events, 0.2 us)
Async XLA Ops:
  0.6 8.6 %copy-start = (bf16[136,2048]{1,0:T(8,128)(2,1)S(1)}, bf16[136,2048]{1,0:T(8,128)(2,1)}, u32[]{:S(2)}) copy-start(bf16[136,2048]{1,0:T(8,128)(2,1)} %param.8) | copy-start | bytes 1671172
  0.6 8.7 %copy-start.1 = (bf16[136,2048]{1,0:T(8,128)(2,1)S(1)}, bf16[136,2048]{1,0:T(8,128)(2,1)}, u32[]{:S(2)}) copy-start(bf16[136,2048]{1,0:T(8,128)(2,1)} %param.9) | copy-start | bytes 1671172
  1.4 8.0 %collective-permute-start = (bf16[8,128]{1,0:T(8,128)(2,1)S(1)}, bf16[8,128]{1,0:T(8,128)(2,1)S(1)}, u32[]{:S(2)}, u32[]{:S(2)}) collective-permute-start(bf16[8,128]{1,0:T(8,128)(2,1)S(1)} %fusion.1), channel_id=1, source_target_pairs={{0,0},{1,4},{2,8},{3,12},{4,128},{5,132},{6,136},{7,140},{8,256},{... | collective-permute-start | bytes 6152 | tf_op jit(solution)/shard_map/ppermute | solution.py:233
  36.5 19.8 %collective-permute-start.4 = (bf16[160,1024]{1,0:T(8,128)(2,1)S(1)}, bf16[160,1024]{1,0:T(8,128)(2,1)S(1)}, u32[]{:S(2)}, u32[]{:S(2)}) collective-permute-start(bf16[160,1024]{1,0:T(8,128)(2,1)S(1)} %get-tuple-element.26), channel_id=1, source_target_pairs={{4,0},{8,4},{12,8},{16,12},{20,16},{24,20},{28,24},{32,28},{36,32}... | collective-permute-start | bytes 983048 | tf_op jit(solution)/shard_map/ppermute | solution.py:221
  37.8 16.0 %collective-permute-start.3 = (bf16[152,1024]{1,0:T(8,128)(2,1)S(1)}, bf16[152,1024]{1,0:T(8,128)(2,1)S(1)}, u32[]{:S(2)}, u32[]{:S(2)}) collective-permute-start(bf16[152,1024]{1,0:T(8,128)(2,1)S(1)} %get-tuple-element.25), channel_id=1, source_target_pairs={{0,4},{4,8},{8,12},{12,16},{16,20},{20,24},{24,28},{28,32},{32,36}... | collective-permute-start | bytes 933896 | tf_op jit(solution)/shard_map/ppermute | solution.py:221
  46.4 23.8 %collective-permute-start.2 = (bf16[160,1024]{1,0:T(8,128)(2,1)S(1)}, bf16[160,1024]{1,0:T(8,128)(2,1)S(1)}, u32[]{:S(2)}, u32[]{:S(2)}) collective-permute-start(bf16[160,1024]{1,0:T(8,128)(2,1)S(1)} %get-tuple-element.24), channel_id=1, source_target_pairs={{4,0},{8,4},{12,8},{16,12},{20,16},{24,20},{28,24},{32,28},{36,32}... | collective-permute-start | bytes 983048 | tf_op jit(solution)/shard_map/ppermute | solution.py:221
  47.7 20.9 %collective-permute-start.1 = (bf16[152,1024]{1,0:T(8,128)(2,1)S(1)}, bf16[152,1024]{1,0:T(8,128)(2,1)S(1)}, u32[]{:S(2)}, u32[]{:S(2)}) collective-permute-start(bf16[152,1024]{1,0:T(8,128)(2,1)S(1)} %get-tuple-element.23), channel_id=1, source_target_pairs={{0,4},{4,8},{8,12},{12,16},{16,20},{20,24},{24,28},{28,32},{32,36}... | collective-permute-start | bytes 933896 | tf_op jit(solution)/shard_map/ppermute | solution.py:221
  82.6 22.6 %all-to-all-start.1 = ((f32[32,8,128]{2,1,0:T(8,128)}), f32[32,8,128]{2,1,0:T(8,128)S(1)}, u32[]{:S(2)}, u32[]{:S(2)}) async-start(f32[32,8,128]{2,1,0:T(8,128)} %get-tuple-element.34), calls=%async_computation.1 | async-start | bytes 262144 | tf_op jit(solution)/shard_map/all_to_all | solution.py:262

commit v6 on v5

--- a/solution.py
+++ b/solution.py
@@ -19,6 +19,7 @@
 MP = ("yl", "core")
 ALL = CTX + MP
 SIZES = (4, 8, 4, 4)
+WIDE = 2 * LANES
 VMEM = 12 * 1024 * 1024
 
 
@@ -39,9 +40,19 @@
 
 def fused_kernel(q, k, v, g, below, above, taps, *refs):
     gq, gk, gv, part, qs, ks, vs, feats = refs[-8:]
+    for b in range(WIDE // LANES):
+        lanes = slice(b * LANES, (b + 1) * LANES)
+        one_block(
+            *(x.at[:, lanes] for x in (q, k, v, g, below, above)), taps, b,
+            *(x.at[:, lanes] for x in (gq, gk, gv)), part.at[2 * b : 2 * b + 2],
+            qs.at[b], ks.at[b], vs.at[b], feats.at[b],
+        )
+
+
+def one_block(q, k, v, g, below, above, taps, b, gq, gk, gv, part, qs, ks, vs, feats):
     rows = gq.shape[0]
     near = rows + 8
-    both = taps[...].reshape(16, LANES)
+    both = taps[2 * b : 2 * b + 2].reshape(16, LANES)
     h = short_taps(both)
     early, late = below[...].astype(F32), above[...].astype(F32)
     made = []
@@ -54,68 +65,64 @@
     gate = jnp.concatenate([g[...].astype(F32)[:rows], late[KB + 24 :]], 0)
     uw = jnp.concatenate([early[:KB], kf * vf], 0)
     dw = jnp.concatenate([gate * qf, late[:KB]], 0)
-    u_low, u_high = uw[: 2 * KB].astype(BF16), uw[16:].astype(BF16)
-    d_low, d_high = dw[: 2 * KB].astype(BF16), dw[16:].astype(BF16)
-    own = jnp.concatenate([dw[:rows], jnp.zeros((8, LANES), F32)], 0).astype(BF16)
+
+    part_rows = near // 2
+    span = part_rows + KB
+    blank = jnp.zeros((2 * KB - span, 2 * LANES), F32)
+
+    def windows(x):
+        pair = jnp.concatenate([x[:span], x[part_rows : part_rows + span]], 1)
+        return jnp.concatenate([pair, blank], 0).astype(BF16)
+
+    u_win, d_win = windows(uw), windows(dw)
+    own = jnp.concatenate([dw[:rows], jnp.zeros((8, LANES), F32)], 0)
+    own = jnp.concatenate([own[:part_rows], own[part_rows:]], 1)
 
     at = lax.broadcasted_iota(jnp.int32, (LANES, LANES), 0)
     to = lax.broadcasted_iota(jnp.int32, (LANES, LANES), 1)
     flip = (at + to == LANES - 1).astype(BF16)
     straight = both.astype(F32)
     turned = jnp.dot(both, flip, preferred_element_type=F32)
-    lane = lax.broadcasted_iota(jnp.int32, (16, LANES), 1)
-    row = lax.broadcasted_iota(jnp.int32, (16, LANES), 0)
-    lane8, row8 = lane[:8], row[:8]
-    contract = (((1,), (1,)), ((), ()))
-    wide = lane_group((2 * KB, LANES))
-
-    def square(line, first):
-        base = pltpu.roll(jnp.broadcast_to(line, (16, LANES)), first, 1, stride=1, stride_axis=0)
+    lane = lax.broadcasted_iota(jnp.int32, (8, LANES), 1)
+    row = lax.broadcasted_iota(jnp.int32, (8, LANES), 0)
+    groups = jnp.concatenate([lane_group((part_rows, LANES))] * 2, 1)
+
+    def squares(lines, first):
         tiles = []
-        for a in range(KB // 16):
-            tile = pltpu.roll(base, 16 * a, 1) if a else base
-            upper = lane > row + 16 * a if first else lane >= row + 16 * a
-            parts = [jnp.where(upper, tile, 0.0), jnp.where(upper, 0.0, tile)]
-            tiles.append(jnp.concatenate(parts, 1).astype(BF16))
-        return tiles
-
-    z_low = du_high = jnp.zeros((KB, LANES), F32)
-    tails, heads, medium = [], [], []
-    rest = jnp.concatenate([jnp.where(wide[:16] == i, own[KB:], 0) for i in range(GPB)], 0)
-    last = lax.dot_general(rest, u_high, contract, preferred_element_type=F32)
+        for i in range(GPB):
+            line = lines[i // 4 * 8 + i % 4 : i // 4 * 8 + i % 4 + 1]
+            base = pltpu.roll(jnp.broadcast_to(line, (8, LANES)), first, 1, stride=1, stride_axis=0)
+            for a in range(part_rows // 8):
+                tile = pltpu.roll(base, 8 * a, 1) if a else base
+                upper = lane > row + 8 * a if first else lane >= row + 8 * a
+                tiles.append(
+                    jnp.concatenate([jnp.where(upper, tile, 0.0), jnp.where(upper, 0.0, tile)], 1)
+                )
+        return jnp.concatenate(tiles, 0).astype(BF16)
+
+    def filtered(matrices, window):
+        every = jnp.dot(matrices, window, preferred_element_type=F32)
+        out = every[:part_rows]
+        for i in range(1, GPB):
+            out = jnp.where(groups == i, every[part_rows * i : part_rows * (i + 1)], out)
+        return jnp.concatenate([out[:, :LANES], out[:, LANES:]], 0)
+
+    z = filtered(squares(turned, 1), u_win)
+    du = filtered(squares(straight, 0), d_win)
+
+    mine = jnp.concatenate([jnp.where(groups == i, own, 0.0) for i in range(GPB)], 0).astype(BF16)
+    prod = lax.dot_general(mine, u_win, (((1,), (1,)), ((), ())), preferred_element_type=F32)
+    medium = []
     for i in range(GPB):
-        line = i // 4 * 8 + i % 4
-        tc = square(turned[line : line + 1], 1)
-        ta = square(straight[line : line + 1], 0)
-        tails.append(tc[-1])
-        heads.append(ta[0])
-        z_low = z_low + jnp.dot(
-            jnp.concatenate(tc, 0), jnp.where(wide == i, u_low, 0), preferred_element_type=F32
-        )
-        du_high = du_high + jnp.dot(
-            jnp.concatenate(ta, 0), jnp.where(wide == i, d_high, 0), preferred_element_type=F32
-        )
-        mine = jnp.where(wide[:KB] == i, own[:KB], 0)
-        prod = lax.dot_general(mine, u_low, contract, preferred_element_type=F32)
         total = None
-        for a in range(KB // 8):
-            tile = prod[8 * a : 8 * a + 8]
-            if a == KB // 8 - 2:
-                tile = tile + last[16 * i : 16 * i + 8]
-            tile = jnp.where(lane8 > row8 + 8 * a, tile[:, :KB], tile[:, KB:])
+        for a in range(part_rows // 8):
+            tile = prod[part_rows * i + 8 * a : part_rows * i + 8 * a + 8]
+            tile = jnp.where(lane > row + 8 * a, tile[:, :KB], tile[:, KB:])
             total = tile if a == 0 else total + pltpu.roll(tile, KB - 8 * a, 1)
         medium.append(jnp.sum(align_left(total), 0, keepdims=True))
     for half in range(2):
         part[half, 0:4] = jnp.concatenate(medium[4 * half : 4 * half + 4], 0)
 
-    z_high = pick_groups(
-        jnp.dot(jnp.concatenate(tails, 0), u_high, preferred_element_type=F32), 16, 0, 16
-    )
-    du_low = pick_groups(
-        jnp.dot(jnp.concatenate(heads, 0), d_low, preferred_element_type=F32), 16, 0, 16
-    )
-    z = jnp.concatenate([z_low, z_high], 0)
-    du = jnp.concatenate([du_low, du_high], 0)
     feats[0] = (gate[:near] * z).astype(BF16).astype(F32)
     feats[1] = (du * vf).astype(BF16).astype(F32)
     feats[2] = (du * kf).astype(BF16).astype(F32)
@@ -139,23 +146,23 @@
 
 def fused(signals, rows, below, above, taps, first, count, written=(), interpret=False):
     channels = signals.shape[1]
-    block = lambda r, n=0: pl.BlockSpec((r, LANES), lambda i: (n, first + i))
-    sent = lambda r: pl.BlockSpec((r, LANES), lambda i: (0, i))
-    chunk = pl.BlockSpec((2, 1, 8, LANES), lambda i: ((first + i) % 2, (first + i) // 2, 0, 0))
+    block = lambda r, n=0: pl.BlockSpec((r, WIDE), lambda i: (n, first + i))
+    sent = lambda r: pl.BlockSpec((r, WIDE), lambda i: (0, i))
+    chunk = pl.BlockSpec((4, 1, 8, LANES), lambda i: (0, first + i, 0, 0))
     return pl.pallas_call(
         fused_kernel,
         grid=(count,),
         in_specs=[block(signals.shape[0] // 4, n) for n in range(4)] + [sent(KB + 24), sent(KB + 32), chunk]
         + [pl.BlockSpec(memory_space=pl.ANY)] * len(written),
-        out_specs=[block(rows)] * 3 + [pl.BlockSpec((2, 8, LANES), lambda i: (first + i, 0, 0))],
+        out_specs=[block(rows)] * 3 + [pl.BlockSpec((4, 8, LANES), lambda i: (first + i, 0, 0))],
         out_shape=[jax.ShapeDtypeStruct((rows, channels), BF16)] * 3
         + [jax.ShapeDtypeStruct((channels // LANES * 2, 8, LANES), F32)],
-        scratch_shapes=[pltpu.VMEM((rows + 16, LANES), F32)] * 3
-        + [pltpu.VMEM((3, rows + 8, LANES), F32)],
+        scratch_shapes=[pltpu.VMEM((WIDE // LANES, rows + 16, LANES), F32)] * 3
+        + [pltpu.VMEM((WIDE // LANES, 3, rows + 8, LANES), F32)],
         input_output_aliases={7 + n: n for n in range(len(written))},
         compiler_params=params(),
         cost_estimate=pl.CostEstimate(
-            flops=250_000_000 * count, bytes_accessed=500_000 * count, transcendentals=0
+            flops=500_000_000 * count, bytes_accessed=1_000_000 * count, transcendentals=0
         ),
         interpret=interpret,
         name="fused",
@@ -170,8 +177,17 @@
 
 
 def products_kernel(q, k, v, g, taps, lower, upper, qs, ks, vs):
+    for b in range(WIDE // LANES):
+        lanes = slice(b * LANES, (b + 1) * LANES)
+        one_product(
+            *(x.at[:, lanes] for x in (q, k, v, g)), taps[2 * b : 2 * b + 2],
+            lower.at[:, lanes], upper.at[:, lanes], qs.at[b], ks.at[b], vs.at[b],
+        )
+
+
+def one_product(q, k, v, g, taps, lower, upper, qs, ks, vs):
     rows = ks.shape[0]
-    h = short_taps(taps[...].reshape(16, LANES))
+    h = short_taps(taps.reshape(16, LANES))
     for slot, x in ((ks, k), (vs, v), (qs, q)):
         slot[...] = x[...].astype(F32)[:rows]
     kf, vf, qf = (causal(h, slot, KB) for slot in (ks, vs, qs))
@@ -183,29 +199,21 @@
 
 def products(signals, rows, taps, first, count, interpret=False):
     assert rows == KB + 8
-    block = lambda n: pl.BlockSpec((signals.shape[0] // 4, LANES), lambda i: (n, first + i))
-    chunk = pl.BlockSpec((2, 1, 8, LANES), lambda i: ((first + i) % 2, (first + i) // 2, 0, 0))
-    out = lambda r: pl.BlockSpec((r, LANES), lambda i: (0, i))
+    block = lambda n: pl.BlockSpec((signals.shape[0] // 4, WIDE), lambda i: (n, first + i))
+    chunk = pl.BlockSpec((4, 1, 8, LANES), lambda i: (0, first + i, 0, 0))
+    out = lambda r: pl.BlockSpec((r, WIDE), lambda i: (0, i))
     return pl.pallas_call(
         products_kernel,
         grid=(count,),
         in_specs=[block(n) for n in range(4)] + [chunk],
         out_specs=[out(KB + 24), out(KB + 32)],
-        out_shape=[jax.ShapeDtypeStruct((KB + r, count * LANES), BF16) for r in (24, 32)],
-        scratch_shapes=[pltpu.VMEM((rows, LANES), F32)] * 3,
+        out_shape=[jax.ShapeDtypeStruct((KB + r, count * WIDE), BF16) for r in (24, 32)],
+        scratch_shapes=[pltpu.VMEM((WIDE // LANES, rows, LANES), F32)] * 3,
         compiler_params=params(),
         cost_estimate=pl.CostEstimate(flops=20_000_000, bytes_accessed=3_000_000, transcendentals=0),
         interpret=interpret,
         name="products",
     )(*[signals] * 4, taps)
-
-
-def pick_groups(stacked, rows, start, count):
-    groups = lane_group((count, LANES))
-    out = stacked[start : start + count]
-    for g in range(1, GPB):
-        out = jnp.where(groups == g, stacked[g * rows + start : g * rows + start + count], out)
-    return out
 
 
 def align_left(tile):
@@ -239,7 +247,7 @@
 
 
 def shards(q, k, v, g, filt_short, filt_medium):
-    blocks = q.shape[1] // LANES
+    blocks = q.shape[1] // WIDE
     rows = q.shape[0]
     pad = jnp.zeros((8, q.shape[1]), BF16)
     own, signals = lax.optimization_barrier((

time: 122 us -> 117 us (0.959)
  Pallas kernels: 32.4 us -> 24.9 us
  waiting for transfers between devices: 15.3 us -> 21.8 us
  starting transfers between devices: 31.1 us -> 25.8 us
  blocking collectives: 38.2 us -> 40 us
    ppermute x4, waiting for transfers between devices: 4.05 us -> 10.5 us  [step_ctx(): lax.ppermute(value, CTX, [(i, i + step) for i in range(count) if 0 <= i +...]
    all_to_all x1, starting transfers between devices: 11.2 us -> 5.94 us  [shards(): parts = lax.all_to_all(part, ('z', 'yh'), 0, 0, tiled=True)]
    pallas_call x2, Pallas kernels: 24.7 us -> 19.4 us  [fused(): pl.pallas_call(fused_kernel, grid=(count,), in_specs=[block(signals.shape...]
    pallas_call x2, Pallas kernels: 6.01 us -> 3.8 us  [products(): pl.pallas_call(products_kernel, grid=(count,), in_specs=[block(n) for n i...]
    all_to_all x1, blocking collectives: 14.1 us -> 15.9 us  [shards(): arrived = lax.all_to_all(spread, ('x',) + MP, 0, 0, tiled=True)]
  transfers between devices with their start and end apart: 6 -> 6, of which waited for: 3 -> 2; matrix products, arithmetic and copies ran while one was open for 2% -> 2% of each run, Pallas kernels for 13% -> 10%
where the time goes in v6:
time: 117 us; the launch traced here: 116 us
  blocking collectives  40 us (34%)
  starting transfers between devices  25.8 us (22%)
  Pallas kernels  24.9 us (21%)
  waiting for transfers between devices  21.8 us (19%)
  local copies, waits for them, and re-layouts  2.3 us (2%)
    all_to_all x1, blocking collectives, shards(): lax.all_to_all(jnp.broadcast_to(own[None], (32, 8, LANES)), ('x', 'z'), 0...  24.1 us
    pallas_call x2, Pallas kernels, fused(): pl.pallas_call(fused_kernel, grid=(count,), in_specs=[block(signals.shape...  19.4 us
    all_to_all x1, blocking collectives, shards(): arrived = lax.all_to_all(spread, ('x',) + MP, 0, 0, tiled=True)  15.9 us
    ppermute x4, starting transfers between devices, step_ctx(): lax.ppermute(value, CTX, [(i, i + step) for i in range(count) if 0 <= i +...  14.2 us
    all_to_all x1, waiting for transfers between devices, shards(): parts = lax.all_to_all(part, ('z', 'yh'), 0, 0, tiled=True)  11.3 us
    ppermute x4, waiting for transfers between devices, step_ctx(): lax.ppermute(value, CTX, [(i, i + step) for i in range(count) if 0 <= i +...  10.5 us
    all_to_all x1, starting transfers between devices, shards(): parts = lax.all_to_all(part, ('z', 'yh'), 0, 0, tiled=True)  5.94 us
    ppermute x1, starting transfers between devices, turn(): return lax.ppermute(value, ALL, pairs)  5.6 us
  transfers between devices with their start and end apart: 6, of which 2 were waited for; matrix products, arithmetic and copies ran while one was open for 2% of the time, Pallas kernels for 10%

profile of v6, /device:TPU:1, one launch (start us, length us, event | category | flops | bytes accessed | tf_op | source)
XLA Modules:
  0.0 116.5 jit_solution(15406659493044834044)
XLA Ops:
  0.6 0.0 copy-start
  0.7 0.8 fusion.1
  1.4 5.6 %collective-permute-start = (bf16[8,128]{1,0:T(8,128)(2,1)S(1)}, bf16[8,128]{1,0:T(8,128)(2,1)S(1)}, u32[]{:S(2)}, u32[]{:S(2)}) collective-permute-start(bf16[8,128]{1,0:T(8,128)(2,1)S(1)} %fusion.1), channel_id=1, source_target_pairs={{0,0},{1,4},{2,8},{3,12},{4,128},{5,132},{6,136},{7,140},{8,256},{... | collective-permute-start | bytes 6152 | tf_op jit(solution)/shard_map/ppermute | solution.py:241
  7.1 1.1 constant_dynamic-update-slice_fusion.7
  8.2 1.1 constant_dynamic-update-slice_fusion.5
  9.4 0.0 collective-permute-done
  9.4 24.1 %all_to_all.15 = bf16[32,8,128]{2,1,0:T(8,128)(2,1)S(1)} all-to-all(bf16[32,8,128]{2,1,0:T(8,128)(2,1)S(1)} %broadcast_in_dim.5), channel_id=1, replica_groups=mesh['x'=4,'z'=8,'yh'=4,'yl'=2,'core'=2] {'x','z'}, dimensions={0} | all-to-all | bytes 131072 | tf_op jit(solution)/shard_map/all_to_all | solution.py:257
  33.5 1.9 %products.3 = (bf16[152,1024]{1,0:T(8,128)(2,1)S(1)}, bf16[160,1024]{1,0:T(8,128)(2,1)S(1)}) custom-call(bf16[576,2048]{1,0:T(8,128)(2,1)S(1)} %constant_dynamic-update-slice_fusion.q.k.v.g, bf16[576,2048]{1,0:T(8,128)(2,1)S(1)} %constant_dynamic-update-slice_fusion.q.k.v.g, bf16[576,2048]{1,0:T(8,128)(2,1)S(1)} %constant_dynamic-update-slice_fusion.q.k.v.g, ...), custom_call_target="tpu_custom_call" | custom-call | flops 20000000 | bytes 3000000 | tf_op jit(solution)/shard_map/products/pallas_call | solution.py:205
  35.4 1.3 %collective-permute-start.4 = (bf16[160,1024]{1,0:T(8,128)(2,1)S(1)}, bf16[160,1024]{1,0:T(8,128)(2,1)S(1)}, u32[]{:S(2)}, u32[]{:S(2)}) collective-permute-start(bf16[160,1024]{1,0:T(8,128)(2,1)S(1)} %get-tuple-element.26), channel_id=1, source_target_pairs={{4,0},{8,4},{12,8},{16,12},{20,16},{24,20},{28,24},{32,28},{36,32}... | collective-permute-start | bytes 983048 | tf_op jit(solution)/shard_map/ppermute | solution.py:229
  36.7 5.5 %collective-permute-start.3 = (bf16[152,1024]{1,0:T(8,128)(2,1)S(1)}, bf16[152,1024]{1,0:T(8,128)(2,1)S(1)}, u32[]{:S(2)}, u32[]{:S(2)}) collective-permute-start(bf16[152,1024]{1,0:T(8,128)(2,1)S(1)} %get-tuple-element.25), channel_id=1, source_target_pairs={{0,4},{4,8},{8,12},{12,16},{16,20},{20,24},{24,28},{28,32},{32,36}... | collective-permute-start | bytes 933896 | tf_op jit(solution)/shard_map/ppermute | solution.py:229
  42.3 1.9 %products.2 = (bf16[152,1024]{1,0:T(8,128)(2,1)S(1)}, bf16[160,1024]{1,0:T(8,128)(2,1)S(1)}) custom-call(bf16[576,2048]{1,0:T(8,128)(2,1)S(1)} %constant_dynamic-update-slice_fusion.q.k.v.g, bf16[576,2048]{1,0:T(8,128)(2,1)S(1)} %constant_dynamic-update-slice_fusion.q.k.v.g, bf16[576,2048]{1,0:T(8,128)(2,1)S(1)} %constant_dynamic-update-slice_fusion.q.k.v.g, ...), custom_call_target="tpu_custom_call" | custom-call | flops 20000000 | bytes 3000000 | tf_op jit(solution)/shard_map/products/pallas_call | solution.py:205
  44.2 1.3 %collective-permute-start.2 = (bf16[160,1024]{1,0:T(8,128)(2,1)S(1)}, bf16[160,1024]{1,0:T(8,128)(2,1)S(1)}, u32[]{:S(2)}, u32[]{:S(2)}) collective-permute-start(bf16[160,1024]{1,0:T(8,128)(2,1)S(1)} %get-tuple-element.24), channel_id=1, source_target_pairs={{4,0},{8,4},{12,8},{16,12},{20,16},{24,20},{28,24},{32,28},{36,32}... | collective-permute-start | bytes 983048 | tf_op jit(solution)/shard_map/ppermute | solution.py:229
  45.5 6.1 %collective-permute-start.1 = (bf16[152,1024]{1,0:T(8,128)(2,1)S(1)}, bf16[152,1024]{1,0:T(8,128)(2,1)S(1)}, u32[]{:S(2)}, u32[]{:S(2)}) collective-permute-start(bf16[152,1024]{1,0:T(8,128)(2,1)S(1)} %get-tuple-element.23), channel_id=1, source_target_pairs={{0,4},{4,8},{8,12},{12,16},{16,20},{20,24},{24,28},{28,32},{32,36}... | collective-permute-start | bytes 933896 | tf_op jit(solution)/shard_map/ppermute | solution.py:229
  51.6 0.0 collective-permute-done.3.below
  51.6 10.5 %collective-permute-done.4.above = bf16[160,1024]{1,0:T(8,128)(2,1)S(1)} collective-permute-done((bf16[160,1024]{1,0:T(8,128)(2,1)S(1)}, bf16[160,1024]{1,0:T(8,128)(2,1)S(1)}, u32[]{:S(2)}, u32[]{:S(2)}) %collective-permute-start.4) | collective-permute-done | bytes 327712 | tf_op jit(solution)/shard_map/ppermute | solution.py:229
  62.1 9.7 %fused.2 = (bf16[136,2048]{1,0:T(8,128)(2,1)}, bf16[136,2048]{1,0:T(8,128)(2,1)}, bf16[136,2048]{1,0:T(8,128)(2,1)}, f32[32,8,128]{2,1,0:T(8,128)}) custom-call(bf16[576,2048]{1,0:T(8,128)(2,1)S(1)} %constant_dynamic-update-slice_fusion.q.k.v.g, bf16[576,2048]{1,0:T(8,128)(2,1)S(1)} %constant_dynamic-update-slice_fusion.q.k.v.g, ...), custom_call_target="tpu_custom_call" | custom-call | flops 2000000000 | bytes 4000000 | tf_op jit(solution)/shard_map/fused/pallas_call | solution.py:152
  71.8 0.0 collective-permute-done.1.below
  71.8 0.0 collective-permute-done.2.above
  71.8 9.7 %fused.3 = (bf16[136,2048]{1,0:T(8,128)(2,1)}, bf16[136,2048]{1,0:T(8,128)(2,1)}, bf16[136,2048]{1,0:T(8,128)(2,1)}, f32[32,8,128]{2,1,0:T(8,128)}) custom-call(bf16[576,2048]{1,0:T(8,128)(2,1)S(1)} %constant_dynamic-update-slice_fusion.q.k.v.g, ...), custom_call_target="tpu_custom_call", output_to_operand_aliasing={{0}: (7, {}), {1}: (8, {}), {2}: (9, {}), {3}: (10, {})} | custom-call | flops 2000000000 | bytes 4000000 | tf_op jit(solution)/shard_map/fused/pallas_call | solution.py:152
  81.5 5.9 %all-to-all-start.1 = ((f32[32,8,128]{2,1,0:T(8,128)}), f32[32,8,128]{2,1,0:T(8,128)S(1)}, u32[]{:S(2)}, u32[]{:S(2)}) async-start(f32[32,8,128]{2,1,0:T(8,128)} %get-tuple-element.34), calls=%async_computation.1 | async-start | bytes 262144 | tf_op jit(solution)/shard_map/all_to_all | solution.py:270
  87.5 11.3 %all-to-all-done.1 = f32[32,8,128]{2,1,0:T(8,128)S(1)} async-done(((f32[32,8,128]{2,1,0:T(8,128)}), f32[32,8,128]{2,1,0:T(8,128)S(1)}, u32[]{:S(2)}, u32[]{:S(2)}) %all-to-all-start.1) | async-done | bytes 131104 | tf_op jit(solution)/shard_map/all_to_all | solution.py:270
  98.8 0.1 broadcast_multiply_fusion
  98.9 15.9 %all_to_all.16.arrived = f32[16,8,128]{2,1,0:T(8,128)} all-to-all(f32[16,8,128]{2,1,0:T(8,128)S(1)} %broadcast_multiply_fusion), channel_id=1, replica_groups=mesh['x'=4,'z'=8,'yh'=4,'yl'=2,'core'=2] {'x','yl','core'}, dimensions={0} | all-to-all | bytes 131072 | tf_op jit(solution)/shard_map/all_to_all | solution.py:273
  114.8 1.7 %finish.1 = (f32[4,7]{1,0:T(4,128)}, f32[4,128]{1,0:T(4,128)}) custom-call(f32[16,8,128]{2,1,0:T(8,128)} %all_to_all.16.arrived), custom_call_target="tpu_custom_call" | custom-call | tf_op jit(solution)/shard_map/finish/pallas_call | solution.py:300
  (12 shorter events, 0.2 us)
Async XLA Ops:
  0.6 8.6 %copy-start = (bf16[136,2048]{1,0:T(8,128)(2,1)S(1)}, bf16[136,2048]{1,0:T(8,128)(2,1)}, u32[]{:S(2)}) copy-start(bf16[136,2048]{1,0:T(8,128)(2,1)} %param.8) | copy-start | bytes 1671172
  0.6 8.7 %copy-start.1 = (bf16[136,2048]{1,0:T(8,128)(2,1)S(1)}, bf16[136,2048]{1,0:T(8,128)(2,1)}, u32[]{:S(2)}) copy-start(bf16[136,2048]{1,0:T(8,128)(2,1)} %param.9) | copy-start | bytes 1671172
  1.4 8.0 %collective-permute-start = (bf16[8,128]{1,0:T(8,128)(2,1)S(1)}, bf16[8,128]{1,0:T(8,128)(2,1)S(1)}, u32[]{:S(2)}, u32[]{:S(2)}) collective-permute-start(bf16[8,128]{1,0:T(8,128)(2,1)S(1)} %fusion.1), channel_id=1, source_target_pairs={{0,0},{1,4},{2,8},{3,12},{4,128},{5,132},{6,136},{7,140},{8,256},{... | collective-permute-start | bytes 6152 | tf_op jit(solution)/shard_map/ppermute | solution.py:241
  35.4 26.7 %collective-permute-start.4 = (bf16[160,1024]{1,0:T(8,128)(2,1)S(1)}, bf16[160,1024]{1,0:T(8,128)(2,1)S(1)}, u32[]{:S(2)}, u32[]{:S(2)}) collective-permute-start(bf16[160,1024]{1,0:T(8,128)(2,1)S(1)} %get-tuple-element.26), channel_id=1, source_target_pairs={{4,0},{8,4},{12,8},{16,12},{20,16},{24,20},{28,24},{32,28},{36,32}... | collective-permute-start | bytes 983048 | tf_op jit(solution)/shard_map/ppermute | solution.py:229
  36.7 14.9 %collective-permute-start.3 = (bf16[152,1024]{1,0:T(8,128)(2,1)S(1)}, bf16[152,1024]{1,0:T(8,128)(2,1)S(1)}, u32[]{:S(2)}, u32[]{:S(2)}) collective-permute-start(bf16[152,1024]{1,0:T(8,128)(2,1)S(1)} %get-tuple-element.25), channel_id=1, source_target_pairs={{0,4},{4,8},{8,12},{12,16},{16,20},{20,24},{24,28},{28,32},{32,36}... | collective-permute-start | bytes 933896 | tf_op jit(solution)/shard_map/ppermute | solution.py:229
  44.2 27.6 %collective-permute-start.2 = (bf16[160,1024]{1,0:T(8,128)(2,1)S(1)}, bf16[160,1024]{1,0:T(8,128)(2,1)S(1)}, u32[]{:S(2)}, u32[]{:S(2)}) collective-permute-start(bf16[160,1024]{1,0:T(8,128)(2,1)S(1)} %get-tuple-element.24), channel_id=1, source_target_pairs={{4,0},{8,4},{12,8},{16,12},{20,16},{24,20},{28,24},{32,28},{36,32}... | collective-permute-start | bytes 983048 | tf_op jit(solution)/shard_map/ppermute | solution.py:229
  45.5 26.3 %collective-permute-start.1 = (bf16[152,1024]{1,0:T(8,128)(2,1)S(1)}, bf16[152,1024]{1,0:T(8,128)(2,1)S(1)}, u32[]{:S(2)}, u32[]{:S(2)}) collective-permute-start(bf16[152,1024]{1,0:T(8,128)(2,1)S(1)} %get-tuple-element.23), channel_id=1, source_target_pairs={{0,4},{4,8},{8,12},{12,16},{16,20},{20,24},{24,28},{28,32},{32,36}... | collective-permute-start | bytes 933896 | tf_op jit(solution)/shard_map/ppermute | solution.py:229
  81.5 17.2 %all-to-all-start.1 = ((f32[32,8,128]{2,1,0:T(8,128)}), f32[32,8,128]{2,1,0:T(8,128)S(1)}, u32[]{:S(2)}, u32[]{:S(2)}) async-start(f32[32,8,128]{2,1,0:T(8,128)} %get-tuple-element.34), calls=%async_computation.1 | async-start | bytes 262144 | tf_op jit(solution)/shard_map/all_to_all | solution.py:270

commit v7 on v6

--- a/solution.py
+++ b/solution.py
@@ -14,6 +14,7 @@
 KB = 128
 LANES = 128
 GPB = LANES // CPG
+STEP = 24
 HALO = 8
 CTX = ("x", "z", "yh")
 MP = ("yl", "core")
@@ -66,17 +67,20 @@
     uw = jnp.concatenate([early[:KB], kf * vf], 0)
     dw = jnp.concatenate([gate * qf, late[:KB]], 0)
 
-    part_rows = near // 2
-    span = part_rows + KB
+    span = STEP + KB
+    starts = range(0, near, STEP)
     blank = jnp.zeros((2 * KB - span, 2 * LANES), F32)
 
     def windows(x):
-        pair = jnp.concatenate([x[:span], x[part_rows : part_rows + span]], 1)
-        return jnp.concatenate([pair, blank], 0).astype(BF16)
+        pairs = [
+            jnp.concatenate([x[t : t + span], x[t + STEP : t + STEP + span]], 1)
+            for t in starts[::2]
+        ]
+        return [jnp.concatenate([pair, blank], 0).astype(BF16) for pair in pairs]
 
     u_win, d_win = windows(uw), windows(dw)
     own = jnp.concatenate([dw[:rows], jnp.zeros((8, LANES), F32)], 0)
-    own = jnp.concatenate([own[:part_rows], own[part_rows:]], 1)
+    own = jnp.concatenate([own[t : t + STEP] for t in starts], 1)
 
     at = lax.broadcasted_iota(jnp.int32, (LANES, LANES), 0)
     to = lax.broadcasted_iota(jnp.int32, (LANES, LANES), 1)
@@ -85,14 +89,14 @@
     turned = jnp.dot(both, flip, preferred_element_type=F32)
     lane = lax.broadcasted_iota(jnp.int32, (8, LANES), 1)
     row = lax.broadcasted_iota(jnp.int32, (8, LANES), 0)
-    groups = jnp.concatenate([lane_group((part_rows, LANES))] * 2, 1)
+    groups = jnp.concatenate([lane_group((STEP, LANES))] * len(starts), 1)
 
     def squares(lines, first):
         tiles = []
         for i in range(GPB):
             line = lines[i // 4 * 8 + i % 4 : i // 4 * 8 + i % 4 + 1]
             base = pltpu.roll(jnp.broadcast_to(line, (8, LANES)), first, 1, stride=1, stride_axis=0)
-            for a in range(part_rows // 8):
+            for a in range(STEP // 8):
                 tile = pltpu.roll(base, 8 * a, 1) if a else base
                 upper = lane > row + 8 * a if first else lane >= row + 8 * a
                 tiles.append(
@@ -101,27 +105,33 @@
         return jnp.concatenate(tiles, 0).astype(BF16)
 
     def filtered(matrices, window):
-        every = jnp.dot(matrices, window, preferred_element_type=F32)
-        out = every[:part_rows]
-        for i in range(1, GPB):
-            out = jnp.where(groups == i, every[part_rows * i : part_rows * (i + 1)], out)
-        return jnp.concatenate([out[:, :LANES], out[:, LANES:]], 0)
+        made = []
+        for pair in window:
+            every = jnp.dot(matrices, pair, preferred_element_type=F32)
+            out = every[:STEP]
+            for i in range(1, GPB):
+                out = jnp.where(groups[:, : 2 * LANES] == i, every[STEP * i : STEP * (i + 1)], out)
+            made += [out[:, :LANES], out[:, LANES:]]
+        return jnp.concatenate(made, 0)
 
     z = filtered(squares(turned, 1), u_win)
     du = filtered(squares(straight, 0), d_win)
 
     mine = jnp.concatenate([jnp.where(groups == i, own, 0.0) for i in range(GPB)], 0).astype(BF16)
-    prod = lax.dot_general(mine, u_win, (((1,), (1,)), ((), ())), preferred_element_type=F32)
-    medium = []
+    prod = lax.dot_general(
+        mine, jnp.concatenate(u_win, 1), (((1,), (1,)), ((), ())), preferred_element_type=F32
+    )
+    totals = []
     for i in range(GPB):
-        total = None
-        for a in range(part_rows // 8):
-            tile = prod[part_rows * i + 8 * a : part_rows * i + 8 * a + 8]
+        for a in range(STEP // 8):
+            tile = prod[STEP * i + 8 * a : STEP * i + 8 * a + 8]
             tile = jnp.where(lane > row + 8 * a, tile[:, :KB], tile[:, KB:])
             total = tile if a == 0 else total + pltpu.roll(tile, KB - 8 * a, 1)
-        medium.append(jnp.sum(align_left(total), 0, keepdims=True))
+        totals.append(total)
+    aligned = align_left(jnp.concatenate(totals, 0))
+    medium = jnp.sum(aligned.reshape(GPB, 8, LANES), 1)
     for half in range(2):
-        part[half, 0:4] = jnp.concatenate(medium[4 * half : 4 * half + 4], 0)
+        part[half, 0:4] = medium[4 * half : 4 * half + 4]
 
     feats[0] = (gate[:near] * z).astype(BF16).astype(F32)
     feats[1] = (du * vf).astype(BF16).astype(F32)

time: 117 us -> 114 us (0.974)
  Pallas kernels: 24.9 us -> 22.2 us
    pallas_call x2, Pallas kernels: 19.4 us -> 16.7 us  [fused(): pl.pallas_call(fused_kernel, grid=(count,), in_specs=[block(signals.shape...]
  transfers between devices with their start and end apart: 6 -> 6, of which waited for: 2 -> 2; matrix products, arithmetic and copies ran while one was open for 2% -> 2% of each run, Pallas kernels for 10% -> 9%
where the time goes in v7:
time: 114 us
  blocking collectives  39.8 us (35%)
  starting transfers between devices  26.1 us (23%)
  Pallas kernels  22.2 us (19%)
  waiting for transfers between devices  21.7 us (19%)
  local copies, waits for them, and re-layouts  2.3 us (2%)
    all_to_all x1, blocking collectives, shards(): lax.all_to_all(jnp.broadcast_to(own[None], (32, 8, LANES)), ('x', 'z'), 0...  24.1 us
    pallas_call x2, Pallas kernels, fused(): pl.pallas_call(fused_kernel, grid=(count,), in_specs=[block(signals.shape...  16.7 us
    all_to_all x1, blocking collectives, shards(): arrived = lax.all_to_all(spread, ('x',) + MP, 0, 0, tiled=True)  15.7 us
    ppermute x4, starting transfers between devices, step_ctx(): lax.ppermute(value, CTX, [(i, i + step) for i in range(count) if 0 <= i +...  14.2 us
    all_to_all x1, waiting for transfers between devices, shards(): parts = lax.all_to_all(part, ('z', 'yh'), 0, 0, tiled=True)  11.2 us
    ppermute x4, waiting for transfers between devices, step_ctx(): lax.ppermute(value, CTX, [(i, i + step) for i in range(count) if 0 <= i +...  10.5 us
    all_to_all x1, starting transfers between devices, shards(): parts = lax.all_to_all(part, ('z', 'yh'), 0, 0, tiled=True)  6.25 us
    ppermute x1, starting transfers between devices, turn(): return lax.ppermute(value, ALL, pairs)  5.6 us
  transfers between devices with their start and end apart: 6, of which 2 were waited for; matrix products, arithmetic and copies ran while one was open for 2% of the time, Pallas kernels for 9%

profile of v7, /device:TPU:1, one launch (start us, length us, event | category | flops | bytes accessed | tf_op | source)
XLA Modules:
  0.0 113.8 jit_solution(7331945925043553468)
XLA Ops:
  0.6 0.0 copy-start
  0.7 0.8 fusion.1
  1.4 5.6 %collective-permute-start = (bf16[8,128]{1,0:T(8,128)(2,1)S(1)}, bf16[8,128]{1,0:T(8,128)(2,1)S(1)}, u32[]{:S(2)}, u32[]{:S(2)}) collective-permute-start(bf16[8,128]{1,0:T(8,128)(2,1)S(1)} %fusion.1), channel_id=1, source_target_pairs={{0,0},{1,4},{2,8},{3,12},{4,128},{5,132},{6,136},{7,140},{8,256},{... | collective-permute-start | bytes 6152 | tf_op jit(solution)/shard_map/ppermute | solution.py:251
  7.1 1.1 constant_dynamic-update-slice_fusion.7
  8.2 1.1 constant_dynamic-update-slice_fusion.5
  9.4 0.0 collective-permute-done
  9.4 24.1 %all_to_all.15 = bf16[32,8,128]{2,1,0:T(8,128)(2,1)S(1)} all-to-all(bf16[32,8,128]{2,1,0:T(8,128)(2,1)S(1)} %broadcast_in_dim.5), channel_id=1, replica_groups=mesh['x'=4,'z'=8,'yh'=4,'yl'=2,'core'=2] {'x','z'}, dimensions={0} | all-to-all | bytes 131072 | tf_op jit(solution)/shard_map/all_to_all | solution.py:267
  33.5 1.9 %products.3 = (bf16[152,1024]{1,0:T(8,128)(2,1)S(1)}, bf16[160,1024]{1,0:T(8,128)(2,1)S(1)}) custom-call(bf16[576,2048]{1,0:T(8,128)(2,1)S(1)} %constant_dynamic-update-slice_fusion.q.k.v.g, bf16[576,2048]{1,0:T(8,128)(2,1)S(1)} %constant_dynamic-update-slice_fusion.q.k.v.g, bf16[576,2048]{1,0:T(8,128)(2,1)S(1)} %constant_dynamic-update-slice_fusion.q.k.v.g, ...), custom_call_target="tpu_custom_call" | custom-call | flops 20000000 | bytes 3000000 | tf_op jit(solution)/shard_map/products/pallas_call | solution.py:215
  35.4 1.3 %collective-permute-start.4 = (bf16[160,1024]{1,0:T(8,128)(2,1)S(1)}, bf16[160,1024]{1,0:T(8,128)(2,1)S(1)}, u32[]{:S(2)}, u32[]{:S(2)}) collective-permute-start(bf16[160,1024]{1,0:T(8,128)(2,1)S(1)} %get-tuple-element.26), channel_id=1, source_target_pairs={{4,0},{8,4},{12,8},{16,12},{20,16},{24,20},{28,24},{32,28},{36,32}... | collective-permute-start | bytes 983048 | tf_op jit(solution)/shard_map/ppermute | solution.py:239
  36.7 5.5 %collective-permute-start.3 = (bf16[152,1024]{1,0:T(8,128)(2,1)S(1)}, bf16[152,1024]{1,0:T(8,128)(2,1)S(1)}, u32[]{:S(2)}, u32[]{:S(2)}) collective-permute-start(bf16[152,1024]{1,0:T(8,128)(2,1)S(1)} %get-tuple-element.25), channel_id=1, source_target_pairs={{0,4},{4,8},{8,12},{12,16},{16,20},{20,24},{24,28},{28,32},{32,36}... | collective-permute-start | bytes 933896 | tf_op jit(solution)/shard_map/ppermute | solution.py:239
  42.3 1.9 %products.2 = (bf16[152,1024]{1,0:T(8,128)(2,1)S(1)}, bf16[160,1024]{1,0:T(8,128)(2,1)S(1)}) custom-call(bf16[576,2048]{1,0:T(8,128)(2,1)S(1)} %constant_dynamic-update-slice_fusion.q.k.v.g, bf16[576,2048]{1,0:T(8,128)(2,1)S(1)} %constant_dynamic-update-slice_fusion.q.k.v.g, bf16[576,2048]{1,0:T(8,128)(2,1)S(1)} %constant_dynamic-update-slice_fusion.q.k.v.g, ...), custom_call_target="tpu_custom_call" | custom-call | flops 20000000 | bytes 3000000 | tf_op jit(solution)/shard_map/products/pallas_call | solution.py:215
  44.2 1.3 %collective-permute-start.2 = (bf16[160,1024]{1,0:T(8,128)(2,1)S(1)}, bf16[160,1024]{1,0:T(8,128)(2,1)S(1)}, u32[]{:S(2)}, u32[]{:S(2)}) collective-permute-start(bf16[160,1024]{1,0:T(8,128)(2,1)S(1)} %get-tuple-element.24), channel_id=1, source_target_pairs={{4,0},{8,4},{12,8},{16,12},{20,16},{24,20},{28,24},{32,28},{36,32}... | collective-permute-start | bytes 983048 | tf_op jit(solution)/shard_map/ppermute | solution.py:239
  45.5 6.1 %collective-permute-start.1 = (bf16[152,1024]{1,0:T(8,128)(2,1)S(1)}, bf16[152,1024]{1,0:T(8,128)(2,1)S(1)}, u32[]{:S(2)}, u32[]{:S(2)}) collective-permute-start(bf16[152,1024]{1,0:T(8,128)(2,1)S(1)} %get-tuple-element.23), channel_id=1, source_target_pairs={{0,4},{4,8},{8,12},{12,16},{16,20},{20,24},{24,28},{28,32},{32,36}... | collective-permute-start | bytes 933896 | tf_op jit(solution)/shard_map/ppermute | solution.py:239
  51.6 0.0 collective-permute-done.3.below
  51.6 10.5 %collective-permute-done.4.above = bf16[160,1024]{1,0:T(8,128)(2,1)S(1)} collective-permute-done((bf16[160,1024]{1,0:T(8,128)(2,1)S(1)}, bf16[160,1024]{1,0:T(8,128)(2,1)S(1)}, u32[]{:S(2)}, u32[]{:S(2)}) %collective-permute-start.4) | collective-permute-done | bytes 327712 | tf_op jit(solution)/shard_map/ppermute | solution.py:239
  62.1 8.3 %fused.2 = (bf16[136,2048]{1,0:T(8,128)(2,1)}, bf16[136,2048]{1,0:T(8,128)(2,1)}, bf16[136,2048]{1,0:T(8,128)(2,1)}, f32[32,8,128]{2,1,0:T(8,128)}) custom-call(bf16[576,2048]{1,0:T(8,128)(2,1)S(1)} %constant_dynamic-update-slice_fusion.q.k.v.g, bf16[576,2048]{1,0:T(8,128)(2,1)S(1)} %constant_dynamic-update-slice_fusion.q.k.v.g, ...), custom_call_target="tpu_custom_call" | custom-call | flops 2000000000 | bytes 4000000 | tf_op jit(solution)/shard_map/fused/pallas_call | solution.py:162
  70.4 0.0 collective-permute-done.1.below
  70.4 0.0 collective-permute-done.2.above
  70.4 8.4 %fused.3 = (bf16[136,2048]{1,0:T(8,128)(2,1)}, bf16[136,2048]{1,0:T(8,128)(2,1)}, bf16[136,2048]{1,0:T(8,128)(2,1)}, f32[32,8,128]{2,1,0:T(8,128)}) custom-call(bf16[576,2048]{1,0:T(8,128)(2,1)S(1)} %constant_dynamic-update-slice_fusion.q.k.v.g, ...), custom_call_target="tpu_custom_call", output_to_operand_aliasing={{0}: (7, {}), {1}: (8, {}), {2}: (9, {}), {3}: (10, {})} | custom-call | flops 2000000000 | bytes 4000000 | tf_op jit(solution)/shard_map/fused/pallas_call | solution.py:162
  78.8 6.3 %all-to-all-start.1 = ((f32[32,8,128]{2,1,0:T(8,128)}), f32[32,8,128]{2,1,0:T(8,128)S(1)}, u32[]{:S(2)}, u32[]{:S(2)}) async-start(f32[32,8,128]{2,1,0:T(8,128)} %get-tuple-element.34), calls=%async_computation.1 | async-start | bytes 262144 | tf_op jit(solution)/shard_map/all_to_all | solution.py:280
  85.1 11.2 %all-to-all-done.1 = f32[32,8,128]{2,1,0:T(8,128)S(1)} async-done(((f32[32,8,128]{2,1,0:T(8,128)}), f32[32,8,128]{2,1,0:T(8,128)S(1)}, u32[]{:S(2)}, u32[]{:S(2)}) %all-to-all-start.1) | async-done | bytes 131104 | tf_op jit(solution)/shard_map/all_to_all | solution.py:280
  96.3 0.1 broadcast_multiply_fusion
  96.4 15.7 %all_to_all.16.arrived = f32[16,8,128]{2,1,0:T(8,128)} all-to-all(f32[16,8,128]{2,1,0:T(8,128)S(1)} %broadcast_multiply_fusion), channel_id=1, replica_groups=mesh['x'=4,'z'=8,'yh'=4,'yl'=2,'core'=2] {'x','yl','core'}, dimensions={0} | all-to-all | bytes 131072 | tf_op jit(solution)/shard_map/all_to_all | solution.py:283
  112.1 1.7 %finish.1 = (f32[4,7]{1,0:T(4,128)}, f32[4,128]{1,0:T(4,128)}) custom-call(f32[16,8,128]{2,1,0:T(8,128)} %all_to_all.16.arrived), custom_call_target="tpu_custom_call" | custom-call | tf_op jit(solution)/shard_map/finish/pallas_call | solution.py:310
  (12 shorter events, 0.2 us)
Async XLA Ops:
  0.6 8.6 %copy-start = (bf16[136,2048]{1,0:T(8,128)(2,1)S(1)}, bf16[136,2048]{1,0:T(8,128)(2,1)}, u32[]{:S(2)}) copy-start(bf16[136,2048]{1,0:T(8,128)(2,1)} %param.8) | copy-start | bytes 1671172
  0.6 8.7 %copy-start.1 = (bf16[136,2048]{1,0:T(8,128)(2,1)S(1)}, bf16[136,2048]{1,0:T(8,128)(2,1)}, u32[]{:S(2)}) copy-start(bf16[136,2048]{1,0:T(8,128)(2,1)} %param.9) | copy-start | bytes 1671172
  1.4 8.0 %collective-permute-start = (bf16[8,128]{1,0:T(8,128)(2,1)S(1)}, bf16[8,128]{1,0:T(8,128)(2,1)S(1)}, u32[]{:S(2)}, u32[]{:S(2)}) collective-permute-start(bf16[8,128]{1,0:T(8,128)(2,1)S(1)} %fusion.1), channel_id=1, source_target_pairs={{0,0},{1,4},{2,8},{3,12},{4,128},{5,132},{6,136},{7,140},{8,256},{... | collective-permute-start | bytes 6152 | tf_op jit(solution)/shard_map/ppermute | solution.py:251
  35.4 26.7 %collective-permute-start.4 = (bf16[160,1024]{1,0:T(8,128)(2,1)S(1)}, bf16[160,1024]{1,0:T(8,128)(2,1)S(1)}, u32[]{:S(2)}, u32[]{:S(2)}) collective-permute-start(bf16[160,1024]{1,0:T(8,128)(2,1)S(1)} %get-tuple-element.26), channel_id=1, source_target_pairs={{4,0},{8,4},{12,8},{16,12},{20,16},{24,20},{28,24},{32,28},{36,32}... | collective-permute-start | bytes 983048 | tf_op jit(solution)/shard_map/ppermute | solution.py:239
  36.7 14.9 %collective-permute-start.3 = (bf16[152,1024]{1,0:T(8,128)(2,1)S(1)}, bf16[152,1024]{1,0:T(8,128)(2,1)S(1)}, u32[]{:S(2)}, u32[]{:S(2)}) collective-permute-start(bf16[152,1024]{1,0:T(8,128)(2,1)S(1)} %get-tuple-element.25), channel_id=1, source_target_pairs={{0,4},{4,8},{8,12},{12,16},{16,20},{20,24},{24,28},{28,32},{32,36}... | collective-permute-start | bytes 933896 | tf_op jit(solution)/shard_map/ppermute | solution.py:239
  44.2 26.2 %collective-permute-start.2 = (bf16[160,1024]{1,0:T(8,128)(2,1)S(1)}, bf16[160,1024]{1,0:T(8,128)(2,1)S(1)}, u32[]{:S(2)}, u32[]{:S(2)}) collective-permute-start(bf16[160,1024]{1,0:T(8,128)(2,1)S(1)} %get-tuple-element.24), channel_id=1, source_target_pairs={{4,0},{8,4},{12,8},{16,12},{20,16},{24,20},{28,24},{32,28},{36,32}... | collective-permute-start | bytes 983048 | tf_op jit(solution)/shard_map/ppermute | solution.py:239
  45.5 24.9 %collective-permute-start.1 = (bf16[152,1024]{1,0:T(8,128)(2,1)S(1)}, bf16[152,1024]{1,0:T(8,128)(2,1)S(1)}, u32[]{:S(2)}, u32[]{:S(2)}) collective-permute-start(bf16[152,1024]{1,0:T(8,128)(2,1)S(1)} %get-tuple-element.23), channel_id=1, source_target_pairs={{0,4},{4,8},{8,12},{12,16},{16,20},{20,24},{24,28},{28,32},{32,36}... | collective-permute-start | bytes 933896 | tf_op jit(solution)/shard_map/ppermute | solution.py:239
  78.8 17.5 %all-to-all-start.1 = ((f32[32,8,128]{2,1,0:T(8,128)}), f32[32,8,128]{2,1,0:T(8,128)S(1)}, u32[]{:S(2)}, u32[]{:S(2)}) async-start(f32[32,8,128]{2,1,0:T(8,128)} %get-tuple-element.34), calls=%async_computation.1 | async-start | bytes 262144 | tf_op jit(solution)/shard_map/all_to_all | solution.py:280

commit v8 on v7

--- a/solution.py
+++ b/solution.py
@@ -20,7 +20,7 @@
 MP = ("yl", "core")
 ALL = CTX + MP
 SIZES = (4, 8, 4, 4)
-WIDE = 2 * LANES
+WIDE = 4 * LANES
 VMEM = 12 * 1024 * 1024
 
 
@@ -53,7 +53,7 @@
 def one_block(q, k, v, g, below, above, taps, b, gq, gk, gv, part, qs, ks, vs, feats):
     rows = gq.shape[0]
     near = rows + 8
-    both = taps[2 * b : 2 * b + 2].reshape(16, LANES)
+    both = taps[2 * (b % 2) : 2 * (b % 2) + 2, b // 2].reshape(16, LANES)
     h = short_taps(both)
     early, late = below[...].astype(F32), above[...].astype(F32)
     made = []
@@ -117,7 +117,8 @@
     z = filtered(squares(turned, 1), u_win)
     du = filtered(squares(straight, 0), d_win)
 
-    mine = jnp.concatenate([jnp.where(groups == i, own, 0.0) for i in range(GPB)], 0).astype(BF16)
+    own = own.astype(BF16)
+    mine = jnp.concatenate([jnp.where(groups == i, own, 0) for i in range(GPB)], 0)
     prod = lax.dot_general(
         mine, jnp.concatenate(u_win, 1), (((1,), (1,)), ((), ())), preferred_element_type=F32
     )
@@ -158,13 +159,13 @@
     channels = signals.shape[1]
     block = lambda r, n=0: pl.BlockSpec((r, WIDE), lambda i: (n, first + i))
     sent = lambda r: pl.BlockSpec((r, WIDE), lambda i: (0, i))
-    chunk = pl.BlockSpec((4, 1, 8, LANES), lambda i: (0, first + i, 0, 0))
+    chunk = pl.BlockSpec((4, WIDE // LANES // 2, 8, LANES), lambda i: (0, first + i, 0, 0))
     return pl.pallas_call(
         fused_kernel,
         grid=(count,),
         in_specs=[block(signals.shape[0] // 4, n) for n in range(4)] + [sent(KB + 24), sent(KB + 32), chunk]
         + [pl.BlockSpec(memory_space=pl.ANY)] * len(written),
-        out_specs=[block(rows)] * 3 + [pl.BlockSpec((4, 8, LANES), lambda i: (first + i, 0, 0))],
+        out_specs=[block(rows)] * 3 + [pl.BlockSpec((WIDE // LANES * 2, 8, LANES), lambda i: (first + i, 0, 0))],
         out_shape=[jax.ShapeDtypeStruct((rows, channels), BF16)] * 3
         + [jax.ShapeDtypeStruct((channels // LANES * 2, 8, LANES), F32)],
         scratch_shapes=[pltpu.VMEM((WIDE // LANES, rows + 16, LANES), F32)] * 3
@@ -190,7 +191,7 @@
     for b in range(WIDE // LANES):
         lanes = slice(b * LANES, (b + 1) * LANES)
         one_product(
-            *(x.at[:, lanes] for x in (q, k, v, g)), taps[2 * b : 2 * b + 2],
+            *(x.at[:, lanes] for x in (q, k, v, g)), taps[2 * (b % 2) : 2 * (b % 2) + 2, b // 2],
             lower.at[:, lanes], upper.at[:, lanes], qs.at[b], ks.at[b], vs.at[b],
         )
 
@@ -210,7 +211,7 @@
 def products(signals, rows, taps, first, count, interpret=False):
     assert rows == KB + 8
     block = lambda n: pl.BlockSpec((signals.shape[0] // 4, WIDE), lambda i: (n, first + i))
-    chunk = pl.BlockSpec((4, 1, 8, LANES), lambda i: (0, first + i, 0, 0))
+    chunk = pl.BlockSpec((4, WIDE // LANES // 2, 8, LANES), lambda i: (0, first + i, 0, 0))
     out = lambda r: pl.BlockSpec((r, WIDE), lambda i: (0, i))
     return pl.pallas_call(
         products_kernel,

time: 114 us -> 112 us (0.982)
  Pallas kernels: 22.2 us -> 18.6 us
  starting transfers between devices: 26.1 us -> 27.4 us
    pallas_call x2, Pallas kernels: 16.7 us -> 14 us  [fused(): pl.pallas_call(fused_kernel, grid=(count,), in_specs=[block(signals.shape...]
    all_to_all x1, starting transfers between devices: 6.25 us -> 7.55 us  [shards(): parts = lax.all_to_all(part, ('z', 'yh'), 0, 0, tiled=True)]
  transfers between devices with their start and end apart: 6 -> 6, of which waited for: 2 -> 2; matrix products, arithmetic and copies ran while one was open for 2% -> 2% of each run, Pallas kernels for 9% -> 8%
where the time goes in v8:
time: 112 us
  blocking collectives  39.4 us (35%)
  starting transfers between devices  27.4 us (24%)
  waiting for transfers between devices  22.2 us (20%)
  Pallas kernels  18.6 us (17%)
  local copies, waits for them, and re-layouts  2.3 us (2%)
    all_to_all x1, blocking collectives, shards(): lax.all_to_all(jnp.broadcast_to(own[None], (32, 8, LANES)), ('x', 'z'), 0...  24.1 us
    all_to_all x1, blocking collectives, shards(): arrived = lax.all_to_all(spread, ('x',) + MP, 0, 0, tiled=True)  15.3 us
    ppermute x4, starting transfers between devices, step_ctx(): lax.ppermute(value, CTX, [(i, i + step) for i in range(count) if 0 <= i +...  14.2 us
    pallas_call x2, Pallas kernels, fused(): pl.pallas_call(fused_kernel, grid=(count,), in_specs=[block(signals.shape...  14 us
    all_to_all x1, waiting for transfers between devices, shards(): parts = lax.all_to_all(part, ('z', 'yh'), 0, 0, tiled=True)  11.2 us
    ppermute x4, waiting for transfers between devices, step_ctx(): lax.ppermute(value, CTX, [(i, i + step) for i in range(count) if 0 <= i +...  11 us
    all_to_all x1, starting transfers between devices, shards(): parts = lax.all_to_all(part, ('z', 'yh'), 0, 0, tiled=True)  7.55 us
    ppermute x1, starting transfers between devices, turn(): return lax.ppermute(value, ALL, pairs)  5.6 us
  transfers between devices with their start and end apart: 6, of which 2 were waited for; matrix products, arithmetic and copies ran while one was open for 2% of the time, Pallas kernels for 8%

profile of v8, /device:TPU:1, one launch (start us, length us, event | category | flops | bytes accessed | tf_op | source)
XLA Modules:
  0.0 111.5 jit_solution(8828044856775262787)
XLA Ops:
  0.7 0.8 fusion.1
  1.4 5.6 %collective-permute-start = (bf16[8,128]{1,0:T(8,128)(2,1)S(1)}, bf16[8,128]{1,0:T(8,128)(2,1)S(1)}, u32[]{:S(2)}, u32[]{:S(2)}) collective-permute-start(bf16[8,128]{1,0:T(8,128)(2,1)S(1)} %fusion.1), channel_id=1, source_target_pairs={{0,0},{1,4},{2,8},{3,12},{4,128},{5,132},{6,136},{7,140},{8,256},{... | collective-permute-start | bytes 6152 | tf_op jit(solution)/shard_map/ppermute | solution.py:252
  7.1 1.1 constant_dynamic-update-slice_fusion.7
  8.2 1.1 constant_dynamic-update-slice_fusion.5
  9.3 0.0 copy-done
  9.4 0.0 collective-permute-done
  9.4 24.1 %all_to_all.15 = bf16[32,8,128]{2,1,0:T(8,128)(2,1)S(1)} all-to-all(bf16[32,8,128]{2,1,0:T(8,128)(2,1)S(1)} %broadcast_in_dim.5), channel_id=1, replica_groups=mesh['x'=4,'z'=8,'yh'=4,'yl'=2,'core'=2] {'x','z'}, dimensions={0} | all-to-all | bytes 131072 | tf_op jit(solution)/shard_map/all_to_all | solution.py:268
  33.5 1.4 %products.3 = (bf16[152,1024]{1,0:T(8,128)(2,1)S(1)}, bf16[160,1024]{1,0:T(8,128)(2,1)S(1)}) custom-call(bf16[576,2048]{1,0:T(8,128)(2,1)S(1)} %constant_dynamic-update-slice_fusion.q.k.v.g, bf16[576,2048]{1,0:T(8,128)(2,1)S(1)} %constant_dynamic-update-slice_fusion.q.k.v.g, bf16[576,2048]{1,0:T(8,128)(2,1)S(1)} %constant_dynamic-update-slice_fusion.q.k.v.g, ...), custom_call_target="tpu_custom_call" | custom-call | flops 20000000 | bytes 3000000 | tf_op jit(solution)/shard_map/products/pallas_call | solution.py:216
  34.9 1.3 %collective-permute-start.4 = (bf16[160,1024]{1,0:T(8,128)(2,1)S(1)}, bf16[160,1024]{1,0:T(8,128)(2,1)S(1)}, u32[]{:S(2)}, u32[]{:S(2)}) collective-permute-start(bf16[160,1024]{1,0:T(8,128)(2,1)S(1)} %get-tuple-element.26), channel_id=1, source_target_pairs={{4,0},{8,4},{12,8},{16,12},{20,16},{24,20},{28,24},{32,28},{36,32}... | collective-permute-start | bytes 983048 | tf_op jit(solution)/shard_map/ppermute | solution.py:240
  36.2 5.5 %collective-permute-start.3 = (bf16[152,1024]{1,0:T(8,128)(2,1)S(1)}, bf16[152,1024]{1,0:T(8,128)(2,1)S(1)}, u32[]{:S(2)}, u32[]{:S(2)}) collective-permute-start(bf16[152,1024]{1,0:T(8,128)(2,1)S(1)} %get-tuple-element.25), channel_id=1, source_target_pairs={{0,4},{4,8},{8,12},{12,16},{16,20},{20,24},{24,28},{28,32},{32,36}... | collective-permute-start | bytes 933896 | tf_op jit(solution)/shard_map/ppermute | solution.py:240
  41.8 1.4 %products.2 = (bf16[152,1024]{1,0:T(8,128)(2,1)S(1)}, bf16[160,1024]{1,0:T(8,128)(2,1)S(1)}) custom-call(bf16[576,2048]{1,0:T(8,128)(2,1)S(1)} %constant_dynamic-update-slice_fusion.q.k.v.g, bf16[576,2048]{1,0:T(8,128)(2,1)S(1)} %constant_dynamic-update-slice_fusion.q.k.v.g, bf16[576,2048]{1,0:T(8,128)(2,1)S(1)} %constant_dynamic-update-slice_fusion.q.k.v.g, ...), custom_call_target="tpu_custom_call" | custom-call | flops 20000000 | bytes 3000000 | tf_op jit(solution)/shard_map/products/pallas_call | solution.py:216
  43.2 1.3 %collective-permute-start.2 = (bf16[160,1024]{1,0:T(8,128)(2,1)S(1)}, bf16[160,1024]{1,0:T(8,128)(2,1)S(1)}, u32[]{:S(2)}, u32[]{:S(2)}) collective-permute-start(bf16[160,1024]{1,0:T(8,128)(2,1)S(1)} %get-tuple-element.24), channel_id=1, source_target_pairs={{4,0},{8,4},{12,8},{16,12},{20,16},{24,20},{28,24},{32,28},{36,32}... | collective-permute-start | bytes 983048 | tf_op jit(solution)/shard_map/ppermute | solution.py:240
  44.5 6.1 %collective-permute-start.1 = (bf16[152,1024]{1,0:T(8,128)(2,1)S(1)}, bf16[152,1024]{1,0:T(8,128)(2,1)S(1)}, u32[]{:S(2)}, u32[]{:S(2)}) collective-permute-start(bf16[152,1024]{1,0:T(8,128)(2,1)S(1)} %get-tuple-element.23), channel_id=1, source_target_pairs={{0,4},{4,8},{8,12},{12,16},{16,20},{20,24},{24,28},{28,32},{32,36}... | collective-permute-start | bytes 933896 | tf_op jit(solution)/shard_map/ppermute | solution.py:240
  50.6 0.0 collective-permute-done.3.below
  50.6 11.0 %collective-permute-done.4.above = bf16[160,1024]{1,0:T(8,128)(2,1)S(1)} collective-permute-done((bf16[160,1024]{1,0:T(8,128)(2,1)S(1)}, bf16[160,1024]{1,0:T(8,128)(2,1)S(1)}, u32[]{:S(2)}, u32[]{:S(2)}) %collective-permute-start.4) | collective-permute-done | bytes 327712 | tf_op jit(solution)/shard_map/ppermute | solution.py:240
  61.6 7.0 %fused.2 = (bf16[136,2048]{1,0:T(8,128)(2,1)}, bf16[136,2048]{1,0:T(8,128)(2,1)}, bf16[136,2048]{1,0:T(8,128)(2,1)}, f32[32,8,128]{2,1,0:T(8,128)}) custom-call(bf16[576,2048]{1,0:T(8,128)(2,1)S(1)} %constant_dynamic-update-slice_fusion.q.k.v.g, bf16[576,2048]{1,0:T(8,128)(2,1)S(1)} %constant_dynamic-update-slice_fusion.q.k.v.g, ...), custom_call_target="tpu_custom_call" | custom-call | flops 1000000000 | bytes 2000000 | tf_op jit(solution)/shard_map/fused/pallas_call | solution.py:163
  68.6 0.0 collective-permute-done.1.below
  68.6 0.0 collective-permute-done.2.above
  68.6 7.0 %fused.3 = (bf16[136,2048]{1,0:T(8,128)(2,1)}, bf16[136,2048]{1,0:T(8,128)(2,1)}, bf16[136,2048]{1,0:T(8,128)(2,1)}, f32[32,8,128]{2,1,0:T(8,128)}) custom-call(bf16[576,2048]{1,0:T(8,128)(2,1)S(1)} %constant_dynamic-update-slice_fusion.q.k.v.g, ...), custom_call_target="tpu_custom_call", output_to_operand_aliasing={{0}: (7, {}), {1}: (8, {}), {2}: (9, {}), {3}: (10, {})} | custom-call | flops 1000000000 | bytes 2000000 | tf_op jit(solution)/shard_map/fused/pallas_call | solution.py:163
  75.7 7.6 %all-to-all-start.1 = ((f32[32,8,128]{2,1,0:T(8,128)}), f32[32,8,128]{2,1,0:T(8,128)S(1)}, u32[]{:S(2)}, u32[]{:S(2)}) async-start(f32[32,8,128]{2,1,0:T(8,128)} %get-tuple-element.34), calls=%async_computation.1 | async-start | bytes 262144 | tf_op jit(solution)/shard_map/all_to_all | solution.py:281
  83.2 11.2 %all-to-all-done.1 = f32[32,8,128]{2,1,0:T(8,128)S(1)} async-done(((f32[32,8,128]{2,1,0:T(8,128)}), f32[32,8,128]{2,1,0:T(8,128)S(1)}, u32[]{:S(2)}, u32[]{:S(2)}) %all-to-all-start.1) | async-done | bytes 131104 | tf_op jit(solution)/shard_map/all_to_all | solution.py:281
  94.5 0.1 broadcast_multiply_fusion
  94.6 15.3 %all_to_all.16.arrived = f32[16,8,128]{2,1,0:T(8,128)} all-to-all(f32[16,8,128]{2,1,0:T(8,128)S(1)} %broadcast_multiply_fusion), channel_id=1, replica_groups=mesh['x'=4,'z'=8,'yh'=4,'yl'=2,'core'=2] {'x','yl','core'}, dimensions={0} | all-to-all | bytes 131072 | tf_op jit(solution)/shard_map/all_to_all | solution.py:284
  109.8 1.7 %finish.1 = (f32[4,7]{1,0:T(4,128)}, f32[4,128]{1,0:T(4,128)}) custom-call(f32[16,8,128]{2,1,0:T(8,128)} %all_to_all.16.arrived), custom_call_target="tpu_custom_call" | custom-call | tf_op jit(solution)/shard_map/finish/pallas_call | solution.py:311
  (12 shorter events, 0.2 us)
Async XLA Ops:
  0.6 8.6 %copy-start = (bf16[136,2048]{1,0:T(8,128)(2,1)S(1)}, bf16[136,2048]{1,0:T(8,128)(2,1)}, u32[]{:S(2)}) copy-start(bf16[136,2048]{1,0:T(8,128)(2,1)} %param.8) | copy-start | bytes 1671172
  0.6 8.7 %copy-start.1 = (bf16[136,2048]{1,0:T(8,128)(2,1)S(1)}, bf16[136,2048]{1,0:T(8,128)(2,1)}, u32[]{:S(2)}) copy-start(bf16[136,2048]{1,0:T(8,128)(2,1)} %param.9) | copy-start | bytes 1671172
  1.4 8.0 %collective-permute-start = (bf16[8,128]{1,0:T(8,128)(2,1)S(1)}, bf16[8,128]{1,0:T(8,128)(2,1)S(1)}, u32[]{:S(2)}, u32[]{:S(2)}) collective-permute-start(bf16[8,128]{1,0:T(8,128)(2,1)S(1)} %fusion.1), channel_id=1, source_target_pairs={{0,0},{1,4},{2,8},{3,12},{4,128},{5,132},{6,136},{7,140},{8,256},{... | collective-permute-start | bytes 6152 | tf_op jit(solution)/shard_map/ppermute | solution.py:252
  34.9 26.7 %collective-permute-start.4 = (bf16[160,1024]{1,0:T(8,128)(2,1)S(1)}, bf16[160,1024]{1,0:T(8,128)(2,1)S(1)}, u32[]{:S(2)}, u32[]{:S(2)}) collective-permute-start(bf16[160,1024]{1,0:T(8,128)(2,1)S(1)} %get-tuple-element.26), channel_id=1, source_target_pairs={{4,0},{8,4},{12,8},{16,12},{20,16},{24,20},{28,24},{32,28},{36,32}... | collective-permute-start | bytes 983048 | tf_op jit(solution)/shard_map/ppermute | solution.py:240
  36.2 14.4 %collective-permute-start.3 = (bf16[152,1024]{1,0:T(8,128)(2,1)S(1)}, bf16[152,1024]{1,0:T(8,128)(2,1)S(1)}, u32[]{:S(2)}, u32[]{:S(2)}) collective-permute-start(bf16[152,1024]{1,0:T(8,128)(2,1)S(1)} %get-tuple-element.25), channel_id=1, source_target_pairs={{0,4},{4,8},{8,12},{12,16},{16,20},{20,24},{24,28},{28,32},{32,36}... | collective-permute-start | bytes 933896 | tf_op jit(solution)/shard_map/ppermute | solution.py:240
  43.2 25.4 %collective-permute-start.2 = (bf16[160,1024]{1,0:T(8,128)(2,1)S(1)}, bf16[160,1024]{1,0:T(8,128)(2,1)S(1)}, u32[]{:S(2)}, u32[]{:S(2)}) collective-permute-start(bf16[160,1024]{1,0:T(8,128)(2,1)S(1)} %get-tuple-element.24), channel_id=1, source_target_pairs={{4,0},{8,4},{12,8},{16,12},{20,16},{24,20},{28,24},{32,28},{36,32}... | collective-permute-start | bytes 983048 | tf_op jit(solution)/shard_map/ppermute | solution.py:240
  44.5 24.1 %collective-permute-start.1 = (bf16[152,1024]{1,0:T(8,128)(2,1)S(1)}, bf16[152,1024]{1,0:T(8,128)(2,1)S(1)}, u32[]{:S(2)}, u32[]{:S(2)}) collective-permute-start(bf16[152,1024]{1,0:T(8,128)(2,1)S(1)} %get-tuple-element.23), channel_id=1, source_target_pairs={{0,4},{4,8},{8,12},{12,16},{16,20},{20,24},{24,28},{28,32},{32,36}... | collective-permute-start | bytes 933896 | tf_op jit(solution)/shard_map/ppermute | solution.py:240
  75.7 18.8 %all-to-all-start.1 = ((f32[32,8,128]{2,1,0:T(8,128)}), f32[32,8,128]{2,1,0:T(8,128)S(1)}, u32[]{:S(2)}, u32[]{:S(2)}) async-start(f32[32,8,128]{2,1,0:T(8,128)} %get-tuple-element.34), calls=%async_computation.1 | async-start | bytes 262144 | tf_op jit(solution)/shard_map/all_to_all | solution.py:281

commit v9 on v8

--- a/solution.py
+++ b/solution.py
@@ -131,8 +131,8 @@
         totals.append(total)
     aligned = align_left(jnp.concatenate(totals, 0))
     medium = jnp.sum(aligned.reshape(GPB, 8, LANES), 1)
-    for half in range(2):
-        part[half, 0:4] = medium[4 * half : 4 * half + 4]
+    for i in range(GPB):
+        part[i // 4, :, LANES * (i % 4) : LANES * (i % 4 + 1)] = medium[i : i + 1]
 
     feats[0] = (gate[:near] * z).astype(BF16).astype(F32)
     feats[1] = (du * vf).astype(BF16).astype(F32)
@@ -149,10 +149,12 @@
             total = total + h[j : j + 1] * feats[i, j : j + rows]
         out[...] = total.astype(BF16)
     short = jnp.concatenate([jnp.sum(x, 0, keepdims=True) for x in sums], 0)
-    swapped = pltpu.roll(short, LANES // 2, 1)
-    left = lane[:4] < LANES // 2
-    part[0, 4:8] = jnp.where(left, short[:4], swapped[4:])
-    part[1, 4:8] = jnp.where(left, swapped[:4], short[4:])
+    for step in (8, 4, 2, 1):
+        short = short + pltpu.roll(short, LANES - step, 1)
+    short = pltpu.roll(short, 0, 1, stride=1, stride_axis=0)
+    line = jnp.sum(jnp.where(lane % CPG == row, short, 0.0), 0, keepdims=True)
+    part[0, :, 4 * LANES :] = line
+    part[1, :, 4 * LANES :] = pltpu.roll(line, LANES // 2, 1)
 
 
 def fused(signals, rows, below, above, taps, first, count, written=(), interpret=False):
@@ -165,9 +167,9 @@
         grid=(count,),
         in_specs=[block(signals.shape[0] // 4, n) for n in range(4)] + [sent(KB + 24), sent(KB + 32), chunk]
         + [pl.BlockSpec(memory_space=pl.ANY)] * len(written),
-        out_specs=[block(rows)] * 3 + [pl.BlockSpec((WIDE // LANES * 2, 8, LANES), lambda i: (first + i, 0, 0))],
+        out_specs=[block(rows)] * 3 + [pl.BlockSpec((WIDE // LANES * 2, 1, 5 * LANES), lambda i: (first + i, 0, 0))],
         out_shape=[jax.ShapeDtypeStruct((rows, channels), BF16)] * 3
-        + [jax.ShapeDtypeStruct((channels // LANES * 2, 8, LANES), F32)],
+        + [jax.ShapeDtypeStruct((channels // LANES * 2, 1, 5 * LANES), F32)],
         scratch_shapes=[pltpu.VMEM((WIDE // LANES, rows + 16, LANES), F32)] * 3
         + [pltpu.VMEM((WIDE // LANES, 3, rows + 8, LANES), F32)],
         input_output_aliases={7 + n: n for n in range(len(written))},
@@ -288,23 +290,19 @@
 
 def finish_kernel(arrived, short, medium):
     total = jnp.sum(arrived[...], 0)
+    rows = jnp.concatenate([total[:, LANES * i : LANES * (i + 1)] for i in range(4)], 0)
     at = lax.broadcasted_iota(jnp.int32, (LANES, LANES), 0)
     to = lax.broadcasted_iota(jnp.int32, (LANES, LANES), 1)
     medium[...] = jnp.dot(
-        total[0:4], ((at + to) % LANES == 0).astype(F32), precision=lax.Precision.HIGHEST,
+        rows, ((at + to) % LANES == 0).astype(F32), precision=lax.Precision.HIGHEST,
         preferred_element_type=F32,
     )
     group = lax.broadcasted_iota(jnp.int32, (4, LANES), 0)
-    halves = []
-    for half in range(2):
-        spread = (lane_group((4, LANES)) == group + 4 * half).astype(F32)
-        halves.append(
-            lax.dot_general(
-                spread, total[4:8], (((1,), (1,)), ((), ())), precision=lax.Precision.HIGHEST,
-                preferred_element_type=F32,
-            )
-        )
-    short[...] = jnp.concatenate(halves, 1)[:, :KS]
+    line = jnp.broadcast_to(total[:, 4 * LANES :], (4, LANES))
+    short[...] = jnp.dot(
+        jnp.where(lane_group((4, LANES)) == group, line, 0.0), (at % CPG == to).astype(F32),
+        precision=lax.Precision.HIGHEST, preferred_element_type=F32,
+    )[:, :KS]
 
 
 def finish(total, interpret=False):

time: 112 us -> 113 us (level)
  no operation moved by 1% of the time
where the time goes in v9:
time: 113 us; the launch traced here: 112 us
  blocking collectives  39.7 us (35%)
  starting transfers between devices  27 us (24%)
  waiting for transfers between devices  22.1 us (20%)
  Pallas kernels  19.5 us (17%)
  local copies, waits for them, and re-layouts  2.32 us (2%)
    all_to_all x1, blocking collectives, shards(): lax.all_to_all(jnp.broadcast_to(own[None], (32, 8, LANES)), ('x', 'z'), 0...  24.1 us
    all_to_all x1, blocking collectives, shards(): arrived = lax.all_to_all(spread, ('x',) + MP, 0, 0, tiled=True)  15.6 us
    pallas_call x2, Pallas kernels, fused(): pl.pallas_call(fused_kernel, grid=(count,), in_specs=[block(signals.shape...  15.1 us
    ppermute x4, starting transfers between devices, step_ctx(): lax.ppermute(value, CTX, [(i, i + step) for i in range(count) if 0 <= i +...  14.2 us
    all_to_all x1, waiting for transfers between devices, shards(): parts = lax.all_to_all(part, ('z', 'yh'), 0, 0, tiled=True)  11.1 us
    ppermute x4, waiting for transfers between devices, step_ctx(): lax.ppermute(value, CTX, [(i, i + step) for i in range(count) if 0 <= i +...  11 us
    all_to_all x1, starting transfers between devices, shards(): parts = lax.all_to_all(part, ('z', 'yh'), 0, 0, tiled=True)  7.15 us
    ppermute x1, starting transfers between devices, turn(): return lax.ppermute(value, ALL, pairs)  5.6 us
  transfers between devices with their start and end apart: 6, of which 2 were waited for; matrix products, arithmetic and copies ran while one was open for 2% of the time, Pallas kernels for 8%

profile of v9, /device:TPU:1, one launch (start us, length us, event | category | flops | bytes accessed | tf_op | source)
XLA Modules:
  0.0 112.4 jit_solution(17121449942485909801)
XLA Ops:
  0.7 0.8 fusion.1
  1.4 5.6 %collective-permute-start = (bf16[8,128]{1,0:T(8,128)(2,1)S(1)}, bf16[8,128]{1,0:T(8,128)(2,1)S(1)}, u32[]{:S(2)}, u32[]{:S(2)}) collective-permute-start(bf16[8,128]{1,0:T(8,128)(2,1)S(1)} %fusion.1), channel_id=1, source_target_pairs={{0,0},{1,4},{2,8},{3,12},{4,128},{5,132},{6,136},{7,140},{8,256},{... | collective-permute-start | bytes 6152 | tf_op jit(solution)/shard_map/ppermute | solution.py:254
  7.1 1.1 constant_dynamic-update-slice_fusion.7
  8.2 1.1 constant_dynamic-update-slice_fusion.5
  9.4 0.0 collective-permute-done
  9.5 24.1 %all_to_all.15 = bf16[32,8,128]{2,1,0:T(8,128)(2,1)S(1)} all-to-all(bf16[32,8,128]{2,1,0:T(8,128)(2,1)S(1)} %broadcast_in_dim.5), channel_id=1, replica_groups=mesh['x'=4,'z'=8,'yh'=4,'yl'=2,'core'=2] {'x','z'}, dimensions={0} | all-to-all | bytes 131072 | tf_op jit(solution)/shard_map/all_to_all | solution.py:270
  33.5 1.4 %products.3 = (bf16[152,1024]{1,0:T(8,128)(2,1)S(1)}, bf16[160,1024]{1,0:T(8,128)(2,1)S(1)}) custom-call(bf16[576,2048]{1,0:T(8,128)(2,1)S(1)} %constant_dynamic-update-slice_fusion.q.k.v.g, bf16[576,2048]{1,0:T(8,128)(2,1)S(1)} %constant_dynamic-update-slice_fusion.q.k.v.g, bf16[576,2048]{1,0:T(8,128)(2,1)S(1)} %constant_dynamic-update-slice_fusion.q.k.v.g, ...), custom_call_target="tpu_custom_call" | custom-call | flops 20000000 | bytes 3000000 | tf_op jit(solution)/shard_map/products/pallas_call | solution.py:218
  34.9 1.3 %collective-permute-start.4 = (bf16[160,1024]{1,0:T(8,128)(2,1)S(1)}, bf16[160,1024]{1,0:T(8,128)(2,1)S(1)}, u32[]{:S(2)}, u32[]{:S(2)}) collective-permute-start(bf16[160,1024]{1,0:T(8,128)(2,1)S(1)} %get-tuple-element.26), channel_id=1, source_target_pairs={{4,0},{8,4},{12,8},{16,12},{20,16},{24,20},{28,24},{32,28},{36,32}... | collective-permute-start | bytes 983048 | tf_op jit(solution)/shard_map/ppermute | solution.py:242
  36.2 5.5 %collective-permute-start.3 = (bf16[152,1024]{1,0:T(8,128)(2,1)S(1)}, bf16[152,1024]{1,0:T(8,128)(2,1)S(1)}, u32[]{:S(2)}, u32[]{:S(2)}) collective-permute-start(bf16[152,1024]{1,0:T(8,128)(2,1)S(1)} %get-tuple-element.25), channel_id=1, source_target_pairs={{0,4},{4,8},{8,12},{12,16},{16,20},{20,24},{24,28},{28,32},{32,36}... | collective-permute-start | bytes 933896 | tf_op jit(solution)/shard_map/ppermute | solution.py:242
  41.8 1.4 %products.2 = (bf16[152,1024]{1,0:T(8,128)(2,1)S(1)}, bf16[160,1024]{1,0:T(8,128)(2,1)S(1)}) custom-call(bf16[576,2048]{1,0:T(8,128)(2,1)S(1)} %constant_dynamic-update-slice_fusion.q.k.v.g, bf16[576,2048]{1,0:T(8,128)(2,1)S(1)} %constant_dynamic-update-slice_fusion.q.k.v.g, bf16[576,2048]{1,0:T(8,128)(2,1)S(1)} %constant_dynamic-update-slice_fusion.q.k.v.g, ...), custom_call_target="tpu_custom_call" | custom-call | flops 20000000 | bytes 3000000 | tf_op jit(solution)/shard_map/products/pallas_call | solution.py:218
  43.2 1.3 %collective-permute-start.2 = (bf16[160,1024]{1,0:T(8,128)(2,1)S(1)}, bf16[160,1024]{1,0:T(8,128)(2,1)S(1)}, u32[]{:S(2)}, u32[]{:S(2)}) collective-permute-start(bf16[160,1024]{1,0:T(8,128)(2,1)S(1)} %get-tuple-element.24), channel_id=1, source_target_pairs={{4,0},{8,4},{12,8},{16,12},{20,16},{24,20},{28,24},{32,28},{36,32}... | collective-permute-start | bytes 983048 | tf_op jit(solution)/shard_map/ppermute | solution.py:242
  44.5 6.1 %collective-permute-start.1 = (bf16[152,1024]{1,0:T(8,128)(2,1)S(1)}, bf16[152,1024]{1,0:T(8,128)(2,1)S(1)}, u32[]{:S(2)}, u32[]{:S(2)}) collective-permute-start(bf16[152,1024]{1,0:T(8,128)(2,1)S(1)} %get-tuple-element.23), channel_id=1, source_target_pairs={{0,4},{4,8},{8,12},{12,16},{16,20},{20,24},{24,28},{28,32},{32,36}... | collective-permute-start | bytes 933896 | tf_op jit(solution)/shard_map/ppermute | solution.py:242
  50.6 0.0 collective-permute-done.3.below
  50.6 11.0 %collective-permute-done.4.above = bf16[160,1024]{1,0:T(8,128)(2,1)S(1)} collective-permute-done((bf16[160,1024]{1,0:T(8,128)(2,1)S(1)}, bf16[160,1024]{1,0:T(8,128)(2,1)S(1)}, u32[]{:S(2)}, u32[]{:S(2)}) %collective-permute-start.4) | collective-permute-done | bytes 327712 | tf_op jit(solution)/shard_map/ppermute | solution.py:242
  61.6 7.5 %fused.2 = (bf16[136,2048]{1,0:T(8,128)(2,1)}, bf16[136,2048]{1,0:T(8,128)(2,1)}, bf16[136,2048]{1,0:T(8,128)(2,1)}, f32[32,1,640]{2,1,0:T(1,128)}) custom-call(bf16[576,2048]{1,0:T(8,128)(2,1)S(1)} %constant_dynamic-update-slice_fusion.q.k.v.g, bf16[576,2048]{1,0:T(8,128)(2,1)S(1)} %constant_dynamic-update-slice_fusion.q.k.v.g, ...), custom_call_target="tpu_custom_call" | custom-call | flops 1000000000 | bytes 2000000 | tf_op jit(solution)/shard_map/fused/pallas_call | solution.py:165
  69.1 0.0 collective-permute-done.1.below
  69.1 0.0 collective-permute-done.2.above
  69.1 7.6 %fused.3 = (bf16[136,2048]{1,0:T(8,128)(2,1)}, bf16[136,2048]{1,0:T(8,128)(2,1)}, bf16[136,2048]{1,0:T(8,128)(2,1)}, f32[32,1,640]{2,1,0:T(1,128)}) custom-call(bf16[576,2048]{1,0:T(8,128)(2,1)S(1)} %constant_dynamic-update-slice_fusion.q.k.v.g, ...), custom_call_target="tpu_custom_call", output_to_operand_aliasing={{0}: (7, {}), {1}: (8, {}), {2}: (9, {}), {3}: (10, {})} | custom-call | flops 1000000000 | bytes 2000000 | tf_op jit(solution)/shard_map/fused/pallas_call | solution.py:165
  76.7 7.1 %all-to-all-start.1 = ((f32[32,1,640]{2,1,0:T(1,128)}), f32[32,1,640]{2,1,0:T(1,128)S(1)}, u32[]{:S(2)}, u32[]{:S(2)}) async-start(f32[32,1,640]{2,1,0:T(1,128)} %get-tuple-element.34), calls=%async_computation.1 | async-start | bytes 163840 | tf_op jit(solution)/shard_map/all_to_all | solution.py:283
  83.9 11.1 %all-to-all-done.1 = f32[32,1,640]{2,1,0:T(1,128)S(1)} async-done(((f32[32,1,640]{2,1,0:T(1,128)}), f32[32,1,640]{2,1,0:T(1,128)S(1)}, u32[]{:S(2)}, u32[]{:S(2)}) %all-to-all-start.1) | async-done | bytes 81952 | tf_op jit(solution)/shard_map/all_to_all | solution.py:283
  95.0 0.1 reduce_sum.9
  95.0 0.1 broadcast_multiply_fusion
  95.1 15.6 %all_to_all.16.arrived = f32[16,1,640]{2,1,0:T(1,128)} all-to-all(f32[16,1,640]{2,1,0:T(1,128)S(1)} %broadcast_multiply_fusion), channel_id=1, replica_groups=mesh['x'=4,'z'=8,'yh'=4,'yl'=2,'core'=2] {'x','yl','core'}, dimensions={0} | all-to-all | bytes 81920 | tf_op jit(solution)/shard_map/all_to_all | solution.py:286
  110.8 1.6 %finish.1 = (f32[4,7]{1,0:T(4,128)}, f32[4,128]{1,0:T(4,128)}) custom-call(f32[16,1,640]{2,1,0:T(1,128)} %all_to_all.16.arrived), custom_call_target="tpu_custom_call" | custom-call | tf_op jit(solution)/shard_map/finish/pallas_call | solution.py:309
  (12 shorter events, 0.1 us)
Async XLA Ops:
  0.6 8.7 %copy-start = (bf16[136,2048]{1,0:T(8,128)(2,1)S(1)}, bf16[136,2048]{1,0:T(8,128)(2,1)}, u32[]{:S(2)}) copy-start(bf16[136,2048]{1,0:T(8,128)(2,1)} %param.8) | copy-start | bytes 1671172
  0.6 8.7 %copy-start.1 = (bf16[136,2048]{1,0:T(8,128)(2,1)S(1)}, bf16[136,2048]{1,0:T(8,128)(2,1)}, u32[]{:S(2)}) copy-start(bf16[136,2048]{1,0:T(8,128)(2,1)} %param.9) | copy-start | bytes 1671172
  1.4 8.0 %collective-permute-start = (bf16[8,128]{1,0:T(8,128)(2,1)S(1)}, bf16[8,128]{1,0:T(8,128)(2,1)S(1)}, u32[]{:S(2)}, u32[]{:S(2)}) collective-permute-start(bf16[8,128]{1,0:T(8,128)(2,1)S(1)} %fusion.1), channel_id=1, source_target_pairs={{0,0},{1,4},{2,8},{3,12},{4,128},{5,132},{6,136},{7,140},{8,256},{... | collective-permute-start | bytes 6152 | tf_op jit(solution)/shard_map/ppermute | solution.py:254
  34.9 26.7 %collective-permute-start.4 = (bf16[160,1024]{1,0:T(8,128)(2,1)S(1)}, bf16[160,1024]{1,0:T(8,128)(2,1)S(1)}, u32[]{:S(2)}, u32[]{:S(2)}) collective-permute-start(bf16[160,1024]{1,0:T(8,128)(2,1)S(1)} %get-tuple-element.26), channel_id=1, source_target_pairs={{4,0},{8,4},{12,8},{16,12},{20,16},{24,20},{28,24},{32,28},{36,32}... | collective-permute-start | bytes 983048 | tf_op jit(solution)/shard_map/ppermute | solution.py:242
  36.2 14.4 %collective-permute-start.3 = (bf16[152,1024]{1,0:T(8,128)(2,1)S(1)}, bf16[152,1024]{1,0:T(8,128)(2,1)S(1)}, u32[]{:S(2)}, u32[]{:S(2)}) collective-permute-start(bf16[152,1024]{1,0:T(8,128)(2,1)S(1)} %get-tuple-element.25), channel_id=1, source_target_pairs={{0,4},{4,8},{8,12},{12,16},{16,20},{20,24},{24,28},{28,32},{32,36}... | collective-permute-start | bytes 933896 | tf_op jit(solution)/shard_map/ppermute | solution.py:242
  43.2 25.9 %collective-permute-start.2 = (bf16[160,1024]{1,0:T(8,128)(2,1)S(1)}, bf16[160,1024]{1,0:T(8,128)(2,1)S(1)}, u32[]{:S(2)}, u32[]{:S(2)}) collective-permute-start(bf16[160,1024]{1,0:T(8,128)(2,1)S(1)} %get-tuple-element.24), channel_id=1, source_target_pairs={{4,0},{8,4},{12,8},{16,12},{20,16},{24,20},{28,24},{32,28},{36,32}... | collective-permute-start | bytes 983048 | tf_op jit(solution)/shard_map/ppermute | solution.py:242
  44.5 24.6 %collective-permute-start.1 = (bf16[152,1024]{1,0:T(8,128)(2,1)S(1)}, bf16[152,1024]{1,0:T(8,128)(2,1)S(1)}, u32[]{:S(2)}, u32[]{:S(2)}) collective-permute-start(bf16[152,1024]{1,0:T(8,128)(2,1)S(1)} %get-tuple-element.23), channel_id=1, source_target_pairs={{0,4},{4,8},{8,12},{12,16},{16,20},{20,24},{24,28},{28,32},{32,36}... | collective-permute-start | bytes 933896 | tf_op jit(solution)/shard_map/ppermute | solution.py:242
  76.7 18.3 %all-to-all-start.1 = ((f32[32,1,640]{2,1,0:T(1,128)}), f32[32,1,640]{2,1,0:T(1,128)S(1)}, u32[]{:S(2)}, u32[]{:S(2)}) async-start(f32[32,1,640]{2,1,0:T(1,128)} %get-tuple-element.34), calls=%async_computation.1 | async-start | bytes 163840 | tf_op jit(solution)/shard_map/all_to_all | solution.py:283
